TPU v7x, 256 devices: a whole 4x4x8 slice. The times are simulated.
256 devices in a mesh: gz: 16 (over z_lo, x, core), gy: 16 (over z_hi, y).
Axes of the slice: x: 4, y: 4, z: 8 (z_hi: 4, z_lo: 2; z = z_hi * 2 + z_lo), core: 2. Of those that a mesh axis runs over, the one named last changes fastest.
Arguments:
- features: bfloat16 [112, 112, 2688], P('gz', 'gy'), may hold values from -6 to 6
- region: int32 [112, 112, 28], P('gz', 'gy'), may hold values from 0 to 3
- labels: int32 [112, 112, 28], P('gz', 'gy'), may hold values from 0 to 13
- attn_gain: float32 [96], replicated, may hold values from 0.25 to 1.75
- qkv_weight: bfloat16 [96, 288], replicated, may hold values from -0.625 to 0.625
- proj_weight: bfloat16 [96, 96], replicated, may hold values from -0.625 to 0.625
- mlp_gain: float32 [96], replicated, may hold values from 0.25 to 1.75
- up_weight: bfloat16 [96, 384], replicated, may hold values from -0.625 to 0.625
- down_weight: bfloat16 [384, 96], replicated, may hold values from -0.3125 to 0.3125
- head_weight: bfloat16 [96, 14], replicated, may hold values from -0.625 to 0.625
Outputs:
- grad_features: bfloat16 [112, 112, 2688], P('gz', 'gy')
All inputs are finite; a program needn't handle non-finite values.
Results may differ from a plain program's by a relative error of at most 0.022.
Values may be sent and summed in bfloat16 or wider, within the bound.
No kernel may reach another device: no remote copies, remote signals or barrier semaphores. Data moves between devices by JAX's collectives and lax.ppermute only.
A program may use at most 128 MiB of HBM per device.

v0:
```python
import jax
import jax.numpy as jnp
from jax import lax
from jax.sharding import PartitionSpec as P

HEADS = 6
WIN = 7
SHIFT = 3


def shifted(block, axis, distance):
    devices = range(lax.axis_size(axis))
    route = [((i - distance) % len(devices), i) for i in devices]
    return lax.ppermute(block, axis, route)


def product(form, left, right):
    return jnp.einsum(form, left.astype(jnp.float32), right.astype(jnp.float32))


def norm_rows(values, gain):
    center = values - jnp.mean(values, axis=1, keepdims=True)
    spread = jnp.mean(center * center, axis=1, keepdims=True)
    return (center * lax.rsqrt(spread + 1e-05) * gain[None, :, None]).astype(jnp.bfloat16)


def attend(queries, key_part, value_part, region_ids):
    channels, token_count = queries.shape
    head_dim = channels // HEADS
    query_heads = queries.reshape(HEADS, head_dim, token_count)
    key_heads = key_part.reshape(HEADS, head_dim, token_count)
    value_heads = value_part.reshape(HEADS, head_dim, token_count)
    scores = product("hdq,hdk->hqk", query_heads, key_heads) * head_dim ** (-0.5)
    allowed = region_ids[:, None] == region_ids[None, :]
    scores = jnp.where(allowed[None], scores, -1000000000.0)
    row_max = lax.stop_gradient(jnp.max(scores, axis=2, keepdims=True))
    raised = jnp.exp(scores - row_max)
    weights_soft = (raised / jnp.sum(raised, axis=2, keepdims=True)).astype(jnp.bfloat16)
    mixed_out = product("hqk,hdk->hdq", weights_soft, value_heads)
    return mixed_out.reshape(channels, token_count).astype(jnp.bfloat16)


def block_loss(
    field_in,
    region,
    labels,
    attn_gain,
    qkv_weight,
    proj_weight,
    mlp_gain,
    up_weight,
    down_weight,
    head_weight,
):
    depth_count, row_count, merged = field_in.shape
    columns = region.shape[2]
    channels = merged // columns
    windows = columns // WIN
    volume = jnp.roll(field_in.reshape(depth_count, row_count, columns, channels), -SHIFT, axis=2)
    tokens = volume.reshape(depth_count, row_count, windows, WIN, channels).transpose(2, 4, 0, 1, 3)
    tokens = tokens.reshape(windows, channels, depth_count * row_count * WIN)
    region_w = (
        region.reshape(depth_count, row_count, windows, WIN)
        .transpose(2, 0, 1, 3)
        .reshape(windows, -1)
    )
    labels_w = (
        labels.reshape(depth_count, row_count, windows, WIN)
        .transpose(2, 0, 1, 3)
        .reshape(windows, -1)
    )
    normed = norm_rows(tokens.astype(jnp.float32), attn_gain)
    mixed_qkv = product("nct,cf->nft", normed, qkv_weight).astype(jnp.bfloat16)
    queries = mixed_qkv[:, :channels]
    key_part = mixed_qkv[:, channels : 2 * channels]
    value_part = mixed_qkv[:, 2 * channels :]
    attended = lax.map(
        lambda window_parts: attend(*window_parts), (queries, key_part, value_part, region_w)
    )
    projected = product("nct,cf->nft", attended, proj_weight)
    hidden = tokens.astype(jnp.float32) + projected
    normed_two = norm_rows(hidden, mlp_gain)
    raised = product("nct,cf->nft", normed_two, up_weight)
    expanded = jax.nn.gelu(raised, approximate=False).astype(jnp.bfloat16)
    output = hidden + product("nft,fc->nct", expanded, down_weight)
    logits = product("nct,ck->nkt", output.astype(jnp.bfloat16), head_weight)
    log_total = jax.nn.logsumexp(logits, axis=1)
    classes = jnp.arange(logits.shape[1], dtype=jnp.int32)
    picked = jnp.sum(jnp.where(labels_w[:, None, :] == classes[None, :, None], logits, 0.0), axis=1)
    return jnp.sum(log_total - picked)


def body(
    features,
    region,
    labels,
    attn_gain,
    qkv_weight,
    proj_weight,
    mlp_gain,
    up_weight,
    down_weight,
    head_weight,
):
    columns = region.shape[2]
    keep_count = WIN - SHIFT
    from_depth = shifted(features[:SHIFT], "gz", -1)
    depth_shifted = jnp.concatenate([features[SHIFT:], from_depth], axis=0)
    from_rows = shifted(depth_shifted[:, :SHIFT], "gy", -1)
    rolled = jnp.concatenate([depth_shifted[:, SHIFT:], from_rows], axis=1)
    weights = (attn_gain, qkv_weight, proj_weight, mlp_gain, up_weight, down_weight, head_weight)

    def local_loss(field_value):
        return block_loss(field_value, region, labels, *weights)

    partial_loss, pullback = jax.vjp(local_loss, rolled)
    loss_scale = 1.0 / (WIN * WIN * columns * lax.axis_size("gz") * lax.axis_size("gy"))
    cotangents = pullback(jnp.asarray(loss_scale, partial_loss.dtype))
    grad_rolled = cotangents[0]
    lower_rim = shifted(grad_rolled[keep_count:], "gz", 1)
    grad_deep = jnp.concatenate([lower_rim, grad_rolled[:keep_count]], axis=0)
    side_rim = shifted(grad_deep[:, keep_count:], "gy", 1)
    grad_field = jnp.concatenate([side_rim, grad_deep[:, :keep_count]], axis=1)
    return grad_field


def solution(mesh):
    in_specs = (
        P("gz", "gy", None),
        P("gz", "gy", None),
        P("gz", "gy", None),
        P(),
        P(),
        P(),
        P(),
        P(),
        P(),
        P(),
    )
    out_specs = P("gz", "gy", None)
    return jax.shard_map(body, mesh=mesh, in_specs=in_specs, out_specs=out_specs, check_vma=False)
```

profile of v0, /device:TPU:32, one launch (start us, length us, event | category | flops | bytes accessed | tf_op | source)
XLA Modules:
  0.0 170.8 jit_solution(4157017417733120461)
XLA Ops:
  6.5 8.8 %collective-permute-start.1 = (bf16[7,3,2688]{2,1,0:T(4,128)(2,1)S(1)}, bf16[7,3,2688]{2,1,0:T(4,128)(2,1)S(1)}, u32[]{:S(2)}, u32[]{:S(2)}) collective-permute-start(bf16[7,3,2688]{2,1,0:T(4,128)(2,1)S(1)} %pad_maximum_fusion.2), channel_id=1, source_target_pairs={{1,0},{2,1},{3,2},{4,3},{5,4},{6,5},{7,6},{8,7},{9,8},{10,9},{11,1... | collective-permute-start | bytes 338696 | tf_op jit(solution)/shard_map/ppermute | solution.py:14
  15.4 2.6 %collective-permute-done.1 = bf16[7,3,2688]{2,1,0:T(4,128)(2,1)S(1)} collective-permute-done((bf16[7,3,2688]{2,1,0:T(4,128)(2,1)S(1)}, bf16[7,3,2688]{2,1,0:T(4,128)(2,1)S(1)}, u32[]{:S(2)}, u32[]{:S(2)}) %collective-permute-start.1) | collective-permute-done | bytes 112928 | tf_op jit(solution)/shard_map/ppermute | solution.py:14
  23.7 41.9 %while.45 = (s32[]{:T(128)}, bf16[4,96,343]{2,1,0:T(8,128)(2,1)}, bf16[4,6,16,343]{3,2,1,0:T(8,128)(2,1)}, bf16[4,6,16,343]{3,2,1,0:T(8,128)(2,1)}, pred[4,6,343...) while((s32[]{:T(128)}, bf16[4,96,343]{2,1,0:T(8,128)(2,1)}, ...), condition=%wide.region_5.6_spmd, body=%wide.region_2.5_spmd.sunk | while | flops 50372292 | bytes 28290652 | solution.py:77
  25.8 2.7 %convert_dynamic-update-slice_fusion.7 = (bf16[4,6,343,343]{2,3,1,0:T(8,128)(2,1)}, bf16[6,343,343]{1,2,0:T(8,128)(2,1)S(1)}, f32[4,6,343,343]{2,3,1,0:T(8,128)}) fusion(bf16[4,6,343,343]{2,3,1,0:T(8,128)(2,1)} %get-tuple-element.746, s32[]{:T(128)} %get-tuple-element.738, f32[6,343,343]{1,2,0:T(8,128)S(1)} %get-tuple-element.697, ...), kind=kLoop, calls=%fused_computation.33.clone.1 | loop fusion | flops 2117682 | bytes 10584716 | tf_op jit(solution)/shard_map/jvp()/while/body/jit(dynamic_update_index_in_dim)/dynamic_update_slice | solution.py:77
  36.3 2.7 %convert_dynamic-update-slice_fusion.7 = (bf16[4,6,343,343]{2,3,1,0:T(8,128)(2,1)}, bf16[6,343,343]{1,2,0:T(8,128)(2,1)S(1)}, f32[4,6,343,343]{2,3,1,0:T(8,128)}) fusion(bf16[4,6,343,343]{2,3,1,0:T(8,128)(2,1)} %get-tuple-element.746, s32[]{:T(128)} %get-tuple-element.738, f32[6,343,343]{1,2,0:T(8,128)S(1)} %get-tuple-element.697, ...), kind=kLoop, calls=%fused_computation.33.clone.1 | loop fusion | flops 2117682 | bytes 10584716 | tf_op jit(solution)/shard_map/jvp()/while/body/jit(dynamic_update_index_in_dim)/dynamic_update_slice | solution.py:77
  46.7 2.8 %convert_dynamic-update-slice_fusion.7 = (bf16[4,6,343,343]{2,3,1,0:T(8,128)(2,1)}, bf16[6,343,343]{1,2,0:T(8,128)(2,1)S(1)}, f32[4,6,343,343]{2,3,1,0:T(8,128)}) fusion(bf16[4,6,343,343]{2,3,1,0:T(8,128)(2,1)} %get-tuple-element.746, s32[]{:T(128)} %get-tuple-element.738, f32[6,343,343]{1,2,0:T(8,128)S(1)} %get-tuple-element.697, ...), kind=kLoop, calls=%fused_computation.33.clone.1 | loop fusion | flops 2117682 | bytes 10584716 | tf_op jit(solution)/shard_map/jvp()/while/body/jit(dynamic_update_index_in_dim)/dynamic_update_slice | solution.py:77
  57.2 2.8 %convert_dynamic-update-slice_fusion.7 = (bf16[4,6,343,343]{2,3,1,0:T(8,128)(2,1)}, bf16[6,343,343]{1,2,0:T(8,128)(2,1)S(1)}, f32[4,6,343,343]{2,3,1,0:T(8,128)}) fusion(bf16[4,6,343,343]{2,3,1,0:T(8,128)(2,1)} %get-tuple-element.746, s32[]{:T(128)} %get-tuple-element.738, f32[6,343,343]{1,2,0:T(8,128)S(1)} %get-tuple-element.697, ...), kind=kLoop, calls=%fused_computation.33.clone.1 | loop fusion | flops 2117682 | bytes 10584716 | tf_op jit(solution)/shard_map/jvp()/while/body/jit(dynamic_update_index_in_dim)/dynamic_update_slice | solution.py:77
  67.9 4.9 %bitcast_reduce_fusion = (f32[4,343]{1,0:T(4,128)S(1)}, f32[4,343,14]{1,2,0:T(8,128)S(1)}) fusion(bf16[96,14]{0,1:T(8,128)(2,1)S(1)} %copy-done.27, f32[4,96,343]{2,1,0:T(8,128)S(1)} %get-tuple-element.526, f32[4,343,384]{2,1,0:T(8,128)S(1)} %fusion.192, bf16[384,96]{0,1:T(8,128)(2,1)S(1)} %copy-done.31), kind=kOutput, calls=%fused_computation.256 | convolution fusion | flops 139369136 | bytes 2792976 | tf_op jit(solution)/shard_map/jvp(nct,ck->nkt)/dot_general | solution.py:18
  73.1 6.1 %multiply_reduce_fusion.2 = (f32[4,343]{1,0:T(4,128)S(1)}, f32[4,96,343]{2,1,0:T(8,128)}) fusion(f32[4,96,343]{2,1,0:T(8,128)S(1)} %get-tuple-element.526, f32[4,343]{1,0:T(4,128)S(1)} %broadcast_multiply_fusion.1, f32[96]{0:T(128)S(1)} %copy-done.28, bf16[96,384]{1,0:T(8,128)(2,1)S(1)} %copy-done, f32[4,343,384]{2,1,0:T(8,128)S(1)} %fusion.192, ...), kind=kOutput, calls=%fused_computation.224 | convolution fusion | flops 241558432 | bytes 3583328 | tf_op jit(solution)/shard_map/transpose(jvp(nct,cf->nft))/dot_general | solution.py:18
  83.9 64.0 %while.46 = (s32[]{:T(128)}, bf16[4,96,343]{2,1,0:T(8,128)(2,1)}, bf16[4,96,343]{2,1,0:T(8,128)(2,1)}, bf16[4,96,343]{2,1,0:T(8,128)(2,1)}, bf16[4,6,16,343]{3,2...) while((s32[]{:T(128)}, bf16[4,96,343]{2,1,0:T(8,128)(2,1)}, ...), condition=%wide.region_14.15_spmd, body=%wide.region_12.14_spmd.sunk | while | flops 98119264 | bytes 21459356 | solution.py:77
  84.7 2.7 %fusion.376 = (f32[6,343]{1,0:T(8,128)S(1)}, bf16[6,343,343]{1,2,0:T(8,128)(2,1)S(1)}) fusion(f32[4,6,343,343]{2,3,1,0:T(8,128)} %get-tuple-element.808, s32[]{:T(128)S(6)} %sub.114, f32[6,343]{1,0:T(8,128)S(1)} %dynamic-slice_bitcast_fusion.4, bf16[6,16,343]{2,1,0:T(8,128)(2,1)S(1)} %bitcast.479, bf16[4,6,16,343]{3,2,1,0:T(8,128)(2,1)} %get-tuple-element.805), kind=kOutput, calls=%fused_computation.7.clone.1 | convolution fusion | flops 25410126 | bytes 4739164 | tf_op jit(solution)/shard_map/transpose(jvp())/while/body/eval_jaxpr/hqk,hdk->hdq/dot_general | solution.py:18
  91.0 2.8 %fusion.377 = bf16[6,343,343]{1,2,0:T(8,128)(2,1)S(1)} fusion(bf16[6,343,343]{1,2,0:T(8,128)(2,1)S(1)} %get-tuple-element.719, pred[1,6,343,343]{2,3,1,0:T(8,128)(4,1)S(1)} %copy.98, f32[4,6,343,343]{2,3,1,0:T(8,128)} %get-tuple-element.808, s32[]{:T(128)S(6)} %sub.114, f32[6,343]{1,0:T(8,128)S(1)} %neg.75, f32[6,343]{1,0:T(8,128)S(1)} %dynamic-slice_bitcast_fusion.5), kind=kLoop, calls=%fused_computation.5.clone.1 | loop fusion | flops 4941258 | bytes 6369514 | tf_op jit(solution)/shard_map/transpose(jvp())/while/body/eval_jaxpr/mul | solution.py:33
  95.3 2.0 %fusion.378 = bf16[6,16,343]{2,1,0:T(8,128)(2,1)S(1)} fusion(bf16[6,16,343]{2,1,0:T(8,128)(2,1)S(1)} %bitcast.480, bf16[4,6,343,343]{2,3,1,0:T(8,128)(2,1)} %get-tuple-element.810, s32[]{:T(128)S(6)} %sub.114), kind=kOutput, calls=%fused_computation.12.clone.1 | convolution fusion | flops 22588608 | bytes 1716868 | tf_op jit(solution)/shard_map/transpose(jvp())/while/body/eval_jaxpr/hqk,hdk->hdq/dot_general | solution.py:18
  100.7 2.7 %fusion.376 = (f32[6,343]{1,0:T(8,128)S(1)}, bf16[6,343,343]{1,2,0:T(8,128)(2,1)S(1)}) fusion(f32[4,6,343,343]{2,3,1,0:T(8,128)} %get-tuple-element.808, s32[]{:T(128)S(6)} %sub.114, f32[6,343]{1,0:T(8,128)S(1)} %dynamic-slice_bitcast_fusion.4, bf16[6,16,343]{2,1,0:T(8,128)(2,1)S(1)} %bitcast.479, bf16[4,6,16,343]{3,2,1,0:T(8,128)(2,1)} %get-tuple-element.805), kind=kOutput, calls=%fused_computation.7.clone.1 | convolution fusion | flops 25410126 | bytes 4739164 | tf_op jit(solution)/shard_map/transpose(jvp())/while/body/eval_jaxpr/hqk,hdk->hdq/dot_general | solution.py:18
  107.0 2.8 %fusion.377 = bf16[6,343,343]{1,2,0:T(8,128)(2,1)S(1)} fusion(bf16[6,343,343]{1,2,0:T(8,128)(2,1)S(1)} %get-tuple-element.719, pred[1,6,343,343]{2,3,1,0:T(8,128)(4,1)S(1)} %copy.98, f32[4,6,343,343]{2,3,1,0:T(8,128)} %get-tuple-element.808, s32[]{:T(128)S(6)} %sub.114, f32[6,343]{1,0:T(8,128)S(1)} %neg.75, f32[6,343]{1,0:T(8,128)S(1)} %dynamic-slice_bitcast_fusion.5), kind=kLoop, calls=%fused_computation.5.clone.1 | loop fusion | flops 4941258 | bytes 6369514 | tf_op jit(solution)/shard_map/transpose(jvp())/while/body/eval_jaxpr/mul | solution.py:33
  111.3 2.0 %fusion.378 = bf16[6,16,343]{2,1,0:T(8,128)(2,1)S(1)} fusion(bf16[6,16,343]{2,1,0:T(8,128)(2,1)S(1)} %bitcast.480, bf16[4,6,343,343]{2,3,1,0:T(8,128)(2,1)} %get-tuple-element.810, s32[]{:T(128)S(6)} %sub.114), kind=kOutput, calls=%fused_computation.12.clone.1 | convolution fusion | flops 22588608 | bytes 1716868 | tf_op jit(solution)/shard_map/transpose(jvp())/while/body/eval_jaxpr/hqk,hdk->hdq/dot_general | solution.py:18
  116.7 2.7 %fusion.376 = (f32[6,343]{1,0:T(8,128)S(1)}, bf16[6,343,343]{1,2,0:T(8,128)(2,1)S(1)}) fusion(f32[4,6,343,343]{2,3,1,0:T(8,128)} %get-tuple-element.808, s32[]{:T(128)S(6)} %sub.114, f32[6,343]{1,0:T(8,128)S(1)} %dynamic-slice_bitcast_fusion.4, bf16[6,16,343]{2,1,0:T(8,128)(2,1)S(1)} %bitcast.479, bf16[4,6,16,343]{3,2,1,0:T(8,128)(2,1)} %get-tuple-element.805), kind=kOutput, calls=%fused_computation.7.clone.1 | convolution fusion | flops 25410126 | bytes 4739164 | tf_op jit(solution)/shard_map/transpose(jvp())/while/body/eval_jaxpr/hqk,hdk->hdq/dot_general | solution.py:18
  123.0 2.8 %fusion.377 = bf16[6,343,343]{1,2,0:T(8,128)(2,1)S(1)} fusion(bf16[6,343,343]{1,2,0:T(8,128)(2,1)S(1)} %get-tuple-element.719, pred[1,6,343,343]{2,3,1,0:T(8,128)(4,1)S(1)} %copy.98, f32[4,6,343,343]{2,3,1,0:T(8,128)} %get-tuple-element.808, s32[]{:T(128)S(6)} %sub.114, f32[6,343]{1,0:T(8,128)S(1)} %neg.75, f32[6,343]{1,0:T(8,128)S(1)} %dynamic-slice_bitcast_fusion.5), kind=kLoop, calls=%fused_computation.5.clone.1 | loop fusion | flops 4941258 | bytes 6369514 | tf_op jit(solution)/shard_map/transpose(jvp())/while/body/eval_jaxpr/mul | solution.py:33
  127.2 2.0 %fusion.378 = bf16[6,16,343]{2,1,0:T(8,128)(2,1)S(1)} fusion(bf16[6,16,343]{2,1,0:T(8,128)(2,1)S(1)} %bitcast.480, bf16[4,6,343,343]{2,3,1,0:T(8,128)(2,1)} %get-tuple-element.810, s32[]{:T(128)S(6)} %sub.114), kind=kOutput, calls=%fused_computation.12.clone.1 | convolution fusion | flops 22588608 | bytes 1716868 | tf_op jit(solution)/shard_map/transpose(jvp())/while/body/eval_jaxpr/hqk,hdk->hdq/dot_general | solution.py:18
  132.7 2.7 %fusion.376 = (f32[6,343]{1,0:T(8,128)S(1)}, bf16[6,343,343]{1,2,0:T(8,128)(2,1)S(1)}) fusion(f32[4,6,343,343]{2,3,1,0:T(8,128)} %get-tuple-element.808, s32[]{:T(128)S(6)} %sub.114, f32[6,343]{1,0:T(8,128)S(1)} %dynamic-slice_bitcast_fusion.4, bf16[6,16,343]{2,1,0:T(8,128)(2,1)S(1)} %bitcast.479, bf16[4,6,16,343]{3,2,1,0:T(8,128)(2,1)} %get-tuple-element.805), kind=kOutput, calls=%fused_computation.7.clone.1 | convolution fusion | flops 25410126 | bytes 4739164 | tf_op jit(solution)/shard_map/transpose(jvp())/while/body/eval_jaxpr/hqk,hdk->hdq/dot_general | solution.py:18
  139.0 2.8 %fusion.377 = bf16[6,343,343]{1,2,0:T(8,128)(2,1)S(1)} fusion(bf16[6,343,343]{1,2,0:T(8,128)(2,1)S(1)} %get-tuple-element.719, pred[1,6,343,343]{2,3,1,0:T(8,128)(4,1)S(1)} %copy.98, f32[4,6,343,343]{2,3,1,0:T(8,128)} %get-tuple-element.808, s32[]{:T(128)S(6)} %sub.114, f32[6,343]{1,0:T(8,128)S(1)} %neg.75, f32[6,343]{1,0:T(8,128)S(1)} %dynamic-slice_bitcast_fusion.5), kind=kLoop, calls=%fused_computation.5.clone.1 | loop fusion | flops 4941258 | bytes 6369514 | tf_op jit(solution)/shard_map/transpose(jvp())/while/body/eval_jaxpr/mul | solution.py:33
  143.2 2.0 %fusion.378 = bf16[6,16,343]{2,1,0:T(8,128)(2,1)S(1)} fusion(bf16[6,16,343]{2,1,0:T(8,128)(2,1)S(1)} %bitcast.480, bf16[4,6,343,343]{2,3,1,0:T(8,128)(2,1)} %get-tuple-element.810, s32[]{:T(128)S(6)} %sub.114), kind=kOutput, calls=%fused_computation.12.clone.1 | convolution fusion | flops 22588608 | bytes 1716868 | tf_op jit(solution)/shard_map/transpose(jvp())/while/body/eval_jaxpr/hqk,hdk->hdq/dot_general | solution.py:18
  151.5 7.5 %collective-permute-done.2 = bf16[3,7,2688]{2,1,0:T(8,128)(2,1)S(1)} collective-permute-done((bf16[3,7,2688]{2,1,0:T(8,128)(2,1)S(1)}, bf16[3,7,2688]{2,1,0:T(8,128)(2,1)S(1)}, u32[]{:S(2)}, u32[]{:S(2)}) %collective-permute-start.2) | collective-permute-done | bytes 112928 | tf_op jit(solution)/shard_map/ppermute | solution.py:14
  159.2 10.7 %collective-permute-done.3 = bf16[7,3,2688]{2,0,1:T(8,128)(2,1)S(1)} collective-permute-done((bf16[7,3,2688]{2,0,1:T(8,128)(2,1)S(1)}, bf16[7,3,2688]{2,0,1:T(8,128)(2,1)S(1)}, u32[]{:S(2)}, u32[]{:S(2)}) %collective-permute-start.3) | collective-permute-done | bytes 112928 | tf_op jit(solution)/shard_map/ppermute | solution.py:14
  (317 shorter events, 87.8 us)
Async XLA Ops:
  0.0 67.2 %copy-start = (bf16[96,384]{1,0:T(8,128)(2,1)S(1)}, bf16[96,384]{1,0:T(8,128)(2,1)}, u32[]{:S(2)}) copy-start(bf16[96,384]{1,0:T(8,128)(2,1)} %param.21) | copy-start | bytes 221188
  1.0 5.4 %collective-permute-start = (bf16[3,7,2688]{2,1,0:T(8,128)(2,1)S(1)}, bf16[3,7,2688]{2,1,0:T(8,128)(2,1)S(1)}, u32[]{:S(2)}, u32[]{:S(2)}) collective-permute-start(bf16[3,7,2688]{2,1,0:T(8,128)(2,1)S(1)} %slice.48), channel_id=1, source_target_pairs={{16,0},{32,16},{48,32},{64,48},{80,64},{96,80},{112,96},{128,112},... | collective-permute-start | bytes 338696 | tf_op jit(solution)/shard_map/ppermute | solution.py:14
  6.5 11.5 %collective-permute-start.1 = (bf16[7,3,2688]{2,1,0:T(4,128)(2,1)S(1)}, bf16[7,3,2688]{2,1,0:T(4,128)(2,1)S(1)}, u32[]{:S(2)}, u32[]{:S(2)}) collective-permute-start(bf16[7,3,2688]{2,1,0:T(4,128)(2,1)S(1)} %pad_maximum_fusion.2), channel_id=1, source_target_pairs={{1,0},{2,1},{3,2},{4,3},{5,4},{6,5},{7,6},{8,7},{9,8},{10,9},{11,1... | collective-permute-start | bytes 338696 | tf_op jit(solution)/shard_map/ppermute | solution.py:14
  28.6 5.5 %copy-start.8 = (bf16[4,96,343]{2,1,0:T(8,128)(2,1)S(1)}, bf16[4,96,343]{2,1,0:T(8,128)(2,1)}, u32[]{:S(2)}) copy-start(bf16[4,96,343]{2,1,0:T(8,128)(2,1)} %copy-done.7) | copy-start | bytes 790276 | tf_op jit(solution)/shard_map/jvp()/while
  28.6 5.5 %copy-start.10 = (bf16[4,96,343]{2,1,0:T(8,128)(2,1)S(1)}, bf16[4,96,343]{2,1,0:T(8,128)(2,1)}, u32[]{:S(2)}) copy-start(bf16[4,96,343]{2,1,0:T(8,128)(2,1)} %copy-done.9) | copy-start | bytes 790276 | tf_op jit(solution)/shard_map/jvp()/while
  28.6 5.5 %copy-start.25 = (s32[4,343]{1,0:T(4,128)S(1)}, s32[4,343]{1,0:T(4,128)}, u32[]{:S(2)}) copy-start(s32[4,343]{1,0:T(4,128)} %copy-done.24) | copy-start | bytes 16468 | tf_op jit(solution)/shard_map/jvp()/while
  39.0 5.5 %copy-start.8 = (bf16[4,96,343]{2,1,0:T(8,128)(2,1)S(1)}, bf16[4,96,343]{2,1,0:T(8,128)(2,1)}, u32[]{:S(2)}) copy-start(bf16[4,96,343]{2,1,0:T(8,128)(2,1)} %copy-done.7) | copy-start | bytes 790276 | tf_op jit(solution)/shard_map/jvp()/while
  39.0 5.5 %copy-start.10 = (bf16[4,96,343]{2,1,0:T(8,128)(2,1)S(1)}, bf16[4,96,343]{2,1,0:T(8,128)(2,1)}, u32[]{:S(2)}) copy-start(bf16[4,96,343]{2,1,0:T(8,128)(2,1)} %copy-done.9) | copy-start | bytes 790276 | tf_op jit(solution)/shard_map/jvp()/while
  39.0 5.5 %copy-start.25 = (s32[4,343]{1,0:T(4,128)S(1)}, s32[4,343]{1,0:T(4,128)}, u32[]{:S(2)}) copy-start(s32[4,343]{1,0:T(4,128)} %copy-done.24) | copy-start | bytes 16468 | tf_op jit(solution)/shard_map/jvp()/while
  46.7 5.4 %copy-start.15 = (bf16[4,6,16,343]{3,2,1,0:T(8,128)(2,1)S(1)}, bf16[4,6,16,343]{3,2,1,0:T(8,128)(2,1)}, u32[]{:S(2)}) copy-start(bf16[4,6,16,343]{3,2,1,0:T(8,128)(2,1)} %get-tuple-element.741) | copy-start | bytes 790276 | tf_op jit(solution)/shard_map/jvp()/while
  46.7 5.4 %copy-start.17 = (bf16[4,6,16,343]{3,2,1,0:T(8,128)(2,1)S(1)}, bf16[4,6,16,343]{3,2,1,0:T(8,128)(2,1)}, u32[]{:S(2)}) copy-start(bf16[4,6,16,343]{3,2,1,0:T(8,128)(2,1)} %get-tuple-element.747) | copy-start | bytes 790276 | tf_op jit(solution)/shard_map/jvp()/while
  49.5 5.6 %copy-start.8 = (bf16[4,96,343]{2,1,0:T(8,128)(2,1)S(1)}, bf16[4,96,343]{2,1,0:T(8,128)(2,1)}, u32[]{:S(2)}) copy-start(bf16[4,96,343]{2,1,0:T(8,128)(2,1)} %copy-done.7) | copy-start | bytes 790276 | tf_op jit(solution)/shard_map/jvp()/while
  49.5 5.6 %copy-start.10 = (bf16[4,96,343]{2,1,0:T(8,128)(2,1)S(1)}, bf16[4,96,343]{2,1,0:T(8,128)(2,1)}, u32[]{:S(2)}) copy-start(bf16[4,96,343]{2,1,0:T(8,128)(2,1)} %copy-done.9) | copy-start | bytes 790276 | tf_op jit(solution)/shard_map/jvp()/while
  49.5 5.6 %copy-start.25 = (s32[4,343]{1,0:T(4,128)S(1)}, s32[4,343]{1,0:T(4,128)}, u32[]{:S(2)}) copy-start(s32[4,343]{1,0:T(4,128)} %copy-done.24) | copy-start | bytes 16468 | tf_op jit(solution)/shard_map/jvp()/while
  57.2 5.4 %copy-start.15 = (bf16[4,6,16,343]{3,2,1,0:T(8,128)(2,1)S(1)}, bf16[4,6,16,343]{3,2,1,0:T(8,128)(2,1)}, u32[]{:S(2)}) copy-start(bf16[4,6,16,343]{3,2,1,0:T(8,128)(2,1)} %get-tuple-element.741) | copy-start | bytes 790276 | tf_op jit(solution)/shard_map/jvp()/while
  60.0 5.5 %copy-start.8 = (bf16[4,96,343]{2,1,0:T(8,128)(2,1)S(1)}, bf16[4,96,343]{2,1,0:T(8,128)(2,1)}, u32[]{:S(2)}) copy-start(bf16[4,96,343]{2,1,0:T(8,128)(2,1)} %copy-done.7) | copy-start | bytes 790276 | tf_op jit(solution)/shard_map/jvp()/while
  60.0 5.5 %copy-start.10 = (bf16[4,96,343]{2,1,0:T(8,128)(2,1)S(1)}, bf16[4,96,343]{2,1,0:T(8,128)(2,1)}, u32[]{:S(2)}) copy-start(bf16[4,96,343]{2,1,0:T(8,128)(2,1)} %copy-done.9) | copy-start | bytes 790276 | tf_op jit(solution)/shard_map/jvp()/while
  60.0 5.5 %copy-start.25 = (s32[4,343]{1,0:T(4,128)S(1)}, s32[4,343]{1,0:T(4,128)}, u32[]{:S(2)}) copy-start(s32[4,343]{1,0:T(4,128)} %copy-done.24) | copy-start | bytes 16468 | tf_op jit(solution)/shard_map/jvp()/while
  73.1 7.4 %copy-start.5 = (bf16[4,343,96]{1,2,0:T(8,128)(2,1)}, bf16[4,343,96]{1,2,0:T(8,128)(2,1)S(1)}, u32[]{:S(2)}) copy-start(bf16[4,343,96]{1,2,0:T(8,128)(2,1)S(1)} %convolution_convert_fusion.6) | copy-start | bytes 790276
  73.1 8.2 %copy-start.19 = (bf16[96,96]{1,0:T(8,128)(2,1)S(1)}, bf16[96,96]{1,0:T(8,128)(2,1)}, u32[]{:S(2)}) copy-start(bf16[96,96]{1,0:T(8,128)(2,1)} %param.19) | copy-start | bytes 55300
  83.9 64.0 %copy-start.21 = (bf16[96,288]{1,0:T(8,128)(2,1)S(1)}, bf16[96,288]{1,0:T(8,128)(2,1)}, u32[]{:S(2)}) copy-start(bf16[96,288]{1,0:T(8,128)(2,1)} %param.18) | copy-start | bytes 165892
  83.9 64.0 %copy-start.30 = (f32[96]{0:T(128)S(1)}, f32[96]{0:T(128)}, u32[]{:S(2)}) copy-start(f32[96]{0:T(128)} %param.17) | copy-start | bytes 1156
  150.9 8.1 %collective-permute-start.2 = (bf16[3,7,2688]{2,1,0:T(8,128)(2,1)S(1)}, bf16[3,7,2688]{2,1,0:T(8,128)(2,1)S(1)}, u32[]{:S(2)}, u32[]{:S(2)}) collective-permute-start(bf16[3,7,2688]{2,1,0:T(8,128)(2,1)S(1)} %slice.57), channel_id=1, source_target_pairs={{240,0},{0,16},{16,32},{32,48},{48,64},{64,80},{80,96},{96,112},{1... | collective-permute-start | bytes 338696 | tf_op jit(solution)/shard_map/ppermute | solution.py:14
  159.2 10.8 %collective-permute-start.3 = (bf16[7,3,2688]{2,0,1:T(8,128)(2,1)S(1)}, bf16[7,3,2688]{2,0,1:T(8,128)(2,1)S(1)}, u32[]{:S(2)}, u32[]{:S(2)}) collective-permute-start(bf16[7,3,2688]{2,0,1:T(8,128)(2,1)S(1)} %pad_maximum_fusion.3), channel_id=1, source_target_pairs={{15,0},{0,1},{1,2},{2,3},{3,4},{4,5},{5,6},{6,7},{7,8},{8,9},{9,10... | collective-permute-start | bytes 338696 | tf_op jit(solution)/shard_map/ppermute | solution.py:14
  (54 other events, 113.7 us)
where the time goes:
time: 173 us; the launch traced here: 171 us
  local copies, waits for them, and re-layouts  57 us (33%)
  matrix products  52.1 us (30%)
  other arithmetic  28.9 us (17%)
  waiting for transfers between devices  20.8 us (12%)
  starting transfers between devices  10.8 us (6%)
    dot_general x28, matrix products, product(): return jnp.einsum(form, left.astype(jnp.float32), right.astype(jnp.float32))  46.8 us
    ppermute x4, waiting for transfers between devices, shifted(): return lax.ppermute(block, axis, route)  20.8 us
    dynamic_slice x28, local copies, waits for them, and re-layouts, block_loss(): lax.map(lambda window_parts: attend(*window_parts), (queries, key_part, v...  15.6 us
    dynamic_update_slice x16, other arithmetic, block_loss(): lax.map(lambda window_parts: attend(*window_parts), (queries, key_part, v...  13.6 us
    dynamic_update_slice x16, local copies, waits for them, and re-layouts, block_loss(): lax.map(lambda window_parts: attend(*window_parts), (queries, key_part, v...  12.5 us
    mul x4, other arithmetic, attend(): product('hdq,hdk->hqk', query_heads, key_heads) * head_dim ** (-0.5)  11.3 us
    ppermute x4, starting transfers between devices, shifted(): return lax.ppermute(block, axis, route)  10.8 us
    while x112, local copies, waits for them, and re-layouts  8.48 us
  transfers between devices with their start and end apart: 4, of which 3 were waited for; matrix products, arithmetic and copies ran while one was open for 2% of the time, Pallas kernels for 0%

commit v1 on v0

v1 whole, which is shorter than its diff:
```python
import functools

import jax
import jax.numpy as jnp
from jax import lax
from jax.experimental import pallas as pl
from jax.experimental.pallas import tpu as pltpu
from jax.sharding import PartitionSpec as P

C = 96
HEADS = 6
HEAD = 16
HID = 384
CLASSES = 14
WIN = 7
SHIFT = 3
KEEP = WIN - SHIFT
NX = 28
WINDOWS = 4
TOKENS = 343
LANES = 384
SLOTS = 64
WIDE = NX * C
FAR = -(2.0**30)
LOG2E = 1.4426950408889634
LN2 = 0.6931471805599453
BF = jnp.bfloat16
F32 = jnp.float32


def nn(a, b):
    return lax.dot_general(a, b, (((1,), (0,)), ((), ())), preferred_element_type=F32)


def nt(a, b):
    return lax.dot_general(a, b, (((1,), (1,)), ((), ())), preferred_element_type=F32)


def piece_rows(cells, depths, rows):
    parts = [cells[d][rows[0] : rows[1]] for d in depths]
    used = len(depths) * (rows[1] - rows[0])
    if used < 16:
        parts.append(jnp.zeros((16 - used, parts[0].shape[1]), parts[0].dtype))
    return jnp.concatenate(parts, axis=0)


def cut_kernel(f_ref, a_ref, b_ref, c_ref, d_ref):
    cells = [f_ref[d].astype(F32) for d in range(WIN)]
    low, high = range(SHIFT), range(SHIFT, WIN)
    a_ref[...] = piece_rows(cells, high, (SHIFT, WIN)).astype(BF)
    b_ref[...] = piece_rows(cells, low, (SHIFT, WIN)).astype(BF)
    c_ref[...] = piece_rows(cells, high, (0, SHIFT)).astype(BF)
    d_ref[...] = piece_rows(cells, low, (0, SHIFT)).astype(BF)


def join_kernel(a_ref, b_ref, c_ref, d_ref, out_ref):
    a = a_ref[...].astype(F32)
    b = b_ref[...].astype(F32)
    c = c_ref[...].astype(F32)
    d = d_ref[...].astype(F32)
    for i in range(WIN):
        if i < SHIFT:
            left, right, k = d, b, i
        else:
            left, right, k = c, a, i - SHIFT
        rows = [left[SHIFT * k : SHIFT * k + SHIFT], right[KEEP * k : KEEP * k + KEEP]]
        out_ref[i] = jnp.concatenate(rows, axis=0).astype(BF)


def selector():
    token = lax.broadcasted_iota(jnp.int32, (1, LANES), 1)
    column = (token * 1338) >> 16
    cell = token - 49 * column
    slot = 64 * column + cell + 4 * (cell >= 28).astype(jnp.int32) + 4 * (cell >= 40).astype(jnp.int32)
    slot = jnp.where(token < TOKENS, slot, -1)
    place = lax.broadcasted_iota(jnp.int32, (WIN * SLOTS, LANES), 0)
    return (place == slot).astype(F32).astype(BF)


def by_slots(values):
    cells = [values[d] for d in range(WIN)]
    low, high = range(KEEP), range(KEEP, WIN)
    return jnp.concatenate(
        [
            piece_rows(cells, low, (0, KEEP)),
            piece_rows(cells, high, (0, KEEP)),
            piece_rows(cells, low, (KEEP, WIN)),
            piece_rows(cells, high, (KEEP, WIN)),
        ],
        axis=0,
    )


def turned(values):
    return values.astype(F32).T.astype(BF)


def ready_kernel(
    region_ref, labels_ref, g1_ref, g2_ref, qkv_ref, proj_ref, up_ref, down_ref, head_ref,
    ids_ref, sel_ref, gain1_ref, gain2_ref, qkvt_ref, projt_ref, upt_ref, downt_ref, headt_ref, heads_ref,
):
    sel = selector()
    sel_ref[...] = sel
    rows = []
    for ref in (region_ref, labels_ref):
        flat = by_slots(ref[...].astype(F32)).T
        for w in range(WINDOWS):
            rows.append(jnp.concatenate([flat[WIN * w + c : WIN * w + c + 1] for c in range(WIN)], axis=1))
    ids = nn(jnp.concatenate(rows, axis=0).astype(BF), sel)
    token = lax.broadcasted_iota(jnp.int32, ids.shape, 1)
    row = lax.broadcasted_iota(jnp.int32, ids.shape, 0)
    ids_ref[...] = jnp.where(token < TOKENS, ids, jnp.where(row < WINDOWS, 4.0, -1.0))
    for ref, out in ((g1_ref, gain1_ref), (g2_ref, gain2_ref)):
        out[...] = jnp.broadcast_to(ref[...], (128, C)).T
    qkvt_ref[...] = turned(qkv_ref[...])
    projt_ref[...] = turned(proj_ref[...])
    upt_ref[...] = turned(up_ref[...])
    downt_ref[...] = turned(down_ref[...])
    head = head_ref[...].astype(F32)
    head = jnp.concatenate([head, jnp.zeros((C, 2), F32)], axis=1)
    headt_ref[...] = head.T.astype(BF)
    heads_ref[...] = head.astype(BF)


def norm(values, gain):
    center = values - jnp.mean(values, axis=0, keepdims=True)
    inverse = lax.rsqrt(jnp.mean(center * center, axis=0, keepdims=True) + 1e-5)
    unit = center * inverse
    return unit, inverse, (unit * gain).astype(BF)


def norm_back(cotangent, unit, inverse, gain):
    scaled = cotangent * gain
    middle = jnp.mean(scaled, axis=0, keepdims=True)
    along = jnp.mean(scaled * unit, axis=0, keepdims=True)
    return inverse * (scaled - middle - unit * along)


def headed(head, rows, extra):
    parts = []
    if head:
        parts.append(jnp.zeros((HEAD * head, LANES), BF))
    parts.append(rows)
    if head < HEADS - 1:
        parts.append(jnp.zeros((C - HEAD * head - HEAD, LANES), BF))
    return jnp.concatenate(parts + [extra, jnp.zeros((16, LANES), BF)], axis=0)


def main_kernel(
    scale,
    a_ref, b_ref, c_ref, d_ref, ids_ref, sel_ref, gain1_ref, gain2_ref,
    qkv_ref, qkvt_ref, proj_ref, projt_ref, up_ref, upt_ref, down_ref, downt_ref, head_ref, headt_ref,
    oa_ref, ob_ref, oc_ref, od_ref,
    x_ref, grad_ref, e_ref, slope_ref, sides_ref,
):
    sel = sel_ref[...]
    rows = jnp.concatenate([r[...].astype(F32) for r in (a_ref, b_ref, c_ref, d_ref)], axis=0)
    tall = rows.T
    for w in range(WINDOWS):
        cols = [(WIN * w + SHIFT + c) % NX for c in range(WIN)]
        wide = jnp.concatenate([tall[C * c : C * c + C] for c in cols], axis=1).astype(BF)
        x_ref[w] = nn(wide, sel).astype(F32)

    def window(w, carry):
        gain1 = jnp.concatenate([gain1_ref[...]] * 3, axis=1)
        gain2 = jnp.concatenate([gain2_ref[...]] * 3, axis=1)
        x = x_ref[w]
        unit1, inverse1, normed1 = norm(x, gain1)
        region = ids_ref[pl.ds(w, 1), :]
        labels = ids_ref[pl.ds(w + WINDOWS, 1), :]
        qkv = nn(qkvt_ref[...], normed1)
        queries = (qkv[:C] * (0.25 * LOG2E)).astype(BF)
        keys = qkv[C : 2 * C].astype(BF)
        values = qkv[2 * C :].astype(BF)
        index = lax.broadcasted_iota(jnp.int32, (16, LANES), 0)
        same = index.astype(F32) == region
        key_side = same.astype(F32).astype(BF)
        query_side = jnp.where(same | (index > 4), 0.0, FAR).astype(BF)
        ones = jnp.where(index < 2, 1.0, 0.0).astype(BF)
        blank = jnp.zeros((16, LANES), BF)
        keys_t = turned(jnp.concatenate([keys, key_side, blank], axis=0))
        values_t = turned(jnp.concatenate([values, ones, blank], axis=0))
        attended = []
        inverse_sums = []
        for h in range(HEADS):
            own = slice(HEAD * h, HEAD * h + HEAD)
            scores = nn(keys_t, headed(h, queries[own], query_side))
            top = jnp.max(scores, axis=0, keepdims=True)
            raised = jnp.exp2(scores - top).astype(BF)
            e_ref[h] = raised
            mixed = nn(jnp.concatenate([values[own], ones], axis=0), raised)
            inverse_sum = 1.0 / mixed[HEAD : HEAD + 1]
            inverse_sums.append(inverse_sum)
            attended.append((mixed[:HEAD] * inverse_sum).astype(BF))
        hidden = x + nn(projt_ref[...], jnp.concatenate(attended, axis=0))
        unit2, inverse2, normed2 = norm(hidden, gain2)
        output = hidden
        for j in range(3):
            part = slice(128 * j, 128 * j + 128)
            raised = nn(upt_ref[part, :], normed2)
            below = 0.5 + 0.5 * lax.erf(raised * (0.5**0.5))
            bell = jnp.exp(-0.5 * raised * raised) * 0.3989422804014327
            slope_ref[part, :] = below + raised * bell
            output = output + nn(downt_ref[:, part], (raised * below).astype(BF))
        logits = nn(headt_ref[...], output.astype(BF))
        kind = lax.broadcasted_iota(jnp.int32, (16, LANES), 0)
        logits = jnp.where(kind < CLASSES, logits, -1e30)
        powers = jnp.exp(logits - jnp.max(logits, axis=0, keepdims=True))
        soft = powers / jnp.sum(powers, axis=0, keepdims=True)
        at_label = (kind.astype(F32) == labels).astype(F32)
        d_logits = jnp.where(labels >= 0.0, (soft - at_label) * scale, 0.0)
        d_output = nn(head_ref[...], d_logits.astype(BF)).astype(BF)
        d_normed2 = jnp.zeros((C, LANES), F32)
        for j in range(3):
            part = slice(128 * j, 128 * j + 128)
            d_expanded = nn(down_ref[part, :], d_output)
            d_raised = (d_expanded * slope_ref[part, :]).astype(BF)
            d_normed2 = d_normed2 + nn(up_ref[:, part], d_raised)
        d_hidden = d_output.astype(F32) + norm_back(d_normed2, unit2, inverse2, gain2)
        d_attended = nn(proj_ref[...], d_hidden.astype(BF))
        d_queries = []
        d_keys = []
        d_values = []
        for h in range(HEADS):
            own = slice(HEAD * h, HEAD * h + HEAD)
            d_mixed = (d_attended[own] * inverse_sums[h]).astype(BF)
            along = -jnp.sum(d_mixed.astype(F32) * attended[h].astype(F32), axis=0, keepdims=True)
            coarse = along.astype(BF).astype(F32)
            extra = jnp.where(index == 0, coarse, jnp.where(index == 1, along - coarse, 0.0)).astype(BF)
            raised = e_ref[h]
            d_scores = (raised.astype(F32) * nn(values_t, headed(h, d_mixed, extra))).astype(BF)
            d_values.append(nt(d_mixed, raised))
            d_queries.append(nn(keys[own], d_scores) * 0.25)
            d_keys.append(nt(queries[own], d_scores) * LN2)
        d_qkv = jnp.concatenate(d_queries + d_keys + d_values, axis=0).astype(BF)
        d_normed1 = nn(qkv_ref[...], d_qkv)
        grad_ref[w] = (d_hidden + norm_back(d_normed1, unit1, inverse1, gain1)).astype(BF)
        return carry

    lax.fori_loop(0, WINDOWS, window, 0)
    blocks = [None] * NX
    for w in range(WINDOWS):
        wide = nt(grad_ref[w], sel)
        for c in range(WIN):
            blocks[(WIN * w + SHIFT + c) % NX] = wide[:, SLOTS * c : SLOTS * c + SLOTS]
    rows = jnp.concatenate(blocks, axis=0).T
    for k, ref in enumerate((oa_ref, ob_ref, oc_ref, od_ref)):
        ref[...] = rows[16 * k : 16 * k + 16].astype(BF)


VMEM = pl.BlockSpec(memory_space=pltpu.VMEM)
PIECE = jax.ShapeDtypeStruct((16, WIDE), BF)


def cut(features):
    return pl.pallas_call(cut_kernel, out_shape=[PIECE] * 4, in_specs=[VMEM], out_specs=[VMEM] * 4)(features)


def join(*pieces):
    out = jax.ShapeDtypeStruct((WIN, WIN, WIDE), BF)
    return pl.pallas_call(join_kernel, out_shape=out, in_specs=[VMEM] * 4, out_specs=VMEM)(*pieces)


def ready(region, labels, attn_gain, mlp_gain, qkv_weight, proj_weight, up_weight, down_weight, head_weight):
    S = jax.ShapeDtypeStruct
    out = [
        S((8, LANES), F32), S((WIN * SLOTS, LANES), BF), S((C, 128), F32), S((C, 128), F32),
        S((3 * C, C), BF), S((C, C), BF), S((HID, C), BF), S((C, HID), BF), S((16, C), BF), S((C, 16), BF),
    ]
    return pl.pallas_call(ready_kernel, out_shape=out, in_specs=[VMEM] * 9, out_specs=[VMEM] * 10)(
        region, labels, attn_gain.reshape(1, C), mlp_gain.reshape(1, C),
        qkv_weight, proj_weight, up_weight, down_weight, head_weight,
    )


def gradient(pieces, prepared, weights, scale):
    ids, sel, gain1, gain2, qkv_t, proj_t, up_t, down_t, head_t, head = prepared
    qkv_weight, proj_weight, up_weight, down_weight = weights
    return pl.pallas_call(
        functools.partial(main_kernel, scale),
        out_shape=[PIECE] * 4,
        in_specs=[VMEM] * 18,
        out_specs=[VMEM] * 4,
        scratch_shapes=[
            pltpu.VMEM((WINDOWS, C, LANES), F32),
            pltpu.VMEM((WINDOWS, C, LANES), BF),
            pltpu.VMEM((HEADS, LANES, LANES), BF),
            pltpu.VMEM((HID, LANES), F32),
            pltpu.VMEM((16, LANES), F32),
        ],
        compiler_params=pltpu.CompilerParams(vmem_limit_bytes=48 * 2**20),
    )(
        *pieces, ids, sel, gain1, gain2, qkv_weight, qkv_t, proj_weight, proj_t,
        up_weight, up_t, down_weight, down_t, head, head_t,
    )


def moved(piece, axes, steps):
    sizes = [lax.axis_size(a) for a in axes]
    route = []
    if len(axes) == 1:
        (n,) = sizes
        route = [((i - steps) % n, i) for i in range(n)]
    else:
        n, m = sizes
        for i in range(n):
            for j in range(m):
                route.append((((i - steps) % n) * m + (j - steps) % m, i * m + j))
    return lax.ppermute(piece, axes if len(axes) > 1 else axes[0], route)


ROADS = (("gz",), ("gy",), ("gz", "gy"))


def body(
    features, region, labels, attn_gain, qkv_weight, proj_weight, mlp_gain, up_weight, down_weight, head_weight,
):
    own, *away = cut(features)
    arrived = [moved(piece, road, -1) for piece, road in zip(away, ROADS)]
    prepared = ready(
        region, labels, attn_gain, mlp_gain, qkv_weight, proj_weight, up_weight, down_weight, head_weight
    )
    scale = 1.0 / (WIN * WIN * NX * lax.axis_size("gz") * lax.axis_size("gy"))
    own, *away = gradient((own, *arrived), prepared, (qkv_weight, proj_weight, up_weight, down_weight), scale)
    arrived = [moved(piece, road, 1) for piece, road in zip(away, ROADS)]
    return join(own, *arrived)


def solution(mesh):
    cells = P("gz", "gy", None)
    in_specs = (cells, cells, cells) + (P(),) * 7
    return jax.shard_map(body, mesh=mesh, in_specs=in_specs, out_specs=cells, check_vma=False)
```

time: 173 us -> 75 us (0.43)
  matrix products: 52.1 us -> 0 us
  local copies, waits for them, and re-layouts: 57 us -> 10.1 us
  Pallas kernels: 0 us -> 33.4 us
  other arithmetic: 28.9 us -> 0 us
  waiting for transfers between devices: 20.8 us -> 18.6 us
    dot_general x28 -> x0, matrix products: 46.8 us -> none  [product(): return jnp.einsum(form, left.astype(jnp.float32), right.astype(jnp.float32))]
    pallas_call x0 -> x4, Pallas kernels: none -> 33.4 us  [the longest x1 27.6 us: gradient(): pl.pallas_call(functools.partial(main_kernel, scale), out_shape=[PIECE] *...]
    dynamic_slice x28 -> x0, local copies, waits for them, and re-layouts: 15.6 us -> none  [block_loss(): lax.map(lambda window_parts: attend(*window_parts), (queries, key_part, v...]
    dynamic_update_slice x16 -> x0, other arithmetic: 13.6 us -> none  [block_loss(): lax.map(lambda window_parts: attend(*window_parts), (queries, key_part, v...]
    dynamic_update_slice x16 -> x0, local copies, waits for them, and re-layouts: 12.5 us -> none  [block_loss(): lax.map(lambda window_parts: attend(*window_parts), (queries, key_part, v...]
    mul x4 -> x0, other arithmetic: 11.3 us -> none  [attend(): product('hdq,hdk->hqk', query_heads, key_heads) * head_dim ** (-0.5)]
    unnamed x36 -> x44, local copies, waits for them, and re-layouts: 0.88 us -> 10.1 us
    while x112 -> x0, local copies, waits for them, and re-layouts: 8.48 us -> none
  transfers between devices with their start and end apart: 4 -> 6, of which waited for: 3 -> 4; matrix products, arithmetic and copies ran while one was open for 2% -> 2% of each run, Pallas kernels for 0% -> 3%
where the time goes in v1:
time: 75 us; the launch traced here: 74.3 us
  Pallas kernels  33.4 us (45%)
  waiting for transfers between devices  18.6 us (25%)
  starting transfers between devices  12.1 us (16%)
  local copies, waits for them, and re-layouts  10.1 us (13%)
    pallas_call x1, Pallas kernels, gradient(): pl.pallas_call(functools.partial(main_kernel, scale), out_shape=[PIECE] *...  27.6 us
    ppermute x6, waiting for transfers between devices, moved(): return lax.ppermute(piece, axes if len(axes) > 1 else axes[0], route)  18.6 us
    ppermute x6, starting transfers between devices, moved(): return lax.ppermute(piece, axes if len(axes) > 1 else axes[0], route)  12.1 us
    unnamed x44, local copies, waits for them, and re-layouts  10.1 us
    pallas_call x1, Pallas kernels, ready(): pl.pallas_call(ready_kernel, out_shape=out, in_specs=[VMEM] * 9, out_spec...  2.2 us
    pallas_call x1, Pallas kernels, join(): pl.pallas_call(join_kernel, out_shape=out, in_specs=[VMEM] * 4, out_specs...  1.84 us
    pallas_call x1, Pallas kernels, cut(): pl.pallas_call(cut_kernel, out_shape=[PIECE] * 4, in_specs=[VMEM], out_sp...  1.77 us
  transfers between devices with their start and end apart: 6, of which 4 were waited for; matrix products, arithmetic and copies ran while one was open for 2% of the time, Pallas kernels for 3%

profile of v1, /device:TPU:32, one launch (start us, length us, event | category | flops | bytes accessed | tf_op | source)
XLA Modules:
  0.0 74.3 jit_solution(12059231993133557852)
XLA Ops:
  0.0 1.8 %shard_map.100 = (bf16[16,2688]{1,0:T(8,128)(2,1)}, bf16[16,2688]{1,0:T(8,128)(2,1)}, bf16[16,2688]{1,0:T(8,128)(2,1)}, bf16[16,2688]{1,0:T(8,128)(2,1)}) custom-call(bf16[7,7,2688]{2,1,0:T(8,128)(2,1)} %f_ref.1), custom_call_target="tpu_custom_call" | custom-call | tf_op jit(solution)/shard_map/pallas_call | solution.py:256
  1.8 1.7 %collective-permute-start = (bf16[16,2688]{1,0:T(8,128)(2,1)}, bf16[16,2688]{1,0:T(8,128)(2,1)S(1)}, u32[]{:S(2)}, u32[]{:S(2)}) collective-permute-start(bf16[16,2688]{1,0:T(8,128)(2,1)} %get-tuple-element.24), channel_id=1, source_target_pairs={{16,0},{32,16},{48,32},{64,48},{80,64},{96,80},{112,96},{128,112},... | collective-permute-start | bytes 258056 | tf_op jit(solution)/shard_map/ppermute | solution.py:309
  3.5 8.8 %collective-permute-start.1 = (bf16[16,2688]{1,0:T(8,128)(2,1)}, bf16[16,2688]{1,0:T(8,128)(2,1)S(1)}, u32[]{:S(2)}, u32[]{:S(2)}) collective-permute-start(bf16[16,2688]{1,0:T(8,128)(2,1)} %get-tuple-element.25), channel_id=1, source_target_pairs={{1,0},{2,1},{3,2},{4,3},{5,4},{6,5},{7,6},{8,7},{9,8},{10,9},{11,1... | collective-permute-start | bytes 258056 | tf_op jit(solution)/shard_map/ppermute | solution.py:309
  12.8 0.7 copy.12.head_ref
  13.6 0.8 %copy.11.down_ref = bf16[384,96]{1,0:T(8,128)(2,1)} copy(bf16[384,96]{0,1:T(8,128)(2,1)S(1)} %copy-done.19) | data formatting | bytes 147456 | tf_op args[8]
  14.3 2.2 %shard_map.101 = (f32[8,384]{1,0:T(8,128)}, bf16[448,384]{1,0:T(8,128)(2,1)}, f32[96,128]{1,0:T(8,128)}, f32[96,128]{1,0:T(8,128)}, bf16[288,96]{1,0:T(8,128)(2,...) custom-call(s32[7,7,28]{2,1,0:T(8,128)} %region_ref.1, ...), custom_call_target="tpu_custom_call" | custom-call | tf_op jit(solution)/shard_map/pallas_call | solution.py:270
  16.6 0.6 collective-permute-done.2.d_ref
  17.2 0.6 copy-done.15
  17.8 1.0 %copy-done.1 = bf16[448,384]{1,0:T(8,128)(2,1)S(1)} copy-done((bf16[448,384]{1,0:T(8,128)(2,1)S(1)}, bf16[448,384]{1,0:T(8,128)(2,1)}, u32[]{:S(2)}) %copy-start.1) | copy-done | bytes 344088
  18.8 0.9 %copy-done.4 = bf16[384,96]{1,0:T(8,128)(2,1)S(1)} copy-done((bf16[384,96]{1,0:T(8,128)(2,1)S(1)}, bf16[384,96]{1,0:T(8,128)(2,1)}, u32[]{:S(2)}) %copy-start.4) | copy-done | bytes 73752
  19.7 0.9 %copy-done.8 = bf16[288,96]{1,0:T(8,128)(2,1)S(1)} copy-done((bf16[288,96]{1,0:T(8,128)(2,1)S(1)}, bf16[288,96]{1,0:T(8,128)(2,1)}, u32[]{:S(2)}) %copy-start.8) | copy-done | bytes 55320
  20.6 0.9 %copy-done.9 = bf16[96,384]{1,0:T(8,128)(2,1)S(1)} copy-done((bf16[96,384]{1,0:T(8,128)(2,1)S(1)}, bf16[96,384]{1,0:T(8,128)(2,1)}, u32[]{:S(2)}) %copy-start.9) | copy-done | bytes 73752
  21.5 0.8 %copy-done.10 = f32[96,128]{1,0:T(8,128)S(1)} copy-done((f32[96,128]{1,0:T(8,128)S(1)}, f32[96,128]{1,0:T(8,128)}, u32[]{:S(2)}) %copy-start.10) | copy-done | bytes 49176
  22.3 0.8 %copy-done.11 = f32[96,128]{1,0:T(8,128)S(1)} copy-done((f32[96,128]{1,0:T(8,128)S(1)}, f32[96,128]{1,0:T(8,128)}, u32[]{:S(2)}) %copy-start.11) | copy-done | bytes 49176
  23.1 0.7 copy-done.12
  23.8 0.7 copy-done.13
  24.5 27.6 %shard_map.102 = (bf16[16,2688]{1,0:T(8,128)(2,1)S(1)}, bf16[16,2688]{1,0:T(8,128)(2,1)S(1)}, bf16[16,2688]{1,0:T(8,128)(2,1)S(1)}, bf16[16,2688]{1,0:T(8,128)(2,1)S(1)}) custom-call(bf16[16,2688]{1,0:T(8,128)(2,1)S(1)} %copy-done.7, bf16[16,2688]{1,0:T(8,128)(2,1)S(1)} %collective-permute-done.b_ref, bf16[16,2688]{1,0:T(8,128)(2,1)S(1)} %collective-permute-done.1.c_ref, ...), custom_call_target="tpu_custom_call" | custom-call | tf_op jit(solution)/shard_map/pallas_call | solution.py:279
  52.2 0.6 copy-done.6
  52.8 1.0 %collective-permute-start.4 = (bf16[16,2688]{1,0:T(8,128)(2,1)S(1)}, bf16[16,2688]{1,0:T(8,128)(2,1)S(1)}, u32[]{:S(2)}, u32[]{:S(2)}) collective-permute-start(bf16[16,2688]{1,0:T(8,128)(2,1)S(1)} %get-tuple-element.39), channel_id=1, source_target_pairs={{15,0},{0,1},{1,2},{2,3},{3,4},{4,5},{5,6},{6,7},{7,8},{8,9},{9,10... | collective-permute-start | bytes 258056 | tf_op jit(solution)/shard_map/ppermute | solution.py:309
  53.8 5.0 %collective-permute-done.3.b_ref = bf16[16,2688]{1,0:T(8,128)(2,1)S(1)} collective-permute-done((bf16[16,2688]{1,0:T(8,128)(2,1)S(1)}, bf16[16,2688]{1,0:T(8,128)(2,1)S(1)}, u32[]{:S(2)}, u32[]{:S(2)}) %collective-permute-start.3) | collective-permute-done | bytes 86048 | tf_op jit(solution)/shard_map/ppermute | solution.py:309
  58.8 3.8 %collective-permute-done.4.c_ref = bf16[16,2688]{1,0:T(8,128)(2,1)S(1)} collective-permute-done((bf16[16,2688]{1,0:T(8,128)(2,1)S(1)}, bf16[16,2688]{1,0:T(8,128)(2,1)S(1)}, u32[]{:S(2)}, u32[]{:S(2)}) %collective-permute-start.4) | collective-permute-done | bytes 86048 | tf_op jit(solution)/shard_map/ppermute | solution.py:309
  62.7 9.2 %collective-permute-done.5.d_ref = bf16[16,2688]{1,0:T(8,128)(2,1)S(1)} collective-permute-done((bf16[16,2688]{1,0:T(8,128)(2,1)S(1)}, bf16[16,2688]{1,0:T(8,128)(2,1)S(1)}, u32[]{:S(2)}, u32[]{:S(2)}) %collective-permute-start.5) | collective-permute-done | bytes 86048 | tf_op jit(solution)/shard_map/ppermute | solution.py:309
  71.9 0.6 copy-done.18
  72.5 1.8 %shard_map.103 = bf16[7,7,2688]{2,1,0:T(8,128)(2,1)} custom-call(bf16[16,2688]{1,0:T(8,128)(2,1)} %copy-done.6, bf16[16,2688]{1,0:T(8,128)(2,1)} %copy-done.16, bf16[16,2688]{1,0:T(8,128)(2,1)} %copy-done.17, bf16[16,2688]{1,0:T(8,128)(2,1)} %copy-done.18), custom_call_target="tpu_custom_call" | custom-call | tf_op jit(solution)/shard_map/pallas_call | solution.py:261
  (36 shorter events, 0.7 us)
Async XLA Ops:
  0.0 13.6 %copy-start.19 = (bf16[384,96]{0,1:T(8,128)(2,1)S(1)}, bf16[384,96]{0,1:T(8,128)(2,1)}, u32[]{:S(2)}) copy-start(bf16[384,96]{0,1:T(8,128)(2,1)} %param.18) | copy-start | bytes 221188
  1.8 11.1 %copy-start.20 = (bf16[96,14]{0,1:T(8,128)(2,1)S(1)}, bf16[96,14]{0,1:T(8,128)(2,1)}, u32[]{:S(2)}) copy-start(bf16[96,14]{0,1:T(8,128)(2,1)} %param.19) | copy-start | bytes 8068
  1.8 14.8 %collective-permute-start = (bf16[16,2688]{1,0:T(8,128)(2,1)}, bf16[16,2688]{1,0:T(8,128)(2,1)S(1)}, u32[]{:S(2)}, u32[]{:S(2)}) collective-permute-start(bf16[16,2688]{1,0:T(8,128)(2,1)} %get-tuple-element.24), channel_id=1, source_target_pairs={{16,0},{32,16},{48,32},{64,48},{80,64},{96,80},{112,96},{128,112},... | collective-permute-start | bytes 258056 | tf_op jit(solution)/shard_map/ppermute | solution.py:309
  3.5 13.0 %collective-permute-start.1 = (bf16[16,2688]{1,0:T(8,128)(2,1)}, bf16[16,2688]{1,0:T(8,128)(2,1)S(1)}, u32[]{:S(2)}, u32[]{:S(2)}) collective-permute-start(bf16[16,2688]{1,0:T(8,128)(2,1)} %get-tuple-element.25), channel_id=1, source_target_pairs={{1,0},{2,1},{3,2},{4,3},{5,4},{6,5},{7,6},{8,7},{9,8},{10,9},{11,1... | collective-permute-start | bytes 258056 | tf_op jit(solution)/shard_map/ppermute | solution.py:309
  12.3 4.9 %collective-permute-start.2 = (bf16[16,2688]{1,0:T(8,128)(2,1)}, bf16[16,2688]{1,0:T(8,128)(2,1)S(1)}, u32[]{:S(2)}, u32[]{:S(2)}) collective-permute-start(bf16[16,2688]{1,0:T(8,128)(2,1)} %get-tuple-element.26), channel_id=1, source_target_pairs={{17,0},{18,1},{19,2},{20,3},{21,4},{22,5},{23,6},{24,7},{25,8},{26... | collective-permute-start | bytes 258056 | tf_op jit(solution)/shard_map/ppermute | solution.py:309
  14.3 2.8 %copy-start = (bf16[384,96]{1,0:T(8,128)(2,1)S(1)}, bf16[384,96]{1,0:T(8,128)(2,1)}, u32[]{:S(2)}) copy-start(bf16[384,96]{1,0:T(8,128)(2,1)} %copy.11.down_ref) | copy-start | bytes 221188
  14.3 2.8 %copy-start.2 = (bf16[96,288]{1,0:T(8,128)(2,1)S(1)}, bf16[96,288]{1,0:T(8,128)(2,1)}, u32[]{:S(2)}) copy-start(bf16[96,288]{1,0:T(8,128)(2,1)} %qkv_ref.3) | copy-start | bytes 165892
  14.3 2.8 %copy-start.3 = (bf16[96,384]{1,0:T(8,128)(2,1)S(1)}, bf16[96,384]{1,0:T(8,128)(2,1)}, u32[]{:S(2)}) copy-start(bf16[96,384]{1,0:T(8,128)(2,1)} %up_ref.3) | copy-start | bytes 221188
  14.3 2.8 %copy-start.5 = (bf16[96,96]{1,0:T(8,128)(2,1)S(1)}, bf16[96,96]{1,0:T(8,128)(2,1)}, u32[]{:S(2)}) copy-start(bf16[96,96]{1,0:T(8,128)(2,1)} %proj_ref.3) | copy-start | bytes 55300
  14.3 2.8 %copy-start.7 = (bf16[16,2688]{1,0:T(8,128)(2,1)S(1)}, bf16[16,2688]{1,0:T(8,128)(2,1)}, u32[]{:S(2)}) copy-start(bf16[16,2688]{1,0:T(8,128)(2,1)} %get-tuple-element.23.a_ref) | copy-start | bytes 258052
  16.5 0.7 copy-start.14
  17.8 1.0 %copy-start.1 = (bf16[448,384]{1,0:T(8,128)(2,1)S(1)}, bf16[448,384]{1,0:T(8,128)(2,1)}, u32[]{:S(2)}) copy-start(bf16[448,384]{1,0:T(8,128)(2,1)} %get-tuple-element.28.sel_ref) | copy-start | bytes 1032196
  18.8 0.9 %copy-start.4 = (bf16[384,96]{1,0:T(8,128)(2,1)S(1)}, bf16[384,96]{1,0:T(8,128)(2,1)}, u32[]{:S(2)}) copy-start(bf16[384,96]{1,0:T(8,128)(2,1)} %get-tuple-element.33.upt_ref) | copy-start | bytes 221188
  19.7 0.9 %copy-start.8 = (bf16[288,96]{1,0:T(8,128)(2,1)S(1)}, bf16[288,96]{1,0:T(8,128)(2,1)}, u32[]{:S(2)}) copy-start(bf16[288,96]{1,0:T(8,128)(2,1)} %get-tuple-element.31.qkvt_ref) | copy-start | bytes 165892
  20.6 0.9 %copy-start.9 = (bf16[96,384]{1,0:T(8,128)(2,1)S(1)}, bf16[96,384]{1,0:T(8,128)(2,1)}, u32[]{:S(2)}) copy-start(bf16[96,384]{1,0:T(8,128)(2,1)} %get-tuple-element.34.downt_ref) | copy-start | bytes 221188
  21.5 0.8 %copy-start.10 = (f32[96,128]{1,0:T(8,128)S(1)}, f32[96,128]{1,0:T(8,128)}, u32[]{:S(2)}) copy-start(f32[96,128]{1,0:T(8,128)} %get-tuple-element.29.gain1_ref) | copy-start | bytes 147460
  22.3 0.8 %copy-start.11 = (f32[96,128]{1,0:T(8,128)S(1)}, f32[96,128]{1,0:T(8,128)}, u32[]{:S(2)}) copy-start(f32[96,128]{1,0:T(8,128)} %get-tuple-element.30.gain2_ref) | copy-start | bytes 147460
  23.1 0.7 copy-start.12
  23.8 0.7 copy-start.13
  52.8 6.0 %collective-permute-start.3 = (bf16[16,2688]{1,0:T(8,128)(2,1)S(1)}, bf16[16,2688]{1,0:T(8,128)(2,1)S(1)}, u32[]{:S(2)}, u32[]{:S(2)}) collective-permute-start(bf16[16,2688]{1,0:T(8,128)(2,1)S(1)} %get-tuple-element.38), channel_id=1, source_target_pairs={{240,0},{0,16},{16,32},{32,48},{48,64},{64,80},{80,96},{96,112},{1... | collective-permute-start | bytes 258056 | tf_op jit(solution)/shard_map/ppermute | solution.py:309
  52.8 9.9 %collective-permute-start.4 = (bf16[16,2688]{1,0:T(8,128)(2,1)S(1)}, bf16[16,2688]{1,0:T(8,128)(2,1)S(1)}, u32[]{:S(2)}, u32[]{:S(2)}) collective-permute-start(bf16[16,2688]{1,0:T(8,128)(2,1)S(1)} %get-tuple-element.39), channel_id=1, source_target_pairs={{15,0},{0,1},{1,2},{2,3},{3,4},{4,5},{5,6},{6,7},{7,8},{8,9},{9,10... | collective-permute-start | bytes 258056 | tf_op jit(solution)/shard_map/ppermute | solution.py:309
  53.8 18.0 %collective-permute-start.5 = (bf16[16,2688]{1,0:T(8,128)(2,1)S(1)}, bf16[16,2688]{1,0:T(8,128)(2,1)S(1)}, u32[]{:S(2)}, u32[]{:S(2)}) collective-permute-start(bf16[16,2688]{1,0:T(8,128)(2,1)S(1)} %get-tuple-element.40), channel_id=1, source_target_pairs={{255,0},{240,1},{241,2},{242,3},{243,4},{244,5},{245,6},{246,7},{2... | collective-permute-start | bytes 258056 | tf_op jit(solution)/shard_map/ppermute | solution.py:309
  58.8 13.0 %copy-start.16 = (bf16[16,2688]{1,0:T(8,128)(2,1)}, bf16[16,2688]{1,0:T(8,128)(2,1)S(1)}, u32[]{:S(2)}) copy-start(bf16[16,2688]{1,0:T(8,128)(2,1)S(1)} %collective-permute-done.3.b_ref) | copy-start | bytes 258052
  62.7 9.2 %copy-start.17 = (bf16[16,2688]{1,0:T(8,128)(2,1)}, bf16[16,2688]{1,0:T(8,128)(2,1)S(1)}, u32[]{:S(2)}) copy-start(bf16[16,2688]{1,0:T(8,128)(2,1)S(1)} %collective-permute-done.4.c_ref) | copy-start | bytes 258052
  (3 other events, 1.9 us)

commit v2 on v1

--- a/solution.py
+++ b/solution.py
@@ -96,8 +96,8 @@
 
 
 def ready_kernel(
-    region_ref, labels_ref, g1_ref, g2_ref, qkv_ref, proj_ref, up_ref, down_ref, head_ref,
-    ids_ref, sel_ref, gain1_ref, gain2_ref, qkvt_ref, projt_ref, upt_ref, downt_ref, headt_ref, heads_ref,
+    region_ref, labels_ref, g1_ref, g2_ref, qkv_ref, proj_ref, up_ref, downt_ref, head_ref,
+    ids_ref, sel_ref, gain1_ref, gain2_ref, qkvt_ref, projt_ref, upt_ref, down_ref, headt_ref, heads_ref,
 ):
     sel = selector()
     sel_ref[...] = sel
@@ -115,11 +115,10 @@
     qkvt_ref[...] = turned(qkv_ref[...])
     projt_ref[...] = turned(proj_ref[...])
     upt_ref[...] = turned(up_ref[...])
-    downt_ref[...] = turned(down_ref[...])
-    head = head_ref[...].astype(F32)
-    head = jnp.concatenate([head, jnp.zeros((C, 2), F32)], axis=1)
-    headt_ref[...] = head.T.astype(BF)
-    heads_ref[...] = head.astype(BF)
+    down_ref[...] = turned(downt_ref[...])
+    head = jnp.concatenate([head_ref[...].astype(F32), jnp.zeros((2, C), F32)], axis=0)
+    headt_ref[...] = head.astype(BF)
+    heads_ref[...] = head.T.astype(BF)
 
 
 def norm(values, gain):
@@ -249,33 +248,34 @@
 
 
 VMEM = pl.BlockSpec(memory_space=pltpu.VMEM)
+SMALL = pltpu.CompilerParams(vmem_limit_bytes=8 * 2**20)
 PIECE = jax.ShapeDtypeStruct((16, WIDE), BF)
 
 
 def cut(features):
-    return pl.pallas_call(cut_kernel, out_shape=[PIECE] * 4, in_specs=[VMEM], out_specs=[VMEM] * 4)(features)
+    return pl.pallas_call(cut_kernel, out_shape=[PIECE] * 4, in_specs=[VMEM], out_specs=[VMEM] * 4, compiler_params=SMALL)(features)
 
 
 def join(*pieces):
     out = jax.ShapeDtypeStruct((WIN, WIN, WIDE), BF)
-    return pl.pallas_call(join_kernel, out_shape=out, in_specs=[VMEM] * 4, out_specs=VMEM)(*pieces)
+    return pl.pallas_call(join_kernel, out_shape=out, in_specs=[VMEM] * 4, out_specs=VMEM, compiler_params=SMALL)(*pieces)
 
 
 def ready(region, labels, attn_gain, mlp_gain, qkv_weight, proj_weight, up_weight, down_weight, head_weight):
     S = jax.ShapeDtypeStruct
     out = [
         S((8, LANES), F32), S((WIN * SLOTS, LANES), BF), S((C, 128), F32), S((C, 128), F32),
-        S((3 * C, C), BF), S((C, C), BF), S((HID, C), BF), S((C, HID), BF), S((16, C), BF), S((C, 16), BF),
+        S((3 * C, C), BF), S((C, C), BF), S((HID, C), BF), S((HID, C), BF), S((16, C), BF), S((C, 16), BF),
     ]
-    return pl.pallas_call(ready_kernel, out_shape=out, in_specs=[VMEM] * 9, out_specs=[VMEM] * 10)(
+    return pl.pallas_call(ready_kernel, out_shape=out, in_specs=[VMEM] * 9, out_specs=[VMEM] * 10, compiler_params=SMALL)(
         region, labels, attn_gain.reshape(1, C), mlp_gain.reshape(1, C),
         qkv_weight, proj_weight, up_weight, down_weight, head_weight,
     )
 
 
 def gradient(pieces, prepared, weights, scale):
-    ids, sel, gain1, gain2, qkv_t, proj_t, up_t, down_t, head_t, head = prepared
-    qkv_weight, proj_weight, up_weight, down_weight = weights
+    ids, sel, gain1, gain2, qkv_t, proj_t, up_t, down, head_t, head = prepared
+    qkv_weight, proj_weight, up_weight, down_t = weights
     return pl.pallas_call(
         functools.partial(main_kernel, scale),
         out_shape=[PIECE] * 4,
@@ -288,10 +288,10 @@
             pltpu.VMEM((HID, LANES), F32),
             pltpu.VMEM((16, LANES), F32),
         ],
-        compiler_params=pltpu.CompilerParams(vmem_limit_bytes=48 * 2**20),
+        compiler_params=pltpu.CompilerParams(vmem_limit_bytes=32 * 2**20),
     )(
         *pieces, ids, sel, gain1, gain2, qkv_weight, qkv_t, proj_weight, proj_t,
-        up_weight, up_t, down_weight, down_t, head, head_t,
+        up_weight, up_t, down, down_t, head, head_t,
     )
 
 
@@ -316,12 +316,13 @@
     features, region, labels, attn_gain, qkv_weight, proj_weight, mlp_gain, up_weight, down_weight, head_weight,
 ):
     own, *away = cut(features)
+    down_t = down_weight.T
     arrived = [moved(piece, road, -1) for piece, road in zip(away, ROADS)]
     prepared = ready(
-        region, labels, attn_gain, mlp_gain, qkv_weight, proj_weight, up_weight, down_weight, head_weight
+        region, labels, attn_gain, mlp_gain, qkv_weight, proj_weight, up_weight, down_t, head_weight.T
     )
     scale = 1.0 / (WIN * WIN * NX * lax.axis_size("gz") * lax.axis_size("gy"))
-    own, *away = gradient((own, *arrived), prepared, (qkv_weight, proj_weight, up_weight, down_weight), scale)
+    own, *away = gradient((own, *arrived), prepared, (qkv_weight, proj_weight, up_weight, down_t), scale)
     arrived = [moved(piece, road, 1) for piece, road in zip(away, ROADS)]
     return join(own, *arrived)
 

time: 75 us -> 64.1 us (0.85)
  local copies, waits for them, and re-layouts: 10.1 us -> 1.61 us
  Pallas kernels: 33.4 us -> 28.9 us
  waiting for transfers between devices: 18.6 us -> 21.9 us
    unnamed x44 -> x20, local copies, waits for them, and re-layouts: 10.1 us -> 1.61 us
    ppermute x6, waiting for transfers between devices: 18.6 us -> 21.9 us  [moved(): return lax.ppermute(piece, axes if len(axes) > 1 else axes[0], route)]
    pallas_call x1, Pallas kernels: 2.2 us -> 0.35 us  [ready(): pl.pallas_call(ready_kernel, out_shape=out, in_specs=[VMEM] * 9, out_spec...]
    pallas_call x1, Pallas kernels: 1.77 us -> 0.11 us  [cut(): pl.pallas_call(cut_kernel, out_shape=[PIECE] * 4, in_specs=[VMEM], out_sp...]
    pallas_call x1, Pallas kernels: 1.84 us -> 0.83 us  [join(): pl.pallas_call(join_kernel, out_shape=out, in_specs=[VMEM] * 4, out_specs...]
  transfers between devices with their start and end apart: 6 -> 6, of which waited for: 4 -> 5; matrix products, arithmetic and copies ran while one was open for 2% -> 0% of each run, Pallas kernels for 3% -> 1%
where the time goes in v2:
time: 64.1 us; the launch traced here: 64 us
  Pallas kernels  28.9 us (45%)
  waiting for transfers between devices  21.9 us (34%)
  starting transfers between devices  11.4 us (18%)
  local copies, waits for them, and re-layouts  1.61 us (3%)
    pallas_call x1, Pallas kernels, gradient(): pl.pallas_call(functools.partial(main_kernel, scale), out_shape=[PIECE] *...  27.6 us
    ppermute x6, waiting for transfers between devices, moved(): return lax.ppermute(piece, axes if len(axes) > 1 else axes[0], route)  21.9 us
    ppermute x6, starting transfers between devices, moved(): return lax.ppermute(piece, axes if len(axes) > 1 else axes[0], route)  11.4 us
    unnamed x20, local copies, waits for them, and re-layouts  1.61 us
  transfers between devices with their start and end apart: 6, of which 5 were waited for; matrix products, arithmetic and copies ran while one was open for 0% of the time, Pallas kernels for 1%

profile of v2, /device:TPU:32, one launch (start us, length us, event | category | flops | bytes accessed | tf_op | source)
XLA Modules:
  0.0 64.0 jit_solution(5470336945870618990)
XLA Ops:
  0.0 1.0 %copy-done = bf16[7,7,2688]{2,1,0:T(8,128)(2,1)S(1)} copy-done((bf16[7,7,2688]{2,1,0:T(8,128)(2,1)S(1)}, bf16[7,7,2688]{2,1,0:T(8,128)(2,1)}, u32[]{:S(2)}) %copy-start) | copy-done | bytes 263448
  1.0 0.0 copy-start.5
  1.0 0.0 copy-start.6
  1.0 0.1 shard_map.100
  1.1 1.8 %collective-permute-start = (bf16[16,2688]{1,0:T(8,128)(2,1)S(1)}, bf16[16,2688]{1,0:T(8,128)(2,1)S(1)}, u32[]{:S(2)}, u32[]{:S(2)}) collective-permute-start(bf16[16,2688]{1,0:T(8,128)(2,1)S(1)} %get-tuple-element.24), channel_id=1, source_target_pairs={{16,0},{32,16},{48,32},{64,48},{80,64},{96,80},{112,96},{128,112},... | collective-permute-start | bytes 258056 | tf_op jit(solution)/shard_map/ppermute | solution.py:309
  2.9 8.8 %collective-permute-start.1 = (bf16[16,2688]{1,0:T(8,128)(2,1)S(1)}, bf16[16,2688]{1,0:T(8,128)(2,1)S(1)}, u32[]{:S(2)}, u32[]{:S(2)}) collective-permute-start(bf16[16,2688]{1,0:T(8,128)(2,1)S(1)} %get-tuple-element.25), channel_id=1, source_target_pairs={{1,0},{2,1},{3,2},{4,3},{5,4},{6,5},{7,6},{8,7},{9,8},{10,9},{11,1... | collective-permute-start | bytes 258056 | tf_op jit(solution)/shard_map/ppermute | solution.py:309
  11.7 0.6 collective-permute-start.2
  12.3 0.0 copy-done.1
  12.3 0.0 copy-done.2
  12.3 0.1 copy-done.7
  12.4 0.5 copy-done.8
  12.9 0.0 copy-done.9
  12.9 0.4 shard_map.101
  13.3 0.0 collective-permute-done.b_ref
  13.3 2.0 %collective-permute-done.1.c_ref = bf16[16,2688]{1,0:T(8,128)(2,1)S(1)} collective-permute-done((bf16[16,2688]{1,0:T(8,128)(2,1)S(1)}, bf16[16,2688]{1,0:T(8,128)(2,1)S(1)}, u32[]{:S(2)}, u32[]{:S(2)}) %collective-permute-start.1) | collective-permute-done | bytes 86048 | tf_op jit(solution)/shard_map/ppermute | solution.py:309
  15.3 0.9 %collective-permute-done.2.d_ref = bf16[16,2688]{1,0:T(8,128)(2,1)S(1)} collective-permute-done((bf16[16,2688]{1,0:T(8,128)(2,1)S(1)}, bf16[16,2688]{1,0:T(8,128)(2,1)S(1)}, u32[]{:S(2)}, u32[]{:S(2)}) %collective-permute-start.2) | collective-permute-done | bytes 86048 | tf_op jit(solution)/shard_map/ppermute | solution.py:309
  16.3 27.6 %shard_map.102 = (bf16[16,2688]{1,0:T(8,128)(2,1)S(1)}, bf16[16,2688]{1,0:T(8,128)(2,1)S(1)}, bf16[16,2688]{1,0:T(8,128)(2,1)S(1)}, bf16[16,2688]{1,0:T(8,128)(2,1)S(1)}) custom-call(bf16[16,2688]{1,0:T(8,128)(2,1)S(1)} %get-tuple-element.23.a_ref, bf16[16,2688]{1,0:T(8,128)(2,1)S(1)} %collective-permute-done.b_ref, ...), custom_call_target="tpu_custom_call" | custom-call | tf_op jit(solution)/shard_map/pallas_call | solution.py:279
  43.9 0.1 collective-permute-start.3
  44.0 0.1 collective-permute-start.4
  44.1 0.1 collective-permute-start.5
  44.2 5.8 %collective-permute-done.3.b_ref = bf16[16,2688]{1,0:T(8,128)(2,1)S(1)} collective-permute-done((bf16[16,2688]{1,0:T(8,128)(2,1)S(1)}, bf16[16,2688]{1,0:T(8,128)(2,1)S(1)}, u32[]{:S(2)}, u32[]{:S(2)}) %collective-permute-start.3) | collective-permute-done | bytes 86048 | tf_op jit(solution)/shard_map/ppermute | solution.py:309
  50.0 3.9 %collective-permute-done.4.c_ref = bf16[16,2688]{1,0:T(8,128)(2,1)S(1)} collective-permute-done((bf16[16,2688]{1,0:T(8,128)(2,1)S(1)}, bf16[16,2688]{1,0:T(8,128)(2,1)S(1)}, u32[]{:S(2)}, u32[]{:S(2)}) %collective-permute-start.4) | collective-permute-done | bytes 86048 | tf_op jit(solution)/shard_map/ppermute | solution.py:309
  53.9 9.2 %collective-permute-done.5.d_ref = bf16[16,2688]{1,0:T(8,128)(2,1)S(1)} collective-permute-done((bf16[16,2688]{1,0:T(8,128)(2,1)S(1)}, bf16[16,2688]{1,0:T(8,128)(2,1)S(1)}, u32[]{:S(2)}, u32[]{:S(2)}) %collective-permute-start.5) | collective-permute-done | bytes 86048 | tf_op jit(solution)/shard_map/ppermute | solution.py:309
  63.1 0.8 %shard_map.103 = bf16[7,7,2688]{2,1,0:T(8,128)(2,1)} custom-call(bf16[16,2688]{1,0:T(8,128)(2,1)S(1)} %get-tuple-element.37.a_ref, bf16[16,2688]{1,0:T(8,128)(2,1)S(1)} %collective-permute-done.3.b_ref, bf16[16,2688]{1,0:T(8,128)(2,1)S(1)} %collective-permute-done.4.c_ref, bf16[16,2688]{1,0:T(8,128)(2,1)S(1)} %collective-permute-done.5.d_ref), custom_call_target="tpu_custom_call" | custom-call | tf_op jit(solution)/shard_map/pallas_call | solution.py:261
  (12 shorter events, 0.0 us)
Async XLA Ops:
  0.0 1.0 %copy-start = (bf16[7,7,2688]{2,1,0:T(8,128)(2,1)S(1)}, bf16[7,7,2688]{2,1,0:T(8,128)(2,1)}, u32[]{:S(2)}) copy-start(bf16[7,7,2688]{2,1,0:T(8,128)(2,1)} %f_ref.1) | copy-start | bytes 790276
  1.0 11.3 %copy-start.1 = (bf16[96,288]{1,0:T(8,128)(2,1)S(1)}, bf16[96,288]{1,0:T(8,128)(2,1)}, u32[]{:S(2)}) copy-start(bf16[96,288]{1,0:T(8,128)(2,1)} %qkv_ref.3) | copy-start | bytes 165892
  1.0 11.3 %copy-start.2 = (bf16[96,384]{1,0:T(8,128)(2,1)S(1)}, bf16[96,384]{1,0:T(8,128)(2,1)}, u32[]{:S(2)}) copy-start(bf16[96,384]{1,0:T(8,128)(2,1)} %up_ref.3) | copy-start | bytes 221188
  1.0 11.3 %copy-start.3 = (bf16[384,96]{0,1:T(8,128)(2,1)S(1)}, bf16[384,96]{0,1:T(8,128)(2,1)}, u32[]{:S(2)}) copy-start(bf16[384,96]{0,1:T(8,128)(2,1)} %param.18) | copy-start | bytes 221188
  1.0 11.3 %copy-start.4 = (bf16[96,96]{1,0:T(8,128)(2,1)S(1)}, bf16[96,96]{1,0:T(8,128)(2,1)}, u32[]{:S(2)}) copy-start(bf16[96,96]{1,0:T(8,128)(2,1)} %proj_ref.3) | copy-start | bytes 55300
  1.0 11.3 %copy-start.5 = (s32[7,7,28]{2,1,0:T(8,128)S(1)}, s32[7,7,28]{2,1,0:T(8,128)}, u32[]{:S(2)}) copy-start(s32[7,7,28]{2,1,0:T(8,128)} %region_ref.1) | copy-start | bytes 16468
  1.0 11.3 %copy-start.6 = (s32[7,7,28]{2,1,0:T(8,128)S(1)}, s32[7,7,28]{2,1,0:T(8,128)}, u32[]{:S(2)}) copy-start(s32[7,7,28]{2,1,0:T(8,128)} %labels_ref.1) | copy-start | bytes 16468
  1.1 12.2 %collective-permute-start = (bf16[16,2688]{1,0:T(8,128)(2,1)S(1)}, bf16[16,2688]{1,0:T(8,128)(2,1)S(1)}, u32[]{:S(2)}, u32[]{:S(2)}) collective-permute-start(bf16[16,2688]{1,0:T(8,128)(2,1)S(1)} %get-tuple-element.24), channel_id=1, source_target_pairs={{16,0},{32,16},{48,32},{64,48},{80,64},{96,80},{112,96},{128,112},... | collective-permute-start | bytes 258056 | tf_op jit(solution)/shard_map/ppermute | solution.py:309
  2.9 12.4 %collective-permute-start.1 = (bf16[16,2688]{1,0:T(8,128)(2,1)S(1)}, bf16[16,2688]{1,0:T(8,128)(2,1)S(1)}, u32[]{:S(2)}, u32[]{:S(2)}) collective-permute-start(bf16[16,2688]{1,0:T(8,128)(2,1)S(1)} %get-tuple-element.25), channel_id=1, source_target_pairs={{1,0},{2,1},{3,2},{4,3},{5,4},{6,5},{7,6},{8,7},{9,8},{10,9},{11,1... | collective-permute-start | bytes 258056 | tf_op jit(solution)/shard_map/ppermute | solution.py:309
  11.7 0.7 %copy-start.7 = (bf16[96,14]{0,1:T(8,128)(2,1)S(1)}, bf16[96,14]{0,1:T(8,128)(2,1)}, u32[]{:S(2)}) copy-start(bf16[96,14]{0,1:T(8,128)(2,1)} %param.19) | copy-start | bytes 8068
  11.7 4.6 %collective-permute-start.2 = (bf16[16,2688]{1,0:T(8,128)(2,1)S(1)}, bf16[16,2688]{1,0:T(8,128)(2,1)S(1)}, u32[]{:S(2)}, u32[]{:S(2)}) collective-permute-start(bf16[16,2688]{1,0:T(8,128)(2,1)S(1)} %get-tuple-element.26), channel_id=1, source_target_pairs={{17,0},{18,1},{19,2},{20,3},{21,4},{22,5},{23,6},{24,7},{25,8},{26... | collective-permute-start | bytes 258056 | tf_op jit(solution)/shard_map/ppermute | solution.py:309
  12.3 0.7 %copy-start.8 = (f32[96]{0:T(128)S(1)}, f32[96]{0:T(128)}, u32[]{:S(2)}) copy-start(f32[96]{0:T(128)} %param.13) | copy-start | bytes 1156
  12.3 0.7 %copy-start.9 = (f32[96]{0:T(128)S(1)}, f32[96]{0:T(128)}, u32[]{:S(2)}) copy-start(f32[96]{0:T(128)} %param.16) | copy-start | bytes 1156
  43.9 6.1 %collective-permute-start.3 = (bf16[16,2688]{1,0:T(8,128)(2,1)S(1)}, bf16[16,2688]{1,0:T(8,128)(2,1)S(1)}, u32[]{:S(2)}, u32[]{:S(2)}) collective-permute-start(bf16[16,2688]{1,0:T(8,128)(2,1)S(1)} %get-tuple-element.38), channel_id=1, source_target_pairs={{240,0},{0,16},{16,32},{32,48},{48,64},{64,80},{80,96},{96,112},{1... | collective-permute-start | bytes 258056 | tf_op jit(solution)/shard_map/ppermute | solution.py:309
  44.0 9.9 %collective-permute-start.4 = (bf16[16,2688]{1,0:T(8,128)(2,1)S(1)}, bf16[16,2688]{1,0:T(8,128)(2,1)S(1)}, u32[]{:S(2)}, u32[]{:S(2)}) collective-permute-start(bf16[16,2688]{1,0:T(8,128)(2,1)S(1)} %get-tuple-element.39), channel_id=1, source_target_pairs={{15,0},{0,1},{1,2},{2,3},{3,4},{4,5},{5,6},{6,7},{7,8},{8,9},{9,10... | collective-permute-start | bytes 258056 | tf_op jit(solution)/shard_map/ppermute | solution.py:309
  44.1 19.0 %collective-permute-start.5 = (bf16[16,2688]{1,0:T(8,128)(2,1)S(1)}, bf16[16,2688]{1,0:T(8,128)(2,1)S(1)}, u32[]{:S(2)}, u32[]{:S(2)}) collective-permute-start(bf16[16,2688]{1,0:T(8,128)(2,1)S(1)} %get-tuple-element.40), channel_id=1, source_target_pairs={{255,0},{240,1},{241,2},{242,3},{243,4},{244,5},{245,6},{246,7},{2... | collective-permute-start | bytes 258056 | tf_op jit(solution)/shard_map/ppermute | solution.py:309

commit v3 on v2

--- a/solution.py
+++ b/solution.py
@@ -19,6 +19,8 @@
 WINDOWS = 4
 TOKENS = 343
 LANES = 384
+ROWS = 352
+PAIRS = 3
 SLOTS = 64
 WIDE = NX * C
 FAR = -(2.0**30)
@@ -135,14 +137,33 @@
     return inverse * (scaled - middle - unit * along)
 
 
-def headed(head, rows, extra):
-    parts = []
-    if head:
-        parts.append(jnp.zeros((HEAD * head, LANES), BF))
-    parts.append(rows)
-    if head < HEADS - 1:
-        parts.append(jnp.zeros((C - HEAD * head - HEAD, LANES), BF))
-    return jnp.concatenate(parts + [extra, jnp.zeros((16, LANES), BF)], axis=0)
+def paired(pair, rows, extra, second=None):
+    halves = []
+    for h in range(2):
+        head = 2 * pair + h
+        parts = [rows[HEAD * h : HEAD * h + HEAD], extra if h == 0 or second is None else second, jnp.zeros((16, LANES), BF)]
+        if head < HEADS - 1:
+            parts.insert(1, jnp.zeros((C - HEAD * head - HEAD, LANES), BF))
+        if head:
+            parts.insert(0, jnp.zeros((HEAD * head, LANES), BF))
+        halves.append(jnp.concatenate(parts, axis=0))
+    return jnp.concatenate(halves, axis=1)
+
+
+def blockdiag(rows):
+    blank = jnp.zeros((HEAD, LANES), BF)
+    first = jnp.concatenate([rows[:HEAD], blank], axis=1)
+    second = jnp.concatenate([blank, rows[HEAD:]], axis=1)
+    return jnp.concatenate([first, second], axis=0)
+
+
+def across(ref):
+    return jnp.concatenate([ref[w] for w in range(WINDOWS)], axis=1)
+
+
+def split(ref, values):
+    for w in range(WINDOWS):
+        ref[w] = values[:, LANES * w : LANES * w + LANES]
 
 
 def main_kernel(
@@ -150,7 +171,8 @@
     a_ref, b_ref, c_ref, d_ref, ids_ref, sel_ref, gain1_ref, gain2_ref,
     qkv_ref, qkvt_ref, proj_ref, projt_ref, up_ref, upt_ref, down_ref, downt_ref, head_ref, headt_ref,
     oa_ref, ob_ref, oc_ref, od_ref,
-    x_ref, grad_ref, e_ref, slope_ref, sides_ref,
+    x_ref, mixed_qkv_ref, keyst_ref, valuest_ref, side_ref, e_ref, ds_ref, attended_ref, inverse_ref,
+    d_hidden_ref, d_mixed_ref, extra_ref, d_qkv_ref, slope_ref,
 ):
     sel = sel_ref[...]
     rows = jnp.concatenate([r[...].astype(F32) for r in (a_ref, b_ref, c_ref, d_ref)], axis=0)
@@ -158,88 +180,140 @@
     for w in range(WINDOWS):
         cols = [(WIN * w + SHIFT + c) % NX for c in range(WIN)]
         wide = jnp.concatenate([tall[C * c : C * c + C] for c in cols], axis=1).astype(BF)
-        x_ref[w] = nn(wide, sel).astype(F32)
-
-    def window(w, carry):
-        gain1 = jnp.concatenate([gain1_ref[...]] * 3, axis=1)
-        gain2 = jnp.concatenate([gain2_ref[...]] * 3, axis=1)
-        x = x_ref[w]
-        unit1, inverse1, normed1 = norm(x, gain1)
-        region = ids_ref[pl.ds(w, 1), :]
-        labels = ids_ref[pl.ds(w + WINDOWS, 1), :]
-        qkv = nn(qkvt_ref[...], normed1)
-        queries = (qkv[:C] * (0.25 * LOG2E)).astype(BF)
-        keys = qkv[C : 2 * C].astype(BF)
-        values = qkv[2 * C :].astype(BF)
-        index = lax.broadcasted_iota(jnp.int32, (16, LANES), 0)
-        same = index.astype(F32) == region
+        x_ref[:, LANES * w : LANES * w + LANES] = nn(wide, sel)
+    e_ref[:, :, ROWS:, :] = jnp.zeros((WINDOWS, PAIRS, LANES - ROWS, 2 * LANES), BF)
+    ds_ref[:, ROWS:, :] = jnp.zeros((PAIRS, LANES - ROWS, 2 * LANES), BF)
+
+    gain1 = jnp.concatenate([gain1_ref[...]] * (3 * WINDOWS), axis=1)
+    gain2 = jnp.concatenate([gain2_ref[...]] * (3 * WINDOWS), axis=1)
+    unit1, inverse1, normed1 = norm(x_ref[...], gain1)
+    for k in range(3):
+        part = nn(qkvt_ref[C * k : C * k + C, :], normed1)
+        part = (part * (0.25 * LOG2E) if k == 0 else part).astype(BF)
+        for w in range(WINDOWS):
+            mixed_qkv_ref[w, C * k : C * k + C, :] = part[:, LANES * w : LANES * w + LANES]
+    index = lax.broadcasted_iota(jnp.int32, (16, LANES), 0)
+    ones = jnp.where(index < 2, 1.0, 0.0).astype(BF)
+    blank = jnp.zeros((16, LANES), BF)
+    for w in range(WINDOWS):
+        same = index.astype(F32) == ids_ref[w : w + 1, :]
         key_side = same.astype(F32).astype(BF)
-        query_side = jnp.where(same | (index > 4), 0.0, FAR).astype(BF)
-        ones = jnp.where(index < 2, 1.0, 0.0).astype(BF)
-        blank = jnp.zeros((16, LANES), BF)
-        keys_t = turned(jnp.concatenate([keys, key_side, blank], axis=0))
-        values_t = turned(jnp.concatenate([values, ones, blank], axis=0))
-        attended = []
-        inverse_sums = []
-        for h in range(HEADS):
-            own = slice(HEAD * h, HEAD * h + HEAD)
-            scores = nn(keys_t, headed(h, queries[own], query_side))
+        side_ref[w] = jnp.where(same | (index > 4), 0.0, FAR).astype(BF)
+        keyst_ref[w] = turned(jnp.concatenate([mixed_qkv_ref[w, C : 2 * C, :], key_side, blank], axis=0))[:ROWS]
+        valuest_ref[w] = turned(jnp.concatenate([mixed_qkv_ref[w, 2 * C :, :], ones, blank], axis=0))[:ROWS]
+
+    units = [(p, j) for p in range(PAIRS) for j in range(3)]
+
+    def forward(w, carry):
+        keys_t = keyst_ref[w]
+        side = side_ref[w]
+        spread = [paired(p, mixed_qkv_ref[w, 32 * p : 32 * p + 32, :], side) for p in range(PAIRS)]
+        scores_of = lambda p, j: nn(keys_t, spread[p][:, 256 * j : 256 * j + 256])
+        following = scores_of(*units[0])
+        mixed = []
+        for u, (p, j) in enumerate(units):
+            scores = following
+            if u + 1 < len(units):
+                following = scores_of(*units[u + 1])
             top = jnp.max(scores, axis=0, keepdims=True)
             raised = jnp.exp2(scores - top).astype(BF)
-            e_ref[h] = raised
-            mixed = nn(jnp.concatenate([values[own], ones], axis=0), raised)
-            inverse_sum = 1.0 / mixed[HEAD : HEAD + 1]
-            inverse_sums.append(inverse_sum)
-            attended.append((mixed[:HEAD] * inverse_sum).astype(BF))
-        hidden = x + nn(projt_ref[...], jnp.concatenate(attended, axis=0))
-        unit2, inverse2, normed2 = norm(hidden, gain2)
-        output = hidden
-        for j in range(3):
-            part = slice(128 * j, 128 * j + 128)
-            raised = nn(upt_ref[part, :], normed2)
-            below = 0.5 + 0.5 * lax.erf(raised * (0.5**0.5))
-            bell = jnp.exp(-0.5 * raised * raised) * 0.3989422804014327
-            slope_ref[part, :] = below + raised * bell
-            output = output + nn(downt_ref[:, part], (raised * below).astype(BF))
-        logits = nn(headt_ref[...], output.astype(BF))
-        kind = lax.broadcasted_iota(jnp.int32, (16, LANES), 0)
-        logits = jnp.where(kind < CLASSES, logits, -1e30)
-        powers = jnp.exp(logits - jnp.max(logits, axis=0, keepdims=True))
-        soft = powers / jnp.sum(powers, axis=0, keepdims=True)
-        at_label = (kind.astype(F32) == labels).astype(F32)
-        d_logits = jnp.where(labels >= 0.0, (soft - at_label) * scale, 0.0)
-        d_output = nn(head_ref[...], d_logits.astype(BF)).astype(BF)
-        d_normed2 = jnp.zeros((C, LANES), F32)
-        for j in range(3):
-            part = slice(128 * j, 128 * j + 128)
-            d_expanded = nn(down_ref[part, :], d_output)
-            d_raised = (d_expanded * slope_ref[part, :]).astype(BF)
-            d_normed2 = d_normed2 + nn(up_ref[:, part], d_raised)
-        d_hidden = d_output.astype(F32) + norm_back(d_normed2, unit2, inverse2, gain2)
-        d_attended = nn(proj_ref[...], d_hidden.astype(BF))
-        d_queries = []
-        d_keys = []
-        d_values = []
-        for h in range(HEADS):
-            own = slice(HEAD * h, HEAD * h + HEAD)
-            d_mixed = (d_attended[own] * inverse_sums[h]).astype(BF)
-            along = -jnp.sum(d_mixed.astype(F32) * attended[h].astype(F32), axis=0, keepdims=True)
-            coarse = along.astype(BF).astype(F32)
-            extra = jnp.where(index == 0, coarse, jnp.where(index == 1, along - coarse, 0.0)).astype(BF)
-            raised = e_ref[h]
-            d_scores = (raised.astype(F32) * nn(values_t, headed(h, d_mixed, extra))).astype(BF)
-            d_values.append(nt(d_mixed, raised))
-            d_queries.append(nn(keys[own], d_scores) * 0.25)
-            d_keys.append(nt(queries[own], d_scores) * LN2)
-        d_qkv = jnp.concatenate(d_queries + d_keys + d_values, axis=0).astype(BF)
-        d_normed1 = nn(qkv_ref[...], d_qkv)
-        grad_ref[w] = (d_hidden + norm_back(d_normed1, unit1, inverse1, gain1)).astype(BF)
+            e_ref[w, p, :ROWS, 256 * j : 256 * j + 256] = raised
+            values = mixed_qkv_ref[w, 2 * C + 32 * p : 2 * C + 32 * p + 32, :]
+            mixed.append(nn(jnp.concatenate([values, ones], axis=0)[:, :ROWS], raised))
+            if j == 2:
+                whole = jnp.concatenate(mixed, axis=1)
+                mixed = []
+                inverse_sum = 1.0 / whole[32:33]
+                for h in range(2):
+                    inverse_head = inverse_sum[:, LANES * h : LANES * h + LANES]
+                    inverse_ref[w, 2 * p + h : 2 * p + h + 1, :] = inverse_head
+                    own = whole[HEAD * h : HEAD * h + HEAD, LANES * h : LANES * h + LANES]
+                    place = 32 * p + HEAD * h
+                    attended_ref[w, place : place + HEAD, :] = (own * inverse_head).astype(BF)
         return carry
 
-    lax.fori_loop(0, WINDOWS, window, 0)
+    lax.fori_loop(0, WINDOWS, forward, 0)
+
+    attended = across(attended_ref)
+    hidden = x_ref[...] + nn(projt_ref[...], attended)
+    unit2, inverse2, normed2 = norm(hidden, gain2)
+    output = hidden
+    for j in range(3):
+        part = slice(128 * j, 128 * j + 128)
+        raised = nn(upt_ref[part, :], normed2)
+        below = 0.5 + 0.5 * lax.erf(raised * (0.5**0.5))
+        bell = jnp.exp(-0.5 * raised * raised) * 0.3989422804014327
+        slope_ref[part, :] = below + raised * bell
+        output = output + nn(downt_ref[:, part], (raised * below).astype(BF))
+    logits = nn(headt_ref[...], output.astype(BF))
+    labels = jnp.concatenate([ids_ref[WINDOWS + w : WINDOWS + w + 1, :] for w in range(WINDOWS)], axis=1)
+    kind = lax.broadcasted_iota(jnp.int32, (16, WINDOWS * LANES), 0)
+    logits = jnp.where(kind < CLASSES, logits, -1e30)
+    powers = jnp.exp(logits - jnp.max(logits, axis=0, keepdims=True))
+    soft = powers / jnp.sum(powers, axis=0, keepdims=True)
+    at_label = (kind.astype(F32) == labels).astype(F32)
+    d_logits = jnp.where(labels >= 0.0, (soft - at_label) * scale, 0.0)
+    d_output = nn(head_ref[...], d_logits.astype(BF)).astype(BF)
+    d_normed2 = jnp.zeros((C, WINDOWS * LANES), F32)
+    for j in range(3):
+        part = slice(128 * j, 128 * j + 128)
+        d_expanded = nn(down_ref[part, :], d_output)
+        d_raised = (d_expanded * slope_ref[part, :]).astype(BF)
+        d_normed2 = d_normed2 + nn(up_ref[:, part], d_raised)
+    d_hidden = d_output.astype(F32) + norm_back(d_normed2, unit2, inverse2, gain2)
+    d_hidden_ref[...] = d_hidden
+    d_attended = nn(proj_ref[...], d_hidden.astype(BF))
+    for h in range(HEADS):
+        own = slice(HEAD * h, HEAD * h + HEAD)
+        sums = jnp.concatenate([inverse_ref[w, h : h + 1, :] for w in range(WINDOWS)], axis=1)
+        d_mixed = (d_attended[own] * sums).astype(BF)
+        along = -jnp.sum(d_mixed.astype(F32) * attended[own].astype(F32), axis=0, keepdims=True)
+        coarse = along.astype(BF).astype(F32)
+        rest = along - coarse
+        for w in range(WINDOWS):
+            lanes = slice(LANES * w, LANES * w + LANES)
+            d_mixed_ref[w, own, :] = d_mixed[:, lanes]
+            extra = jnp.where(index == 0, coarse[:, lanes], jnp.where(index == 1, rest[:, lanes], 0.0))
+            extra_ref[w, own, :] = extra.astype(BF)
+
+    def backward(w, carry):
+        values_t = valuest_ref[w]
+        spread = [
+            paired(p, d_mixed_ref[w, 32 * p : 32 * p + 32, :], *[extra_ref[w, 32 * p + HEAD * h : 32 * p + HEAD * h + HEAD, :] for h in range(2)])
+            for p in range(PAIRS)
+        ]
+        weights_of = lambda p, j: nn(values_t, spread[p][:, 256 * j : 256 * j + 256])
+        following = weights_of(*units[0])
+        both = []
+        for u, (p, j) in enumerate(units):
+            own = slice(32 * p, 32 * p + 32)
+            cols = slice(256 * j, 256 * j + 256)
+            d_weights = following
+            if u + 1 < len(units):
+                following = weights_of(*units[u + 1])
+            d_scores = (e_ref[w, p, :ROWS, cols].astype(F32) * d_weights).astype(BF)
+            ds_ref[p, :ROWS, cols] = d_scores
+            keys = mixed_qkv_ref[w, C + 32 * p : C + 32 * p + 32, :]
+            both.append(nn(keys[:, :ROWS], d_scores))
+            if j == 2:
+                whole = jnp.concatenate(both, axis=1) * 0.25
+                both = []
+                d_queries = jnp.concatenate([whole[:HEAD, :LANES], whole[HEAD:, LANES:]], axis=0)
+                d_qkv_ref[w, own, :] = d_queries.astype(BF)
+                d_keys = nt(blockdiag(mixed_qkv_ref[w, own, :]), ds_ref[p]) * LN2
+                d_qkv_ref[w, C + 32 * p : C + 32 * p + 32, :] = d_keys.astype(BF)
+                d_values = nt(blockdiag(d_mixed_ref[w, own, :]), e_ref[w, p])
+                d_qkv_ref[w, 2 * C + 32 * p : 2 * C + 32 * p + 32, :] = d_values.astype(BF)
+        return carry
+
+    lax.fori_loop(0, WINDOWS, backward, 0)
+
+    d_normed1 = nn(qkv_ref[...], across(d_qkv_ref))
+    unit1, inverse1, normed1 = norm(x_ref[...], gain1)
+    grad = (d_hidden_ref[...] + norm_back(d_normed1, unit1, inverse1, gain1)).astype(BF)
     blocks = [None] * NX
     for w in range(WINDOWS):
-        wide = nt(grad_ref[w], sel)
+        wide = nt(grad[:, LANES * w : LANES * w + LANES], sel)
         for c in range(WIN):
             blocks[(WIN * w + SHIFT + c) % NX] = wide[:, SLOTS * c : SLOTS * c + SLOTS]
     rows = jnp.concatenate(blocks, axis=0).T
@@ -282,11 +356,20 @@
         in_specs=[VMEM] * 18,
         out_specs=[VMEM] * 4,
         scratch_shapes=[
-            pltpu.VMEM((WINDOWS, C, LANES), F32),
+            pltpu.VMEM((C, WINDOWS * LANES), F32),
+            pltpu.VMEM((WINDOWS, 3 * C, LANES), BF),
+            pltpu.VMEM((WINDOWS, ROWS, 128), BF),
+            pltpu.VMEM((WINDOWS, ROWS, 128), BF),
+            pltpu.VMEM((WINDOWS, 16, LANES), BF),
+            pltpu.VMEM((WINDOWS, PAIRS, LANES, 2 * LANES), BF),
+            pltpu.VMEM((PAIRS, LANES, 2 * LANES), BF),
             pltpu.VMEM((WINDOWS, C, LANES), BF),
-            pltpu.VMEM((HEADS, LANES, LANES), BF),
-            pltpu.VMEM((HID, LANES), F32),
-            pltpu.VMEM((16, LANES), F32),
+            pltpu.VMEM((WINDOWS, 8, LANES), F32),
+            pltpu.VMEM((C, WINDOWS * LANES), F32),
+            pltpu.VMEM((WINDOWS, C, LANES), BF),
+            pltpu.VMEM((WINDOWS, C, LANES), BF),
+            pltpu.VMEM((WINDOWS, 3 * C, LANES), BF),
+            pltpu.VMEM((HID, WINDOWS * LANES), F32),
         ],
         compiler_params=pltpu.CompilerParams(vmem_limit_bytes=32 * 2**20),
     )(

time: 64.1 us -> 56.7 us (0.88)
  Pallas kernels: 28.9 us -> 21.5 us
    pallas_call x1, Pallas kernels: 27.6 us -> 20.2 us  [gradient(): pl.pallas_call(functools.partial(main_kernel, scale), out_shape=[PIECE] *...]
where the time goes in v3:
time: 56.7 us; the launch traced here: 56.5 us
  waiting for transfers between devices  21.9 us (39%)
  Pallas kernels  21.5 us (38%)
  starting transfers between devices  11.4 us (20%)
  local copies, waits for them, and re-layouts  1.61 us (3%)
    ppermute x6, waiting for transfers between devices, moved(): return lax.ppermute(piece, axes if len(axes) > 1 else axes[0], route)  21.9 us
    pallas_call x1, Pallas kernels, gradient(): pl.pallas_call(functools.partial(main_kernel, scale), out_shape=[PIECE] *...  20.2 us
    ppermute x6, starting transfers between devices, moved(): return lax.ppermute(piece, axes if len(axes) > 1 else axes[0], route)  11.4 us
    unnamed x20, local copies, waits for them, and re-layouts  1.61 us
  transfers between devices with their start and end apart: 6, of which 5 were waited for; matrix products, arithmetic and copies ran while one was open for 0% of the time, Pallas kernels for 1%

profile of v3, /device:TPU:32, one launch (start us, length us, event | category | flops | bytes accessed | tf_op | source)
XLA Modules:
  0.0 56.5 jit_solution(11247557280269459482)
XLA Ops:
  0.0 1.0 %copy-done = bf16[7,7,2688]{2,1,0:T(8,128)(2,1)S(1)} copy-done((bf16[7,7,2688]{2,1,0:T(8,128)(2,1)S(1)}, bf16[7,7,2688]{2,1,0:T(8,128)(2,1)}, u32[]{:S(2)}) %copy-start) | copy-done | bytes 263448
  1.0 0.0 copy-start.5
  1.0 0.0 copy-start.6
  1.0 0.1 shard_map.100
  1.1 1.8 %collective-permute-start = (bf16[16,2688]{1,0:T(8,128)(2,1)S(1)}, bf16[16,2688]{1,0:T(8,128)(2,1)S(1)}, u32[]{:S(2)}, u32[]{:S(2)}) collective-permute-start(bf16[16,2688]{1,0:T(8,128)(2,1)S(1)} %get-tuple-element.24), channel_id=1, source_target_pairs={{16,0},{32,16},{48,32},{64,48},{80,64},{96,80},{112,96},{128,112},... | collective-permute-start | bytes 258056 | tf_op jit(solution)/shard_map/ppermute | solution.py:392
  2.9 8.8 %collective-permute-start.1 = (bf16[16,2688]{1,0:T(8,128)(2,1)S(1)}, bf16[16,2688]{1,0:T(8,128)(2,1)S(1)}, u32[]{:S(2)}, u32[]{:S(2)}) collective-permute-start(bf16[16,2688]{1,0:T(8,128)(2,1)S(1)} %get-tuple-element.25), channel_id=1, source_target_pairs={{1,0},{2,1},{3,2},{4,3},{5,4},{6,5},{7,6},{8,7},{9,8},{10,9},{11,1... | collective-permute-start | bytes 258056 | tf_op jit(solution)/shard_map/ppermute | solution.py:392
  11.7 0.6 %collective-permute-start.2 = (bf16[16,2688]{1,0:T(8,128)(2,1)S(1)}, bf16[16,2688]{1,0:T(8,128)(2,1)S(1)}, u32[]{:S(2)}, u32[]{:S(2)}) collective-permute-start(bf16[16,2688]{1,0:T(8,128)(2,1)S(1)} %get-tuple-element.26), channel_id=1, source_target_pairs={{17,0},{18,1},{19,2},{20,3},{21,4},{22,5},{23,6},{24,7},{25,8},{26... | collective-permute-start | bytes 258056 | tf_op jit(solution)/shard_map/ppermute | solution.py:392
  12.3 0.0 copy-done.1
  12.3 0.0 copy-done.2
  12.3 0.1 copy-done.7
  12.4 0.5 copy-done.8
  12.9 0.0 copy-done.9
  12.9 0.4 shard_map.101
  13.3 0.0 collective-permute-done.b_ref
  13.3 2.0 %collective-permute-done.1.c_ref = bf16[16,2688]{1,0:T(8,128)(2,1)S(1)} collective-permute-done((bf16[16,2688]{1,0:T(8,128)(2,1)S(1)}, bf16[16,2688]{1,0:T(8,128)(2,1)S(1)}, u32[]{:S(2)}, u32[]{:S(2)}) %collective-permute-start.1) | collective-permute-done | bytes 86048 | tf_op jit(solution)/shard_map/ppermute | solution.py:392
  15.3 0.9 %collective-permute-done.2.d_ref = bf16[16,2688]{1,0:T(8,128)(2,1)S(1)} collective-permute-done((bf16[16,2688]{1,0:T(8,128)(2,1)S(1)}, bf16[16,2688]{1,0:T(8,128)(2,1)S(1)}, u32[]{:S(2)}, u32[]{:S(2)}) %collective-permute-start.2) | collective-permute-done | bytes 86048 | tf_op jit(solution)/shard_map/ppermute | solution.py:392
  16.3 20.2 %shard_map.102 = (bf16[16,2688]{1,0:T(8,128)(2,1)S(1)}, bf16[16,2688]{1,0:T(8,128)(2,1)S(1)}, bf16[16,2688]{1,0:T(8,128)(2,1)S(1)}, bf16[16,2688]{1,0:T(8,128)(2,1)S(1)}) custom-call(bf16[16,2688]{1,0:T(8,128)(2,1)S(1)} %get-tuple-element.23.a_ref, bf16[16,2688]{1,0:T(8,128)(2,1)S(1)} %collective-permute-done.b_ref, ...), custom_call_target="tpu_custom_call" | custom-call | tf_op jit(solution)/shard_map/pallas_call | solution.py:353
  36.5 0.1 collective-permute-start.3
  36.5 0.1 collective-permute-start.4
  36.6 0.1 collective-permute-start.5
  36.7 5.8 %collective-permute-done.3.b_ref = bf16[16,2688]{1,0:T(8,128)(2,1)S(1)} collective-permute-done((bf16[16,2688]{1,0:T(8,128)(2,1)S(1)}, bf16[16,2688]{1,0:T(8,128)(2,1)S(1)}, u32[]{:S(2)}, u32[]{:S(2)}) %collective-permute-start.3) | collective-permute-done | bytes 86048 | tf_op jit(solution)/shard_map/ppermute | solution.py:392
  42.6 3.9 %collective-permute-done.4.c_ref = bf16[16,2688]{1,0:T(8,128)(2,1)S(1)} collective-permute-done((bf16[16,2688]{1,0:T(8,128)(2,1)S(1)}, bf16[16,2688]{1,0:T(8,128)(2,1)S(1)}, u32[]{:S(2)}, u32[]{:S(2)}) %collective-permute-start.4) | collective-permute-done | bytes 86048 | tf_op jit(solution)/shard_map/ppermute | solution.py:392
  46.5 9.2 %collective-permute-done.5.d_ref = bf16[16,2688]{1,0:T(8,128)(2,1)S(1)} collective-permute-done((bf16[16,2688]{1,0:T(8,128)(2,1)S(1)}, bf16[16,2688]{1,0:T(8,128)(2,1)S(1)}, u32[]{:S(2)}, u32[]{:S(2)}) %collective-permute-start.5) | collective-permute-done | bytes 86048 | tf_op jit(solution)/shard_map/ppermute | solution.py:392
  55.7 0.8 %shard_map.103 = bf16[7,7,2688]{2,1,0:T(8,128)(2,1)} custom-call(bf16[16,2688]{1,0:T(8,128)(2,1)S(1)} %get-tuple-element.37.a_ref, bf16[16,2688]{1,0:T(8,128)(2,1)S(1)} %collective-permute-done.3.b_ref, bf16[16,2688]{1,0:T(8,128)(2,1)S(1)} %collective-permute-done.4.c_ref, bf16[16,2688]{1,0:T(8,128)(2,1)S(1)} %collective-permute-done.5.d_ref), custom_call_target="tpu_custom_call" | custom-call | tf_op jit(solution)/shard_map/pallas_call | solution.py:335
  (12 shorter events, 0.0 us)
Async XLA Ops:
  0.0 1.0 %copy-start = (bf16[7,7,2688]{2,1,0:T(8,128)(2,1)S(1)}, bf16[7,7,2688]{2,1,0:T(8,128)(2,1)}, u32[]{:S(2)}) copy-start(bf16[7,7,2688]{2,1,0:T(8,128)(2,1)} %f_ref.1) | copy-start | bytes 790276
  1.0 11.3 %copy-start.1 = (bf16[96,288]{1,0:T(8,128)(2,1)S(1)}, bf16[96,288]{1,0:T(8,128)(2,1)}, u32[]{:S(2)}) copy-start(bf16[96,288]{1,0:T(8,128)(2,1)} %qkv_ref.3) | copy-start | bytes 165892
  1.0 11.3 %copy-start.2 = (bf16[96,384]{1,0:T(8,128)(2,1)S(1)}, bf16[96,384]{1,0:T(8,128)(2,1)}, u32[]{:S(2)}) copy-start(bf16[96,384]{1,0:T(8,128)(2,1)} %up_ref.3) | copy-start | bytes 221188
  1.0 11.3 %copy-start.3 = (bf16[384,96]{0,1:T(8,128)(2,1)S(1)}, bf16[384,96]{0,1:T(8,128)(2,1)}, u32[]{:S(2)}) copy-start(bf16[384,96]{0,1:T(8,128)(2,1)} %param.18) | copy-start | bytes 221188
  1.0 11.3 %copy-start.4 = (bf16[96,96]{1,0:T(8,128)(2,1)S(1)}, bf16[96,96]{1,0:T(8,128)(2,1)}, u32[]{:S(2)}) copy-start(bf16[96,96]{1,0:T(8,128)(2,1)} %proj_ref.3) | copy-start | bytes 55300
  1.0 11.3 %copy-start.5 = (s32[7,7,28]{2,1,0:T(8,128)S(1)}, s32[7,7,28]{2,1,0:T(8,128)}, u32[]{:S(2)}) copy-start(s32[7,7,28]{2,1,0:T(8,128)} %region_ref.1) | copy-start | bytes 16468
  1.0 11.3 %copy-start.6 = (s32[7,7,28]{2,1,0:T(8,128)S(1)}, s32[7,7,28]{2,1,0:T(8,128)}, u32[]{:S(2)}) copy-start(s32[7,7,28]{2,1,0:T(8,128)} %labels_ref.1) | copy-start | bytes 16468
  1.1 12.2 %collective-permute-start = (bf16[16,2688]{1,0:T(8,128)(2,1)S(1)}, bf16[16,2688]{1,0:T(8,128)(2,1)S(1)}, u32[]{:S(2)}, u32[]{:S(2)}) collective-permute-start(bf16[16,2688]{1,0:T(8,128)(2,1)S(1)} %get-tuple-element.24), channel_id=1, source_target_pairs={{16,0},{32,16},{48,32},{64,48},{80,64},{96,80},{112,96},{128,112},... | collective-permute-start | bytes 258056 | tf_op jit(solution)/shard_map/ppermute | solution.py:392
  2.9 12.4 %collective-permute-start.1 = (bf16[16,2688]{1,0:T(8,128)(2,1)S(1)}, bf16[16,2688]{1,0:T(8,128)(2,1)S(1)}, u32[]{:S(2)}, u32[]{:S(2)}) collective-permute-start(bf16[16,2688]{1,0:T(8,128)(2,1)S(1)} %get-tuple-element.25), channel_id=1, source_target_pairs={{1,0},{2,1},{3,2},{4,3},{5,4},{6,5},{7,6},{8,7},{9,8},{10,9},{11,1... | collective-permute-start | bytes 258056 | tf_op jit(solution)/shard_map/ppermute | solution.py:392
  11.7 0.7 %copy-start.7 = (bf16[96,14]{0,1:T(8,128)(2,1)S(1)}, bf16[96,14]{0,1:T(8,128)(2,1)}, u32[]{:S(2)}) copy-start(bf16[96,14]{0,1:T(8,128)(2,1)} %param.19) | copy-start | bytes 8068
  11.7 4.6 %collective-permute-start.2 = (bf16[16,2688]{1,0:T(8,128)(2,1)S(1)}, bf16[16,2688]{1,0:T(8,128)(2,1)S(1)}, u32[]{:S(2)}, u32[]{:S(2)}) collective-permute-start(bf16[16,2688]{1,0:T(8,128)(2,1)S(1)} %get-tuple-element.26), channel_id=1, source_target_pairs={{17,0},{18,1},{19,2},{20,3},{21,4},{22,5},{23,6},{24,7},{25,8},{26... | collective-permute-start | bytes 258056 | tf_op jit(solution)/shard_map/ppermute | solution.py:392
  12.3 0.7 %copy-start.8 = (f32[96]{0:T(128)S(1)}, f32[96]{0:T(128)}, u32[]{:S(2)}) copy-start(f32[96]{0:T(128)} %param.13) | copy-start | bytes 1156
  12.3 0.7 %copy-start.9 = (f32[96]{0:T(128)S(1)}, f32[96]{0:T(128)}, u32[]{:S(2)}) copy-start(f32[96]{0:T(128)} %param.16) | copy-start | bytes 1156
  36.5 6.1 %collective-permute-start.3 = (bf16[16,2688]{1,0:T(8,128)(2,1)S(1)}, bf16[16,2688]{1,0:T(8,128)(2,1)S(1)}, u32[]{:S(2)}, u32[]{:S(2)}) collective-permute-start(bf16[16,2688]{1,0:T(8,128)(2,1)S(1)} %get-tuple-element.38), channel_id=1, source_target_pairs={{240,0},{0,16},{16,32},{32,48},{48,64},{64,80},{80,96},{96,112},{1... | collective-permute-start | bytes 258056 | tf_op jit(solution)/shard_map/ppermute | solution.py:392
  36.5 9.9 %collective-permute-start.4 = (bf16[16,2688]{1,0:T(8,128)(2,1)S(1)}, bf16[16,2688]{1,0:T(8,128)(2,1)S(1)}, u32[]{:S(2)}, u32[]{:S(2)}) collective-permute-start(bf16[16,2688]{1,0:T(8,128)(2,1)S(1)} %get-tuple-element.39), channel_id=1, source_target_pairs={{15,0},{0,1},{1,2},{2,3},{3,4},{4,5},{5,6},{6,7},{7,8},{8,9},{9,10... | collective-permute-start | bytes 258056 | tf_op jit(solution)/shard_map/ppermute | solution.py:392
  36.6 19.0 %collective-permute-start.5 = (bf16[16,2688]{1,0:T(8,128)(2,1)S(1)}, bf16[16,2688]{1,0:T(8,128)(2,1)S(1)}, u32[]{:S(2)}, u32[]{:S(2)}) collective-permute-start(bf16[16,2688]{1,0:T(8,128)(2,1)S(1)} %get-tuple-element.40), channel_id=1, source_target_pairs={{255,0},{240,1},{241,2},{242,3},{243,4},{244,5},{245,6},{246,7},{2... | collective-permute-start | bytes 258056 | tf_op jit(solution)/shard_map/ppermute | solution.py:392

commit v4 on v3

--- a/solution.py
+++ b/solution.py
@@ -23,6 +23,7 @@
 PAIRS = 3
 SLOTS = 64
 WIDE = NX * C
+HALF = 1408
 FAR = -(2.0**30)
 LOG2E = 1.4426950408889634
 LN2 = 0.6931471805599453
@@ -46,20 +47,42 @@
     return jnp.concatenate(parts, axis=0)
 
 
+def packed(rows, count):
+    if count == 12:
+        rest = rows[8:12]
+        last = jnp.concatenate([rest[:, HALF:], jnp.zeros((4, 2 * HALF - WIDE), F32)], axis=1)
+        tail = jnp.concatenate([rest[:, :HALF], last], axis=0)
+    else:
+        parts = [rows[8:9, LANES * k : LANES * k + LANES] for k in range(WIN)]
+        tail = jnp.concatenate(parts + [jnp.zeros((1, LANES), F32)], axis=0)
+    return jnp.concatenate([rows[:8], tail], axis=1).astype(BF)
+
+
+def unpacked(ref, count):
+    values = ref[...].astype(F32)
+    tail = values[:, WIDE:]
+    if count == 12:
+        rest = jnp.concatenate([tail[:4], tail[4:8, : WIDE - HALF]], axis=1)
+    else:
+        rest = jnp.concatenate([tail[k : k + 1] for k in range(WIN)], axis=1)
+    blank = jnp.zeros((16 - count, WIDE), F32)
+    return jnp.concatenate([values[:, :WIDE], rest, blank], axis=0)
+
+
 def cut_kernel(f_ref, a_ref, b_ref, c_ref, d_ref):
     cells = [f_ref[d].astype(F32) for d in range(WIN)]
     low, high = range(SHIFT), range(SHIFT, WIN)
     a_ref[...] = piece_rows(cells, high, (SHIFT, WIN)).astype(BF)
-    b_ref[...] = piece_rows(cells, low, (SHIFT, WIN)).astype(BF)
-    c_ref[...] = piece_rows(cells, high, (0, SHIFT)).astype(BF)
-    d_ref[...] = piece_rows(cells, low, (0, SHIFT)).astype(BF)
+    b_ref[...] = packed(piece_rows(cells, low, (SHIFT, WIN)), 12)
+    c_ref[...] = packed(piece_rows(cells, high, (0, SHIFT)), 12)
+    d_ref[...] = packed(piece_rows(cells, low, (0, SHIFT)), 9)
 
 
 def join_kernel(a_ref, b_ref, c_ref, d_ref, out_ref):
     a = a_ref[...].astype(F32)
-    b = b_ref[...].astype(F32)
-    c = c_ref[...].astype(F32)
-    d = d_ref[...].astype(F32)
+    b = unpacked(b_ref, 12)
+    c = unpacked(c_ref, 12)
+    d = unpacked(d_ref, 9)
     for i in range(WIN):
         if i < SHIFT:
             left, right, k = d, b, i
@@ -175,7 +198,8 @@
     d_hidden_ref, d_mixed_ref, extra_ref, d_qkv_ref, slope_ref,
 ):
     sel = sel_ref[...]
-    rows = jnp.concatenate([r[...].astype(F32) for r in (a_ref, b_ref, c_ref, d_ref)], axis=0)
+    pieces = [a_ref[...].astype(F32), unpacked(b_ref, 12), unpacked(c_ref, 12), unpacked(d_ref, 9)]
+    rows = jnp.concatenate(pieces, axis=0)
     tall = rows.T
     for w in range(WINDOWS):
         cols = [(WIN * w + SHIFT + c) % NX for c in range(WIN)]
@@ -317,17 +341,18 @@
         for c in range(WIN):
             blocks[(WIN * w + SHIFT + c) % NX] = wide[:, SLOTS * c : SLOTS * c + SLOTS]
     rows = jnp.concatenate(blocks, axis=0).T
-    for k, ref in enumerate((oa_ref, ob_ref, oc_ref, od_ref)):
-        ref[...] = rows[16 * k : 16 * k + 16].astype(BF)
+    oa_ref[...] = rows[:16].astype(BF)
+    for k, (ref, count) in enumerate(((ob_ref, 12), (oc_ref, 12), (od_ref, 9))):
+        ref[...] = packed(rows[16 * k + 16 : 16 * k + 32], count)
 
 
 VMEM = pl.BlockSpec(memory_space=pltpu.VMEM)
 SMALL = pltpu.CompilerParams(vmem_limit_bytes=8 * 2**20)
-PIECE = jax.ShapeDtypeStruct((16, WIDE), BF)
+PIECES = [jax.ShapeDtypeStruct(s, BF) for s in ((16, WIDE), (8, 4096), (8, 4096), (8, 3072))]
 
 
 def cut(features):
-    return pl.pallas_call(cut_kernel, out_shape=[PIECE] * 4, in_specs=[VMEM], out_specs=[VMEM] * 4, compiler_params=SMALL)(features)
+    return pl.pallas_call(cut_kernel, out_shape=PIECES, in_specs=[VMEM], out_specs=[VMEM] * 4, compiler_params=SMALL)(features)
 
 
 def join(*pieces):
@@ -352,7 +377,7 @@
     qkv_weight, proj_weight, up_weight, down_t = weights
     return pl.pallas_call(
         functools.partial(main_kernel, scale),
-        out_shape=[PIECE] * 4,
+        out_shape=PIECES,
         in_specs=[VMEM] * 18,
         out_specs=[VMEM] * 4,
         scratch_shapes=[

time: 56.7 us -> 52.6 us (0.928)
  waiting for transfers between devices: 21.9 us -> 17.8 us
    ppermute x6, waiting for transfers between devices: 21.9 us -> 17.8 us  [moved(): return lax.ppermute(piece, axes if len(axes) > 1 else axes[0], route)]
  transfers between devices with their start and end apart: 6 -> 6, of which waited for: 5 -> 2; matrix products, arithmetic and copies ran while one was open for 0% -> 0% of each run, Pallas kernels for 1% -> 1%
where the time goes in v4:
time: 52.6 us; the launch traced here: 52.4 us
  Pallas kernels  21.5 us (41%)
  waiting for transfers between devices  17.8 us (34%)
  starting transfers between devices  11.4 us (22%)
  local copies, waits for them, and re-layouts  1.61 us (3%)
    pallas_call x1, Pallas kernels, gradient(): pl.pallas_call(functools.partial(main_kernel, scale), out_shape=PIECES, i...  20.2 us
    ppermute x6, waiting for transfers between devices, moved(): return lax.ppermute(piece, axes if len(axes) > 1 else axes[0], route)  17.8 us
    ppermute x6, starting transfers between devices, moved(): return lax.ppermute(piece, axes if len(axes) > 1 else axes[0], route)  11.4 us
    unnamed x20, local copies, waits for them, and re-layouts  1.61 us
  transfers between devices with their start and end apart: 6, of which 2 were waited for; matrix products, arithmetic and copies ran while one was open for 0% of the time, Pallas kernels for 1%

profile of v4, /device:TPU:32, one launch (start us, length us, event | category | flops | bytes accessed | tf_op | source)
XLA Modules:
  0.0 52.4 jit_solution(2214460443334408551)
XLA Ops:
  0.0 1.0 %copy-done = bf16[7,7,2688]{2,1,0:T(8,128)(2,1)S(1)} copy-done((bf16[7,7,2688]{2,1,0:T(8,128)(2,1)S(1)}, bf16[7,7,2688]{2,1,0:T(8,128)(2,1)}, u32[]{:S(2)}) %copy-start) | copy-done | bytes 263448
  1.0 0.0 copy-start.5
  1.0 0.0 copy-start.6
  1.0 0.1 shard_map.100
  1.1 1.8 %collective-permute-start = (bf16[8,4096]{1,0:T(8,128)(2,1)S(1)}, bf16[8,4096]{1,0:T(8,128)(2,1)S(1)}, u32[]{:S(2)}, u32[]{:S(2)}) collective-permute-start(bf16[8,4096]{1,0:T(8,128)(2,1)S(1)} %get-tuple-element.24), channel_id=1, source_target_pairs={{16,0},{32,16},{48,32},{64,48},{80,64},{96,80},{112,96},{128,112},... | collective-permute-start | bytes 196616 | tf_op jit(solution)/shard_map/ppermute | solution.py:417
  2.9 8.8 %collective-permute-start.1 = (bf16[8,4096]{1,0:T(8,128)(2,1)S(1)}, bf16[8,4096]{1,0:T(8,128)(2,1)S(1)}, u32[]{:S(2)}, u32[]{:S(2)}) collective-permute-start(bf16[8,4096]{1,0:T(8,128)(2,1)S(1)} %get-tuple-element.25), channel_id=1, source_target_pairs={{1,0},{2,1},{3,2},{4,3},{5,4},{6,5},{7,6},{8,7},{9,8},{10,9},{11,1... | collective-permute-start | bytes 196616 | tf_op jit(solution)/shard_map/ppermute | solution.py:417
  11.7 0.6 %collective-permute-start.2 = (bf16[8,3072]{1,0:T(8,128)(2,1)S(1)}, bf16[8,3072]{1,0:T(8,128)(2,1)S(1)}, u32[]{:S(2)}, u32[]{:S(2)}) collective-permute-start(bf16[8,3072]{1,0:T(8,128)(2,1)S(1)} %get-tuple-element.26), channel_id=1, source_target_pairs={{17,0},{18,1},{19,2},{20,3},{21,4},{22,5},{23,6},{24,7},{25,8},{26... | collective-permute-start | bytes 147464 | tf_op jit(solution)/shard_map/ppermute | solution.py:417
  12.3 0.0 copy-done.1
  12.3 0.0 copy-done.2
  12.3 0.1 copy-done.7
  12.4 0.5 %copy-done.8 = f32[96]{0:T(128)S(1)} copy-done((f32[96]{0:T(128)S(1)}, f32[96]{0:T(128)}, u32[]{:S(2)}) %copy-start.8) | copy-done | bytes 408
  12.9 0.0 copy-done.9
  12.9 0.4 shard_map.101
  13.3 1.9 %collective-permute-done.2.d_ref = bf16[8,3072]{1,0:T(8,128)(2,1)S(1)} collective-permute-done((bf16[8,3072]{1,0:T(8,128)(2,1)S(1)}, bf16[8,3072]{1,0:T(8,128)(2,1)S(1)}, u32[]{:S(2)}, u32[]{:S(2)}) %collective-permute-start.2) | collective-permute-done | bytes 49184 | tf_op jit(solution)/shard_map/ppermute | solution.py:417
  15.2 0.0 collective-permute-done.b_ref
  15.2 0.0 collective-permute-done.1.c_ref
  15.2 20.2 %shard_map.102 = (bf16[16,2688]{1,0:T(8,128)(2,1)S(1)}, bf16[8,4096]{1,0:T(8,128)(2,1)S(1)}, bf16[8,4096]{1,0:T(8,128)(2,1)S(1)}, bf16[8,3072]{1,0:T(8,128)(2,1)S(1)}) custom-call(bf16[16,2688]{1,0:T(8,128)(2,1)S(1)} %get-tuple-element.23.a_ref, bf16[8,4096]{1,0:T(8,128)(2,1)S(1)} %collective-permute-done.b_ref, ...), custom_call_target="tpu_custom_call" | custom-call | tf_op jit(solution)/shard_map/pallas_call | solution.py:378
  35.4 0.1 collective-permute-start.3
  35.5 0.2 collective-permute-start.4
  35.7 0.0 collective-permute-start.5
  35.7 15.9 %collective-permute-done.5.d_ref = bf16[8,3072]{1,0:T(8,128)(2,1)S(1)} collective-permute-done((bf16[8,3072]{1,0:T(8,128)(2,1)S(1)}, bf16[8,3072]{1,0:T(8,128)(2,1)S(1)}, u32[]{:S(2)}, u32[]{:S(2)}) %collective-permute-start.5) | collective-permute-done | bytes 49184 | tf_op jit(solution)/shard_map/ppermute | solution.py:417
  51.6 0.0 collective-permute-done.3.b_ref
  51.6 0.0 collective-permute-done.4.c_ref
  51.6 0.8 %shard_map.103 = bf16[7,7,2688]{2,1,0:T(8,128)(2,1)} custom-call(bf16[16,2688]{1,0:T(8,128)(2,1)S(1)} %get-tuple-element.37.a_ref, bf16[8,4096]{1,0:T(8,128)(2,1)S(1)} %collective-permute-done.3.b_ref, bf16[8,4096]{1,0:T(8,128)(2,1)S(1)} %collective-permute-done.4.c_ref, bf16[8,3072]{1,0:T(8,128)(2,1)S(1)} %collective-permute-done.5.d_ref), custom_call_target="tpu_custom_call" | custom-call | tf_op jit(solution)/shard_map/pallas_call | solution.py:360
  (12 shorter events, 0.0 us)
Async XLA Ops:
  0.0 1.0 %copy-start = (bf16[7,7,2688]{2,1,0:T(8,128)(2,1)S(1)}, bf16[7,7,2688]{2,1,0:T(8,128)(2,1)}, u32[]{:S(2)}) copy-start(bf16[7,7,2688]{2,1,0:T(8,128)(2,1)} %f_ref.1) | copy-start | bytes 790276
  1.0 11.3 %copy-start.1 = (bf16[96,288]{1,0:T(8,128)(2,1)S(1)}, bf16[96,288]{1,0:T(8,128)(2,1)}, u32[]{:S(2)}) copy-start(bf16[96,288]{1,0:T(8,128)(2,1)} %qkv_ref.3) | copy-start | bytes 165892
  1.0 11.3 %copy-start.2 = (bf16[96,384]{1,0:T(8,128)(2,1)S(1)}, bf16[96,384]{1,0:T(8,128)(2,1)}, u32[]{:S(2)}) copy-start(bf16[96,384]{1,0:T(8,128)(2,1)} %up_ref.3) | copy-start | bytes 221188
  1.0 11.3 %copy-start.3 = (bf16[384,96]{0,1:T(8,128)(2,1)S(1)}, bf16[384,96]{0,1:T(8,128)(2,1)}, u32[]{:S(2)}) copy-start(bf16[384,96]{0,1:T(8,128)(2,1)} %param.18) | copy-start | bytes 221188
  1.0 11.3 %copy-start.4 = (bf16[96,96]{1,0:T(8,128)(2,1)S(1)}, bf16[96,96]{1,0:T(8,128)(2,1)}, u32[]{:S(2)}) copy-start(bf16[96,96]{1,0:T(8,128)(2,1)} %proj_ref.3) | copy-start | bytes 55300
  1.0 11.3 %copy-start.5 = (s32[7,7,28]{2,1,0:T(8,128)S(1)}, s32[7,7,28]{2,1,0:T(8,128)}, u32[]{:S(2)}) copy-start(s32[7,7,28]{2,1,0:T(8,128)} %region_ref.1) | copy-start | bytes 16468
  1.0 11.3 %copy-start.6 = (s32[7,7,28]{2,1,0:T(8,128)S(1)}, s32[7,7,28]{2,1,0:T(8,128)}, u32[]{:S(2)}) copy-start(s32[7,7,28]{2,1,0:T(8,128)} %labels_ref.1) | copy-start | bytes 16468
  1.1 14.1 %collective-permute-start = (bf16[8,4096]{1,0:T(8,128)(2,1)S(1)}, bf16[8,4096]{1,0:T(8,128)(2,1)S(1)}, u32[]{:S(2)}, u32[]{:S(2)}) collective-permute-start(bf16[8,4096]{1,0:T(8,128)(2,1)S(1)} %get-tuple-element.24), channel_id=1, source_target_pairs={{16,0},{32,16},{48,32},{64,48},{80,64},{96,80},{112,96},{128,112},... | collective-permute-start | bytes 196616 | tf_op jit(solution)/shard_map/ppermute | solution.py:417
  2.9 12.3 %collective-permute-start.1 = (bf16[8,4096]{1,0:T(8,128)(2,1)S(1)}, bf16[8,4096]{1,0:T(8,128)(2,1)S(1)}, u32[]{:S(2)}, u32[]{:S(2)}) collective-permute-start(bf16[8,4096]{1,0:T(8,128)(2,1)S(1)} %get-tuple-element.25), channel_id=1, source_target_pairs={{1,0},{2,1},{3,2},{4,3},{5,4},{6,5},{7,6},{8,7},{9,8},{10,9},{11,1... | collective-permute-start | bytes 196616 | tf_op jit(solution)/shard_map/ppermute | solution.py:417
  11.7 0.7 %copy-start.7 = (bf16[96,14]{0,1:T(8,128)(2,1)S(1)}, bf16[96,14]{0,1:T(8,128)(2,1)}, u32[]{:S(2)}) copy-start(bf16[96,14]{0,1:T(8,128)(2,1)} %param.19) | copy-start | bytes 8068
  11.7 3.5 %collective-permute-start.2 = (bf16[8,3072]{1,0:T(8,128)(2,1)S(1)}, bf16[8,3072]{1,0:T(8,128)(2,1)S(1)}, u32[]{:S(2)}, u32[]{:S(2)}) collective-permute-start(bf16[8,3072]{1,0:T(8,128)(2,1)S(1)} %get-tuple-element.26), channel_id=1, source_target_pairs={{17,0},{18,1},{19,2},{20,3},{21,4},{22,5},{23,6},{24,7},{25,8},{26... | collective-permute-start | bytes 147464 | tf_op jit(solution)/shard_map/ppermute | solution.py:417
  12.3 0.7 %copy-start.8 = (f32[96]{0:T(128)S(1)}, f32[96]{0:T(128)}, u32[]{:S(2)}) copy-start(f32[96]{0:T(128)} %param.13) | copy-start | bytes 1156
  12.3 0.7 %copy-start.9 = (f32[96]{0:T(128)S(1)}, f32[96]{0:T(128)}, u32[]{:S(2)}) copy-start(f32[96]{0:T(128)} %param.16) | copy-start | bytes 1156
  35.4 16.2 %collective-permute-start.3 = (bf16[8,4096]{1,0:T(8,128)(2,1)S(1)}, bf16[8,4096]{1,0:T(8,128)(2,1)S(1)}, u32[]{:S(2)}, u32[]{:S(2)}) collective-permute-start(bf16[8,4096]{1,0:T(8,128)(2,1)S(1)} %get-tuple-element.38), channel_id=1, source_target_pairs={{240,0},{0,16},{16,32},{32,48},{48,64},{64,80},{80,96},{96,112},{1... | collective-permute-start | bytes 196616 | tf_op jit(solution)/shard_map/ppermute | solution.py:417
  35.5 16.1 %collective-permute-start.4 = (bf16[8,4096]{1,0:T(8,128)(2,1)S(1)}, bf16[8,4096]{1,0:T(8,128)(2,1)S(1)}, u32[]{:S(2)}, u32[]{:S(2)}) collective-permute-start(bf16[8,4096]{1,0:T(8,128)(2,1)S(1)} %get-tuple-element.39), channel_id=1, source_target_pairs={{15,0},{0,1},{1,2},{2,3},{3,4},{4,5},{5,6},{6,7},{7,8},{8,9},{9,10... | collective-permute-start | bytes 196616 | tf_op jit(solution)/shard_map/ppermute | solution.py:417
  35.7 15.9 %collective-permute-start.5 = (bf16[8,3072]{1,0:T(8,128)(2,1)S(1)}, bf16[8,3072]{1,0:T(8,128)(2,1)S(1)}, u32[]{:S(2)}, u32[]{:S(2)}) collective-permute-start(bf16[8,3072]{1,0:T(8,128)(2,1)S(1)} %get-tuple-element.40), channel_id=1, source_target_pairs={{255,0},{240,1},{241,2},{242,3},{243,4},{244,5},{245,6},{246,7},{2... | collective-permute-start | bytes 147464 | tf_op jit(solution)/shard_map/ppermute | solution.py:417

commit v5 on v4

--- a/solution.py
+++ b/solution.py
@@ -69,7 +69,7 @@
     return jnp.concatenate([values[:, :WIDE], rest, blank], axis=0)
 
 
-def cut_kernel(f_ref, a_ref, b_ref, c_ref, d_ref):
+def cut_kernel(f_ref, a_ref, c_ref, d_ref, b_ref):
     cells = [f_ref[d].astype(F32) for d in range(WIN)]
     low, high = range(SHIFT), range(SHIFT, WIN)
     a_ref[...] = piece_rows(cells, high, (SHIFT, WIN)).astype(BF)
@@ -78,7 +78,7 @@
     d_ref[...] = packed(piece_rows(cells, low, (0, SHIFT)), 9)
 
 
-def join_kernel(a_ref, b_ref, c_ref, d_ref, out_ref):
+def join_kernel(a_ref, c_ref, d_ref, b_ref, out_ref):
     a = a_ref[...].astype(F32)
     b = unpacked(b_ref, 12)
     c = unpacked(c_ref, 12)
@@ -160,17 +160,11 @@
     return inverse * (scaled - middle - unit * along)
 
 
-def paired(pair, rows, extra, second=None):
-    halves = []
-    for h in range(2):
-        head = 2 * pair + h
-        parts = [rows[HEAD * h : HEAD * h + HEAD], extra if h == 0 or second is None else second, jnp.zeros((16, LANES), BF)]
-        if head < HEADS - 1:
-            parts.insert(1, jnp.zeros((C - HEAD * head - HEAD, LANES), BF))
-        if head:
-            parts.insert(0, jnp.zeros((HEAD * head, LANES), BF))
-        halves.append(jnp.concatenate(parts, axis=0))
-    return jnp.concatenate(halves, axis=1)
+def paired(rows, first, second):
+    blank = jnp.zeros((HEAD, LANES), BF)
+    left = jnp.concatenate([rows[:HEAD], blank, first], axis=0)
+    right = jnp.concatenate([blank, rows[HEAD:], second], axis=0)
+    return jnp.concatenate([left, right], axis=1)
 
 
 def blockdiag(rows):
@@ -180,22 +174,54 @@
     return jnp.concatenate([first, second], axis=0)
 
 
+def by_columns(rows, weights):
+    rows = rows[:, :ROWS]
+    left = nn(rows[:HEAD], weights[:, :256])
+    middle = nn(rows, weights[:, 256:512])
+    right = nn(rows[HEAD:], weights[:, 512:])
+    first = jnp.concatenate([left, middle[:HEAD, :128]], axis=1)
+    second = jnp.concatenate([middle[HEAD:, 128:], right], axis=1)
+    return jnp.concatenate([first, second], axis=0)
+
+
 def across(ref):
-    return jnp.concatenate([ref[w] for w in range(WINDOWS)], axis=1)
-
-
-def split(ref, values):
+    columns = []
     for w in range(WINDOWS):
-        ref[w] = values[:, LANES * w : LANES * w + LANES]
+        columns.append(jnp.concatenate([ref[PAIRS * w + p] for p in range(PAIRS)], axis=0))
+    return jnp.concatenate(columns, axis=1)
+
+
+def each_pair(values):
+    for w in range(WINDOWS):
+        for p in range(PAIRS):
+            yield PAIRS * w + p, values[32 * p : 32 * p + 32, LANES * w : LANES * w + LANES]
+
+
+def in_turn(start, finish, buffers):
+    first, second = buffers
+    last = WINDOWS * PAIRS - 2
+
+    def two(i, carry):
+        start(2 * i + 1, *second)
+        finish(2 * i, *first)
+        start(2 * i + 2, *first)
+        finish(2 * i + 1, *second)
+        return carry
+
+    start(0, *first)
+    lax.fori_loop(0, last // 2, two, 0)
+    start(last + 1, *second)
+    finish(last, *first)
+    finish(last + 1, *second)
 
 
 def main_kernel(
     scale,
-    a_ref, b_ref, c_ref, d_ref, ids_ref, sel_ref, gain1_ref, gain2_ref,
+    a_ref, c_ref, d_ref, b_ref, ids_ref, sel_ref, gain1_ref, gain2_ref,
     qkv_ref, qkvt_ref, proj_ref, projt_ref, up_ref, upt_ref, down_ref, downt_ref, head_ref, headt_ref,
-    oa_ref, ob_ref, oc_ref, od_ref,
-    x_ref, mixed_qkv_ref, keyst_ref, valuest_ref, side_ref, e_ref, ds_ref, attended_ref, inverse_ref,
-    d_hidden_ref, d_mixed_ref, extra_ref, d_qkv_ref, slope_ref,
+    oa_ref, oc_ref, od_ref, ob_ref,
+    x_ref, q_ref, k_ref, v_ref, keyst_ref, valuest_ref, side_ref, e_ref, s0_ref, s1_ref, top0_ref, top1_ref,
+    attended_ref, inverse_ref, d_hidden_ref, d_mixed_ref, extra_ref, dq_ref, dk_ref, dv_ref, slope_ref,
 ):
     sel = sel_ref[...]
     pieces = [a_ref[...].astype(F32), unpacked(b_ref, 12), unpacked(c_ref, 12), unpacked(d_ref, 9)]
@@ -205,58 +231,48 @@
         cols = [(WIN * w + SHIFT + c) % NX for c in range(WIN)]
         wide = jnp.concatenate([tall[C * c : C * c + C] for c in cols], axis=1).astype(BF)
         x_ref[:, LANES * w : LANES * w + LANES] = nn(wide, sel)
-    e_ref[:, :, ROWS:, :] = jnp.zeros((WINDOWS, PAIRS, LANES - ROWS, 2 * LANES), BF)
-    ds_ref[:, ROWS:, :] = jnp.zeros((PAIRS, LANES - ROWS, 2 * LANES), BF)
+    dk_ref[...] = jnp.zeros(dk_ref.shape, BF)
+    dv_ref[...] = jnp.zeros(dv_ref.shape, BF)
 
     gain1 = jnp.concatenate([gain1_ref[...]] * (3 * WINDOWS), axis=1)
     gain2 = jnp.concatenate([gain2_ref[...]] * (3 * WINDOWS), axis=1)
     unit1, inverse1, normed1 = norm(x_ref[...], gain1)
-    for k in range(3):
-        part = nn(qkvt_ref[C * k : C * k + C, :], normed1)
-        part = (part * (0.25 * LOG2E) if k == 0 else part).astype(BF)
-        for w in range(WINDOWS):
-            mixed_qkv_ref[w, C * k : C * k + C, :] = part[:, LANES * w : LANES * w + LANES]
     index = lax.broadcasted_iota(jnp.int32, (16, LANES), 0)
     ones = jnp.where(index < 2, 1.0, 0.0).astype(BF)
-    blank = jnp.zeros((16, LANES), BF)
+    key_sides = []
     for w in range(WINDOWS):
         same = index.astype(F32) == ids_ref[w : w + 1, :]
-        key_side = same.astype(F32).astype(BF)
+        key_sides.append(same.astype(F32).astype(BF))
         side_ref[w] = jnp.where(same | (index > 4), 0.0, FAR).astype(BF)
-        keyst_ref[w] = turned(jnp.concatenate([mixed_qkv_ref[w, C : 2 * C, :], key_side, blank], axis=0))[:ROWS]
-        valuest_ref[w] = turned(jnp.concatenate([mixed_qkv_ref[w, 2 * C :, :], ones, blank], axis=0))[:ROWS]
-
-    units = [(p, j) for p in range(PAIRS) for j in range(3)]
-
-    def forward(w, carry):
-        keys_t = keyst_ref[w]
-        side = side_ref[w]
-        spread = [paired(p, mixed_qkv_ref[w, 32 * p : 32 * p + 32, :], side) for p in range(PAIRS)]
-        scores_of = lambda p, j: nn(keys_t, spread[p][:, 256 * j : 256 * j + 256])
-        following = scores_of(*units[0])
-        mixed = []
-        for u, (p, j) in enumerate(units):
-            scores = following
-            if u + 1 < len(units):
-                following = scores_of(*units[u + 1])
-            top = jnp.max(scores, axis=0, keepdims=True)
-            raised = jnp.exp2(scores - top).astype(BF)
-            e_ref[w, p, :ROWS, 256 * j : 256 * j + 256] = raised
-            values = mixed_qkv_ref[w, 2 * C + 32 * p : 2 * C + 32 * p + 32, :]
-            mixed.append(nn(jnp.concatenate([values, ones], axis=0)[:, :ROWS], raised))
-            if j == 2:
-                whole = jnp.concatenate(mixed, axis=1)
-                mixed = []
-                inverse_sum = 1.0 / whole[32:33]
-                for h in range(2):
-                    inverse_head = inverse_sum[:, LANES * h : LANES * h + LANES]
-                    inverse_ref[w, 2 * p + h : 2 * p + h + 1, :] = inverse_head
-                    own = whole[HEAD * h : HEAD * h + HEAD, LANES * h : LANES * h + LANES]
-                    place = 32 * p + HEAD * h
-                    attended_ref[w, place : place + HEAD, :] = (own * inverse_head).astype(BF)
-        return carry
-
-    lax.fori_loop(0, WINDOWS, forward, 0)
+    for t, part in each_pair((nn(qkvt_ref[:C, :], normed1) * (0.25 * LOG2E)).astype(BF)):
+        q_ref[t] = part
+    for t, part in each_pair(nn(qkvt_ref[C : 2 * C, :], normed1).astype(BF)):
+        k_ref[t] = part
+        keyst_ref[t] = turned(jnp.concatenate([part, key_sides[t // PAIRS]], axis=0))[:ROWS]
+    for t, part in each_pair(nn(qkvt_ref[2 * C :, :], normed1).astype(BF)):
+        v_ref[t] = part
+        valuest_ref[t] = turned(jnp.concatenate([part, ones], axis=0))[:ROWS]
+
+    def score(t, out_ref, top_ref):
+        side = side_ref[lax.div(t, PAIRS)]
+        scores = nn(keyst_ref[t], paired(q_ref[t], side, side))
+        out_ref[...] = scores
+        top_ref[0:1, :] = jnp.max(scores, axis=0, keepdims=True)
+
+    def mix(t, in_ref, top_ref):
+        powers = jnp.exp2(in_ref[...] - top_ref[0:1, :])
+        raised = powers.astype(BF)
+        e_ref[t] = raised
+        inverse_sum = 1.0 / jnp.sum(powers, axis=0, keepdims=True)
+        sums = []
+        for h in range(2):
+            part = inverse_sum[:, LANES * h : LANES * h + LANES]
+            inverse_ref[t, h : h + 1, :] = part
+            sums.append(jnp.broadcast_to(part, (HEAD, LANES)))
+        attended_ref[t] = (by_columns(v_ref[t], raised) * jnp.concatenate(sums, axis=0)).astype(BF)
+
+    buffers = ((s0_ref, top0_ref), (s1_ref, top1_ref))
+    in_turn(score, mix, buffers)
 
     attended = across(attended_ref)
     hidden = x_ref[...] + nn(projt_ref[...], attended)
@@ -289,50 +305,34 @@
     d_attended = nn(proj_ref[...], d_hidden.astype(BF))
     for h in range(HEADS):
         own = slice(HEAD * h, HEAD * h + HEAD)
-        sums = jnp.concatenate([inverse_ref[w, h : h + 1, :] for w in range(WINDOWS)], axis=1)
+        sums = jnp.concatenate(
+            [inverse_ref[PAIRS * w + h // 2, h % 2 : h % 2 + 1, :] for w in range(WINDOWS)], axis=1
+        )
         d_mixed = (d_attended[own] * sums).astype(BF)
         along = -jnp.sum(d_mixed.astype(F32) * attended[own].astype(F32), axis=0, keepdims=True)
         coarse = along.astype(BF).astype(F32)
         rest = along - coarse
+        place = slice(HEAD * (h % 2), HEAD * (h % 2) + HEAD)
         for w in range(WINDOWS):
             lanes = slice(LANES * w, LANES * w + LANES)
-            d_mixed_ref[w, own, :] = d_mixed[:, lanes]
+            d_mixed_ref[PAIRS * w + h // 2, place, :] = d_mixed[:, lanes]
             extra = jnp.where(index == 0, coarse[:, lanes], jnp.where(index == 1, rest[:, lanes], 0.0))
-            extra_ref[w, own, :] = extra.astype(BF)
-
-    def backward(w, carry):
-        values_t = valuest_ref[w]
-        spread = [
-            paired(p, d_mixed_ref[w, 32 * p : 32 * p + 32, :], *[extra_ref[w, 32 * p + HEAD * h : 32 * p + HEAD * h + HEAD, :] for h in range(2)])
-            for p in range(PAIRS)
-        ]
-        weights_of = lambda p, j: nn(values_t, spread[p][:, 256 * j : 256 * j + 256])
-        following = weights_of(*units[0])
-        both = []
-        for u, (p, j) in enumerate(units):
-            own = slice(32 * p, 32 * p + 32)
-            cols = slice(256 * j, 256 * j + 256)
-            d_weights = following
-            if u + 1 < len(units):
-                following = weights_of(*units[u + 1])
-            d_scores = (e_ref[w, p, :ROWS, cols].astype(F32) * d_weights).astype(BF)
-            ds_ref[p, :ROWS, cols] = d_scores
-            keys = mixed_qkv_ref[w, C + 32 * p : C + 32 * p + 32, :]
-            both.append(nn(keys[:, :ROWS], d_scores))
-            if j == 2:
-                whole = jnp.concatenate(both, axis=1) * 0.25
-                both = []
-                d_queries = jnp.concatenate([whole[:HEAD, :LANES], whole[HEAD:, LANES:]], axis=0)
-                d_qkv_ref[w, own, :] = d_queries.astype(BF)
-                d_keys = nt(blockdiag(mixed_qkv_ref[w, own, :]), ds_ref[p]) * LN2
-                d_qkv_ref[w, C + 32 * p : C + 32 * p + 32, :] = d_keys.astype(BF)
-                d_values = nt(blockdiag(d_mixed_ref[w, own, :]), e_ref[w, p])
-                d_qkv_ref[w, 2 * C + 32 * p : 2 * C + 32 * p + 32, :] = d_values.astype(BF)
-        return carry
-
-    lax.fori_loop(0, WINDOWS, backward, 0)
-
-    d_normed1 = nn(qkv_ref[...], across(d_qkv_ref))
+            extra_ref[PAIRS * w + h // 2, place, :] = extra.astype(BF)
+
+    def weigh(t, out_ref, unused):
+        extra = extra_ref[t]
+        out_ref[...] = nn(valuest_ref[t], paired(d_mixed_ref[t], extra[:HEAD], extra[HEAD:]))
+
+    def unmix(t, in_ref, unused):
+        raised = e_ref[t]
+        d_scores = (raised.astype(F32) * in_ref[...]).astype(BF)
+        dv_ref[t, :, :ROWS] = nt(raised, blockdiag(d_mixed_ref[t])).T.astype(BF)
+        dq_ref[t] = (by_columns(k_ref[t], d_scores) * 0.25).astype(BF)
+        dk_ref[t, :, :ROWS] = (nt(d_scores, blockdiag(q_ref[t])).T * LN2).astype(BF)
+
+    in_turn(weigh, unmix, buffers)
+
+    d_normed1 = nn(qkv_ref[...], jnp.concatenate([across(r) for r in (dq_ref, dk_ref, dv_ref)], axis=0))
     unit1, inverse1, normed1 = norm(x_ref[...], gain1)
     grad = (d_hidden_ref[...] + norm_back(d_normed1, unit1, inverse1, gain1)).astype(BF)
     blocks = [None] * NX
@@ -348,7 +348,7 @@
 
 VMEM = pl.BlockSpec(memory_space=pltpu.VMEM)
 SMALL = pltpu.CompilerParams(vmem_limit_bytes=8 * 2**20)
-PIECES = [jax.ShapeDtypeStruct(s, BF) for s in ((16, WIDE), (8, 4096), (8, 4096), (8, 3072))]
+PIECES = [jax.ShapeDtypeStruct(s, BF) for s in ((16, WIDE), (8, 4096), (8, 3072), (8, 4096))]
 
 
 def cut(features):
@@ -382,18 +382,25 @@
         out_specs=[VMEM] * 4,
         scratch_shapes=[
             pltpu.VMEM((C, WINDOWS * LANES), F32),
-            pltpu.VMEM((WINDOWS, 3 * C, LANES), BF),
-            pltpu.VMEM((WINDOWS, ROWS, 128), BF),
-            pltpu.VMEM((WINDOWS, ROWS, 128), BF),
+            pltpu.VMEM((12, 32, LANES), BF),
+            pltpu.VMEM((12, 32, LANES), BF),
+            pltpu.VMEM((12, 32, LANES), BF),
+            pltpu.VMEM((12, ROWS, 48), BF),
+            pltpu.VMEM((12, ROWS, 48), BF),
             pltpu.VMEM((WINDOWS, 16, LANES), BF),
-            pltpu.VMEM((WINDOWS, PAIRS, LANES, 2 * LANES), BF),
-            pltpu.VMEM((PAIRS, LANES, 2 * LANES), BF),
-            pltpu.VMEM((WINDOWS, C, LANES), BF),
-            pltpu.VMEM((WINDOWS, 8, LANES), F32),
+            pltpu.VMEM((12, ROWS, 2 * LANES), BF),
+            pltpu.VMEM((ROWS, 2 * LANES), F32),
+            pltpu.VMEM((ROWS, 2 * LANES), F32),
+            pltpu.VMEM((8, 2 * LANES), F32),
+            pltpu.VMEM((8, 2 * LANES), F32),
+            pltpu.VMEM((12, 32, LANES), BF),
+            pltpu.VMEM((12, 8, LANES), F32),
             pltpu.VMEM((C, WINDOWS * LANES), F32),
-            pltpu.VMEM((WINDOWS, C, LANES), BF),
-            pltpu.VMEM((WINDOWS, C, LANES), BF),
-            pltpu.VMEM((WINDOWS, 3 * C, LANES), BF),
+            pltpu.VMEM((12, 32, LANES), BF),
+            pltpu.VMEM((12, 32, LANES), BF),
+            pltpu.VMEM((12, 32, LANES), BF),
+            pltpu.VMEM((12, 32, LANES), BF),
+            pltpu.VMEM((12, 32, LANES), BF),
             pltpu.VMEM((HID, WINDOWS * LANES), F32),
         ],
         compiler_params=pltpu.CompilerParams(vmem_limit_bytes=32 * 2**20),
@@ -417,7 +424,7 @@
     return lax.ppermute(piece, axes if len(axes) > 1 else axes[0], route)
 
 
-ROADS = (("gz",), ("gy",), ("gz", "gy"))
+ROADS = (("gy",), ("gz", "gy"), ("gz",))
 
 
 def body(

time: 52.6 us -> 47 us (0.89)
  Pallas kernels: 21.5 us -> 17.8 us
  waiting for transfers between devices: 17.8 us -> 15.2 us
  starting transfers between devices: 11.4 us -> 12.2 us
    pallas_call x1, Pallas kernels: 20.2 us -> 16.5 us  [gradient(): pl.pallas_call(functools.partial(main_kernel, scale), out_shape=PIECES, i...]
    ppermute x6, waiting for transfers between devices: 17.8 us -> 15.2 us  [moved(): return lax.ppermute(piece, axes if len(axes) > 1 else axes[0], route)]
    ppermute x6, starting transfers between devices: 11.4 us -> 12.2 us  [moved(): return lax.ppermute(piece, axes if len(axes) > 1 else axes[0], route)]
where the time goes in v5:
time: 47 us; the launch traced here: 46.8 us
  Pallas kernels  17.8 us (38%)
  waiting for transfers between devices  15.2 us (32%)
  starting transfers between devices  12.2 us (26%)
  local copies, waits for them, and re-layouts  1.6 us (3%)
    pallas_call x1, Pallas kernels, gradient(): pl.pallas_call(functools.partial(main_kernel, scale), out_shape=PIECES, i...  16.5 us
    ppermute x6, waiting for transfers between devices, moved(): return lax.ppermute(piece, axes if len(axes) > 1 else axes[0], route)  15.2 us
    ppermute x6, starting transfers between devices, moved(): return lax.ppermute(piece, axes if len(axes) > 1 else axes[0], route)  12.2 us
    unnamed x20, local copies, waits for them, and re-layouts  1.6 us
  transfers between devices with their start and end apart: 6, of which 2 were waited for; matrix products, arithmetic and copies ran while one was open for 0% of the time, Pallas kernels for 1%

profile of v5, /device:TPU:32, one launch (start us, length us, event | category | flops | bytes accessed | tf_op | source)
XLA Modules:
  0.0 46.8 jit_solution(16160701291110051675)
XLA Ops:
  0.0 1.0 %copy-done = bf16[7,7,2688]{2,1,0:T(8,128)(2,1)S(1)} copy-done((bf16[7,7,2688]{2,1,0:T(8,128)(2,1)S(1)}, bf16[7,7,2688]{2,1,0:T(8,128)(2,1)}, u32[]{:S(2)}) %copy-start) | copy-done | bytes 263448
  1.0 0.0 copy-start.5
  1.0 0.0 copy-start.6
  1.0 0.1 shard_map.100
  1.1 7.9 %collective-permute-start = (bf16[8,4096]{1,0:T(8,128)(2,1)S(1)}, bf16[8,4096]{1,0:T(8,128)(2,1)S(1)}, u32[]{:S(2)}, u32[]{:S(2)}) collective-permute-start(bf16[8,4096]{1,0:T(8,128)(2,1)S(1)} %get-tuple-element.24), channel_id=1, source_target_pairs={{1,0},{2,1},{3,2},{4,3},{5,4},{6,5},{7,6},{8,7},{9,8},{10,9},{11,1... | collective-permute-start | bytes 196616 | tf_op jit(solution)/shard_map/ppermute | solution.py:424
  9.1 2.4 %collective-permute-start.2 = (bf16[8,4096]{1,0:T(8,128)(2,1)S(1)}, bf16[8,4096]{1,0:T(8,128)(2,1)S(1)}, u32[]{:S(2)}, u32[]{:S(2)}) collective-permute-start(bf16[8,4096]{1,0:T(8,128)(2,1)S(1)} %get-tuple-element.26), channel_id=1, source_target_pairs={{16,0},{32,16},{48,32},{64,48},{80,64},{96,80},{112,96},{128,112},... | collective-permute-start | bytes 196616 | tf_op jit(solution)/shard_map/ppermute | solution.py:424
  11.4 1.1 %collective-permute-start.1 = (bf16[8,3072]{1,0:T(8,128)(2,1)S(1)}, bf16[8,3072]{1,0:T(8,128)(2,1)S(1)}, u32[]{:S(2)}, u32[]{:S(2)}) collective-permute-start(bf16[8,3072]{1,0:T(8,128)(2,1)S(1)} %get-tuple-element.25), channel_id=1, source_target_pairs={{17,0},{18,1},{19,2},{20,3},{21,4},{22,5},{23,6},{24,7},{25,8},{26... | collective-permute-start | bytes 147464 | tf_op jit(solution)/shard_map/ppermute | solution.py:424
  12.6 0.0 copy-done.1
  12.6 0.0 copy-done.2
  12.6 0.0 copy-done.3
  12.6 0.6 %copy-done.8 = f32[96]{0:T(128)S(1)} copy-done((f32[96]{0:T(128)S(1)}, f32[96]{0:T(128)}, u32[]{:S(2)}) %copy-start.8) | copy-done | bytes 408
  13.2 0.0 copy-done.9
  13.2 0.4 shard_map.101
  13.6 1.4 %collective-permute-done.1.d_ref = bf16[8,3072]{1,0:T(8,128)(2,1)S(1)} collective-permute-done((bf16[8,3072]{1,0:T(8,128)(2,1)S(1)}, bf16[8,3072]{1,0:T(8,128)(2,1)S(1)}, u32[]{:S(2)}, u32[]{:S(2)}) %collective-permute-start.1) | collective-permute-done | bytes 49184 | tf_op jit(solution)/shard_map/ppermute | solution.py:424
  14.9 0.0 collective-permute-done.c_ref
  14.9 0.0 collective-permute-done.2.b_ref
  14.9 16.5 %shard_map.102 = (bf16[16,2688]{1,0:T(8,128)(2,1)S(1)}, bf16[8,4096]{1,0:T(8,128)(2,1)S(1)}, bf16[8,3072]{1,0:T(8,128)(2,1)S(1)}, bf16[8,4096]{1,0:T(8,128)(2,1)S(1)}) custom-call(bf16[16,2688]{1,0:T(8,128)(2,1)S(1)} %get-tuple-element.23.a_ref, bf16[8,4096]{1,0:T(8,128)(2,1)S(1)} %collective-permute-done.c_ref, ...), custom_call_target="tpu_custom_call" | custom-call | tf_op jit(solution)/shard_map/pallas_call | solution.py:378
  31.4 0.7 %collective-permute-start.3 = (bf16[8,4096]{1,0:T(8,128)(2,1)S(1)}, bf16[8,4096]{1,0:T(8,128)(2,1)S(1)}, u32[]{:S(2)}, u32[]{:S(2)}) collective-permute-start(bf16[8,4096]{1,0:T(8,128)(2,1)S(1)} %get-tuple-element.38), channel_id=1, source_target_pairs={{15,0},{0,1},{1,2},{2,3},{3,4},{4,5},{5,6},{6,7},{7,8},{8,9},{9,10... | collective-permute-start | bytes 196616 | tf_op jit(solution)/shard_map/ppermute | solution.py:424
  32.2 0.0 collective-permute-start.5
  32.2 0.0 collective-permute-start.4
  32.2 13.8 %collective-permute-done.4.d_ref = bf16[8,3072]{1,0:T(8,128)(2,1)S(1)} collective-permute-done((bf16[8,3072]{1,0:T(8,128)(2,1)S(1)}, bf16[8,3072]{1,0:T(8,128)(2,1)S(1)}, u32[]{:S(2)}, u32[]{:S(2)}) %collective-permute-start.4) | collective-permute-done | bytes 49184 | tf_op jit(solution)/shard_map/ppermute | solution.py:424
  46.0 0.0 collective-permute-done.3.c_ref
  46.0 0.0 collective-permute-done.5.b_ref
  46.0 0.8 %shard_map.103 = bf16[7,7,2688]{2,1,0:T(8,128)(2,1)} custom-call(bf16[16,2688]{1,0:T(8,128)(2,1)S(1)} %get-tuple-element.37.a_ref, bf16[8,4096]{1,0:T(8,128)(2,1)S(1)} %collective-permute-done.3.c_ref, bf16[8,3072]{1,0:T(8,128)(2,1)S(1)} %collective-permute-done.4.d_ref, bf16[8,4096]{1,0:T(8,128)(2,1)S(1)} %collective-permute-done.5.b_ref), custom_call_target="tpu_custom_call" | custom-call | tf_op jit(solution)/shard_map/pallas_call | solution.py:360
  (12 shorter events, 0.0 us)
Async XLA Ops:
  0.0 1.0 %copy-start = (bf16[7,7,2688]{2,1,0:T(8,128)(2,1)S(1)}, bf16[7,7,2688]{2,1,0:T(8,128)(2,1)}, u32[]{:S(2)}) copy-start(bf16[7,7,2688]{2,1,0:T(8,128)(2,1)} %f_ref.1) | copy-start | bytes 790276
  1.0 11.6 %copy-start.1 = (bf16[96,288]{1,0:T(8,128)(2,1)S(1)}, bf16[96,288]{1,0:T(8,128)(2,1)}, u32[]{:S(2)}) copy-start(bf16[96,288]{1,0:T(8,128)(2,1)} %qkv_ref.3) | copy-start | bytes 165892
  1.0 11.6 %copy-start.2 = (bf16[96,384]{1,0:T(8,128)(2,1)S(1)}, bf16[96,384]{1,0:T(8,128)(2,1)}, u32[]{:S(2)}) copy-start(bf16[96,384]{1,0:T(8,128)(2,1)} %up_ref.3) | copy-start | bytes 221188
  1.0 11.6 %copy-start.3 = (bf16[384,96]{0,1:T(8,128)(2,1)S(1)}, bf16[384,96]{0,1:T(8,128)(2,1)}, u32[]{:S(2)}) copy-start(bf16[384,96]{0,1:T(8,128)(2,1)} %param.18) | copy-start | bytes 221188
  1.0 11.6 %copy-start.4 = (bf16[96,96]{1,0:T(8,128)(2,1)S(1)}, bf16[96,96]{1,0:T(8,128)(2,1)}, u32[]{:S(2)}) copy-start(bf16[96,96]{1,0:T(8,128)(2,1)} %proj_ref.3) | copy-start | bytes 55300
  1.0 11.6 %copy-start.5 = (s32[7,7,28]{2,1,0:T(8,128)S(1)}, s32[7,7,28]{2,1,0:T(8,128)}, u32[]{:S(2)}) copy-start(s32[7,7,28]{2,1,0:T(8,128)} %region_ref.1) | copy-start | bytes 16468
  1.0 11.6 %copy-start.6 = (s32[7,7,28]{2,1,0:T(8,128)S(1)}, s32[7,7,28]{2,1,0:T(8,128)}, u32[]{:S(2)}) copy-start(s32[7,7,28]{2,1,0:T(8,128)} %labels_ref.1) | copy-start | bytes 16468
  1.1 13.8 %collective-permute-start = (bf16[8,4096]{1,0:T(8,128)(2,1)S(1)}, bf16[8,4096]{1,0:T(8,128)(2,1)S(1)}, u32[]{:S(2)}, u32[]{:S(2)}) collective-permute-start(bf16[8,4096]{1,0:T(8,128)(2,1)S(1)} %get-tuple-element.24), channel_id=1, source_target_pairs={{1,0},{2,1},{3,2},{4,3},{5,4},{6,5},{7,6},{8,7},{9,8},{10,9},{11,1... | collective-permute-start | bytes 196616 | tf_op jit(solution)/shard_map/ppermute | solution.py:424
  9.1 5.9 %collective-permute-start.2 = (bf16[8,4096]{1,0:T(8,128)(2,1)S(1)}, bf16[8,4096]{1,0:T(8,128)(2,1)S(1)}, u32[]{:S(2)}, u32[]{:S(2)}) collective-permute-start(bf16[8,4096]{1,0:T(8,128)(2,1)S(1)} %get-tuple-element.26), channel_id=1, source_target_pairs={{16,0},{32,16},{48,32},{64,48},{80,64},{96,80},{112,96},{128,112},... | collective-permute-start | bytes 196616 | tf_op jit(solution)/shard_map/ppermute | solution.py:424
  11.4 1.2 %copy-start.7 = (bf16[96,14]{0,1:T(8,128)(2,1)S(1)}, bf16[96,14]{0,1:T(8,128)(2,1)}, u32[]{:S(2)}) copy-start(bf16[96,14]{0,1:T(8,128)(2,1)} %param.19) | copy-start | bytes 8068
  11.4 3.5 %collective-permute-start.1 = (bf16[8,3072]{1,0:T(8,128)(2,1)S(1)}, bf16[8,3072]{1,0:T(8,128)(2,1)S(1)}, u32[]{:S(2)}, u32[]{:S(2)}) collective-permute-start(bf16[8,3072]{1,0:T(8,128)(2,1)S(1)} %get-tuple-element.25), channel_id=1, source_target_pairs={{17,0},{18,1},{19,2},{20,3},{21,4},{22,5},{23,6},{24,7},{25,8},{26... | collective-permute-start | bytes 147464 | tf_op jit(solution)/shard_map/ppermute | solution.py:424
  12.6 0.7 %copy-start.8 = (f32[96]{0:T(128)S(1)}, f32[96]{0:T(128)}, u32[]{:S(2)}) copy-start(f32[96]{0:T(128)} %param.13) | copy-start | bytes 1156
  12.6 0.7 %copy-start.9 = (f32[96]{0:T(128)S(1)}, f32[96]{0:T(128)}, u32[]{:S(2)}) copy-start(f32[96]{0:T(128)} %param.16) | copy-start | bytes 1156
  31.4 14.5 %collective-permute-start.3 = (bf16[8,4096]{1,0:T(8,128)(2,1)S(1)}, bf16[8,4096]{1,0:T(8,128)(2,1)S(1)}, u32[]{:S(2)}, u32[]{:S(2)}) collective-permute-start(bf16[8,4096]{1,0:T(8,128)(2,1)S(1)} %get-tuple-element.38), channel_id=1, source_target_pairs={{15,0},{0,1},{1,2},{2,3},{3,4},{4,5},{5,6},{6,7},{7,8},{8,9},{9,10... | collective-permute-start | bytes 196616 | tf_op jit(solution)/shard_map/ppermute | solution.py:424
  32.2 13.8 %collective-permute-start.5 = (bf16[8,4096]{1,0:T(8,128)(2,1)S(1)}, bf16[8,4096]{1,0:T(8,128)(2,1)S(1)}, u32[]{:S(2)}, u32[]{:S(2)}) collective-permute-start(bf16[8,4096]{1,0:T(8,128)(2,1)S(1)} %get-tuple-element.40), channel_id=1, source_target_pairs={{240,0},{0,16},{16,32},{32,48},{48,64},{64,80},{80,96},{96,112},{1... | collective-permute-start | bytes 196616 | tf_op jit(solution)/shard_map/ppermute | solution.py:424
  32.2 13.8 %collective-permute-start.4 = (bf16[8,3072]{1,0:T(8,128)(2,1)S(1)}, bf16[8,3072]{1,0:T(8,128)(2,1)S(1)}, u32[]{:S(2)}, u32[]{:S(2)}) collective-permute-start(bf16[8,3072]{1,0:T(8,128)(2,1)S(1)} %get-tuple-element.39), channel_id=1, source_target_pairs={{255,0},{240,1},{241,2},{242,3},{243,4},{244,5},{245,6},{246,7},{2... | collective-permute-start | bytes 147464 | tf_op jit(solution)/shard_map/ppermute | solution.py:424

commit v6 on v5

--- a/solution.py
+++ b/solution.py
@@ -58,6 +58,15 @@
     return jnp.concatenate([rows[:8], tail], axis=1).astype(BF)
 
 
+def halved(values, first, second):
+    first[...] = values[:, :2048]
+    second[...] = values[:, 2048:]
+
+
+def whole_of(first, second):
+    return jnp.concatenate([first[...], second[...]], axis=1)
+
+
 def unpacked(ref, count):
     values = ref[...].astype(F32)
     tail = values[:, WIDE:]
@@ -69,18 +78,18 @@
     return jnp.concatenate([values[:, :WIDE], rest, blank], axis=0)
 
 
-def cut_kernel(f_ref, a_ref, c_ref, d_ref, b_ref):
+def cut_kernel(f_ref, a_ref, c_ref, d_ref, b_ref, b2_ref):
     cells = [f_ref[d].astype(F32) for d in range(WIN)]
     low, high = range(SHIFT), range(SHIFT, WIN)
     a_ref[...] = piece_rows(cells, high, (SHIFT, WIN)).astype(BF)
-    b_ref[...] = packed(piece_rows(cells, low, (SHIFT, WIN)), 12)
+    halved(packed(piece_rows(cells, low, (SHIFT, WIN)), 12), b_ref, b2_ref)
     c_ref[...] = packed(piece_rows(cells, high, (0, SHIFT)), 12)
     d_ref[...] = packed(piece_rows(cells, low, (0, SHIFT)), 9)
 
 
-def join_kernel(a_ref, c_ref, d_ref, b_ref, out_ref):
+def join_kernel(a_ref, c_ref, d_ref, b_ref, b2_ref, out_ref):
     a = a_ref[...].astype(F32)
-    b = unpacked(b_ref, 12)
+    b = unpacked(whole_of(b_ref, b2_ref), 12)
     c = unpacked(c_ref, 12)
     d = unpacked(d_ref, 9)
     for i in range(WIN):
@@ -209,7 +218,7 @@
         return carry
 
     start(0, *first)
-    lax.fori_loop(0, last // 2, two, 0)
+    lax.fori_loop(0, last // 2, two, 0, unroll=5)
     start(last + 1, *second)
     finish(last, *first)
     finish(last + 1, *second)
@@ -217,26 +226,31 @@
 
 def main_kernel(
     scale,
-    a_ref, c_ref, d_ref, b_ref, ids_ref, sel_ref, gain1_ref, gain2_ref,
+    a_ref, c_ref, d_ref, b_ref, b2_ref, ids_ref, sel_ref, gain1_ref, gain2_ref,
     qkv_ref, qkvt_ref, proj_ref, projt_ref, up_ref, upt_ref, down_ref, downt_ref, head_ref, headt_ref,
-    oa_ref, oc_ref, od_ref, ob_ref,
-    x_ref, q_ref, k_ref, v_ref, keyst_ref, valuest_ref, side_ref, e_ref, s0_ref, s1_ref, top0_ref, top1_ref,
+    oa_ref, oc_ref, od_ref, ob_ref, ob2_ref,
+    x_ref, unit1_ref, inverse1_ref, q_ref, k_ref, v_ref, keyst_ref, valuest_ref, side_ref, e_ref, s0_ref, s1_ref, top0_ref, top1_ref,
     attended_ref, inverse_ref, d_hidden_ref, d_mixed_ref, extra_ref, dq_ref, dk_ref, dv_ref, slope_ref,
 ):
     sel = sel_ref[...]
-    pieces = [a_ref[...].astype(F32), unpacked(b_ref, 12), unpacked(c_ref, 12), unpacked(d_ref, 9)]
+    pieces = [a_ref[...].astype(F32), unpacked(whole_of(b_ref, b2_ref), 12), unpacked(c_ref, 12), unpacked(d_ref, 9)]
     rows = jnp.concatenate(pieces, axis=0)
     tall = rows.T
+    wides = []
     for w in range(WINDOWS):
         cols = [(WIN * w + SHIFT + c) % NX for c in range(WIN)]
-        wide = jnp.concatenate([tall[C * c : C * c + C] for c in cols], axis=1).astype(BF)
-        x_ref[:, LANES * w : LANES * w + LANES] = nn(wide, sel)
+        wides.append(jnp.concatenate([tall[C * c : C * c + C] for c in cols], axis=1).astype(BF))
+    stacked = nn(jnp.concatenate(wides, axis=0), sel)
+    x = jnp.concatenate([stacked[C * w : C * w + C] for w in range(WINDOWS)], axis=1)
+    x_ref[...] = x
     dk_ref[...] = jnp.zeros(dk_ref.shape, BF)
     dv_ref[...] = jnp.zeros(dv_ref.shape, BF)
 
     gain1 = jnp.concatenate([gain1_ref[...]] * (3 * WINDOWS), axis=1)
     gain2 = jnp.concatenate([gain2_ref[...]] * (3 * WINDOWS), axis=1)
-    unit1, inverse1, normed1 = norm(x_ref[...], gain1)
+    unit1, inverse1, normed1 = norm(x, gain1)
+    unit1_ref[...] = unit1
+    inverse1_ref[0:1, :] = inverse1
     index = lax.broadcasted_iota(jnp.int32, (16, LANES), 0)
     ones = jnp.where(index < 2, 1.0, 0.0).astype(BF)
     key_sides = []
@@ -281,9 +295,10 @@
     for j in range(3):
         part = slice(128 * j, 128 * j + 128)
         raised = nn(upt_ref[part, :], normed2)
-        below = 0.5 + 0.5 * lax.erf(raised * (0.5**0.5))
-        bell = jnp.exp(-0.5 * raised * raised) * 0.3989422804014327
-        slope_ref[part, :] = below + raised * bell
+        inner = raised * (0.5**0.5)
+        below = 0.5 + 0.5 * lax.erf(inner)
+        bell = jnp.exp2(inner * inner * -LOG2E)
+        slope_ref[part, :] = below + (raised * 0.3989422804014327) * bell
         output = output + nn(downt_ref[:, part], (raised * below).astype(BF))
     logits = nn(headt_ref[...], output.astype(BF))
     labels = jnp.concatenate([ids_ref[WINDOWS + w : WINDOWS + w + 1, :] for w in range(WINDOWS)], axis=1)
@@ -326,38 +341,40 @@
     def unmix(t, in_ref, unused):
         raised = e_ref[t]
         d_scores = (raised.astype(F32) * in_ref[...]).astype(BF)
-        dv_ref[t, :, :ROWS] = nt(raised, blockdiag(d_mixed_ref[t])).T.astype(BF)
+        dv_ref[t, :, :ROWS] = nt(blockdiag(d_mixed_ref[t]), raised).astype(BF)
         dq_ref[t] = (by_columns(k_ref[t], d_scores) * 0.25).astype(BF)
         dk_ref[t, :, :ROWS] = (nt(d_scores, blockdiag(q_ref[t])).T * LN2).astype(BF)
 
     in_turn(weigh, unmix, buffers)
 
     d_normed1 = nn(qkv_ref[...], jnp.concatenate([across(r) for r in (dq_ref, dk_ref, dv_ref)], axis=0))
-    unit1, inverse1, normed1 = norm(x_ref[...], gain1)
+    unit1, inverse1 = unit1_ref[...], inverse1_ref[0:1, :]
     grad = (d_hidden_ref[...] + norm_back(d_normed1, unit1, inverse1, gain1)).astype(BF)
     blocks = [None] * NX
+    stacked = nt(jnp.concatenate([grad[:, LANES * w : LANES * w + LANES] for w in range(WINDOWS)], axis=0), sel)
     for w in range(WINDOWS):
-        wide = nt(grad[:, LANES * w : LANES * w + LANES], sel)
+        wide = stacked[C * w : C * w + C]
         for c in range(WIN):
             blocks[(WIN * w + SHIFT + c) % NX] = wide[:, SLOTS * c : SLOTS * c + SLOTS]
     rows = jnp.concatenate(blocks, axis=0).T
     oa_ref[...] = rows[:16].astype(BF)
-    for k, (ref, count) in enumerate(((ob_ref, 12), (oc_ref, 12), (od_ref, 9))):
-        ref[...] = packed(rows[16 * k + 16 : 16 * k + 32], count)
+    halved(packed(rows[16:32], 12), ob_ref, ob2_ref)
+    oc_ref[...] = packed(rows[32:48], 12)
+    od_ref[...] = packed(rows[48:], 9)
 
 
 VMEM = pl.BlockSpec(memory_space=pltpu.VMEM)
 SMALL = pltpu.CompilerParams(vmem_limit_bytes=8 * 2**20)
-PIECES = [jax.ShapeDtypeStruct(s, BF) for s in ((16, WIDE), (8, 4096), (8, 3072), (8, 4096))]
+PIECES = [jax.ShapeDtypeStruct(s, BF) for s in ((16, WIDE), (8, 4096), (8, 3072), (8, 2048), (8, 2048))]
 
 
 def cut(features):
-    return pl.pallas_call(cut_kernel, out_shape=PIECES, in_specs=[VMEM], out_specs=[VMEM] * 4, compiler_params=SMALL)(features)
+    return pl.pallas_call(cut_kernel, out_shape=PIECES, in_specs=[VMEM], out_specs=[VMEM] * 5, compiler_params=SMALL)(features)
 
 
 def join(*pieces):
     out = jax.ShapeDtypeStruct((WIN, WIN, WIDE), BF)
-    return pl.pallas_call(join_kernel, out_shape=out, in_specs=[VMEM] * 4, out_specs=VMEM, compiler_params=SMALL)(*pieces)
+    return pl.pallas_call(join_kernel, out_shape=out, in_specs=[VMEM] * 5, out_specs=VMEM, compiler_params=SMALL)(*pieces)
 
 
 def ready(region, labels, attn_gain, mlp_gain, qkv_weight, proj_weight, up_weight, down_weight, head_weight):
@@ -378,10 +395,12 @@
     return pl.pallas_call(
         functools.partial(main_kernel, scale),
         out_shape=PIECES,
-        in_specs=[VMEM] * 18,
-        out_specs=[VMEM] * 4,
+        in_specs=[VMEM] * 19,
+        out_specs=[VMEM] * 5,
         scratch_shapes=[
             pltpu.VMEM((C, WINDOWS * LANES), F32),
+            pltpu.VMEM((C, WINDOWS * LANES), F32),
+            pltpu.VMEM((8, WINDOWS * LANES), F32),
             pltpu.VMEM((12, 32, LANES), BF),
             pltpu.VMEM((12, 32, LANES), BF),
             pltpu.VMEM((12, 32, LANES), BF),
@@ -424,7 +443,7 @@
     return lax.ppermute(piece, axes if len(axes) > 1 else axes[0], route)
 
 
-ROADS = (("gy",), ("gz", "gy"), ("gz",))
+ROADS = (("gy",), ("gz", "gy"), ("gz",), ("gz",))
 
 
 def body(

time: 47 us -> 45.5 us (0.968)
  waiting for transfers between devices: 15.2 us -> 12.8 us
  starting transfers between devices: 12.2 us -> 13.8 us
  Pallas kernels: 17.8 us -> 16.9 us
    ppermute x6 -> x8, waiting for transfers between devices: 15.2 us -> 12.8 us  [moved(): return lax.ppermute(piece, axes if len(axes) > 1 else axes[0], route)]
    ppermute x6 -> x8, starting transfers between devices: 12.2 us -> 13.8 us  [moved(): return lax.ppermute(piece, axes if len(axes) > 1 else axes[0], route)]
    pallas_call x1, Pallas kernels: 16.5 us -> 15.6 us  [gradient(): pl.pallas_call(functools.partial(main_kernel, scale), out_shape=PIECES, i...]
  transfers between devices with their start and end apart: 6 -> 8, of which waited for: 2 -> 5; matrix products, arithmetic and copies ran while one was open for 0% -> 0% of each run, Pallas kernels for 1% -> 1%
where the time goes in v6:
time: 45.5 us; the launch traced here: 45.2 us
  Pallas kernels  16.9 us (37%)
  starting transfers between devices  13.8 us (30%)
  waiting for transfers between devices  12.8 us (28%)
  local copies, waits for them, and re-layouts  1.61 us (4%)
    pallas_call x1, Pallas kernels, gradient(): pl.pallas_call(functools.partial(main_kernel, scale), out_shape=PIECES, i...  15.6 us
    ppermute x8, starting transfers between devices, moved(): return lax.ppermute(piece, axes if len(axes) > 1 else axes[0], route)  13.8 us
    ppermute x8, waiting for transfers between devices, moved(): return lax.ppermute(piece, axes if len(axes) > 1 else axes[0], route)  12.8 us
    unnamed x20, local copies, waits for them, and re-layouts  1.61 us
  transfers between devices with their start and end apart: 8, of which 5 were waited for; matrix products, arithmetic and copies ran while one was open for 0% of the time, Pallas kernels for 1%

profile of v6, /device:TPU:32, one launch (start us, length us, event | category | flops | bytes accessed | tf_op | source)
XLA Modules:
  0.0 45.2 jit_solution(4906584919536201982)
XLA Ops:
  0.0 1.0 %copy-done = bf16[7,7,2688]{2,1,0:T(8,128)(2,1)S(1)} copy-done((bf16[7,7,2688]{2,1,0:T(8,128)(2,1)S(1)}, bf16[7,7,2688]{2,1,0:T(8,128)(2,1)}, u32[]{:S(2)}) %copy-start) | copy-done | bytes 263448
  1.0 0.0 copy-start.5
  1.0 0.1 shard_map.100
  1.1 7.9 %collective-permute-start = (bf16[8,4096]{1,0:T(8,128)(2,1)S(1)}, bf16[8,4096]{1,0:T(8,128)(2,1)S(1)}, u32[]{:S(2)}, u32[]{:S(2)}) collective-permute-start(bf16[8,4096]{1,0:T(8,128)(2,1)S(1)} %get-tuple-element.26), channel_id=1, source_target_pairs={{1,0},{2,1},{3,2},{4,3},{5,4},{6,5},{7,6},{8,7},{9,8},{10,9},{11,1... | collective-permute-start | bytes 196616 | tf_op jit(solution)/shard_map/ppermute | solution.py:443
  9.1 2.5 %collective-permute-start.1 = (bf16[8,3072]{1,0:T(8,128)(2,1)S(1)}, bf16[8,3072]{1,0:T(8,128)(2,1)S(1)}, u32[]{:S(2)}, u32[]{:S(2)}) collective-permute-start(bf16[8,3072]{1,0:T(8,128)(2,1)S(1)} %get-tuple-element.27), channel_id=1, source_target_pairs={{17,0},{18,1},{19,2},{20,3},{21,4},{22,5},{23,6},{24,7},{25,8},{26... | collective-permute-start | bytes 147464 | tf_op jit(solution)/shard_map/ppermute | solution.py:443
  11.6 1.1 %collective-permute-start.2 = (bf16[8,2048]{1,0:T(8,128)(2,1)S(1)}, bf16[8,2048]{1,0:T(8,128)(2,1)S(1)}, u32[]{:S(2)}, u32[]{:S(2)}) collective-permute-start(bf16[8,2048]{1,0:T(8,128)(2,1)S(1)} %get-tuple-element.28), channel_id=1, source_target_pairs={{16,0},{32,16},{48,32},{64,48},{80,64},{96,80},{112,96},{128,112},... | collective-permute-start | bytes 98312 | tf_op jit(solution)/shard_map/ppermute | solution.py:443
  12.7 0.0 collective-permute-start.3
  12.8 0.6 %copy-done.7 = bf16[96,14]{0,1:T(8,128)(2,1)S(1)} copy-done((bf16[96,14]{0,1:T(8,128)(2,1)S(1)}, bf16[96,14]{0,1:T(8,128)(2,1)}, u32[]{:S(2)}) %copy-start.7) | copy-done | bytes 2712
  13.4 0.0 copy-done.9
  13.4 0.4 shard_map.101
  13.8 0.5 %collective-permute-done.2.b_ref = bf16[8,2048]{1,0:T(8,128)(2,1)S(1)} collective-permute-done((bf16[8,2048]{1,0:T(8,128)(2,1)S(1)}, bf16[8,2048]{1,0:T(8,128)(2,1)S(1)}, u32[]{:S(2)}, u32[]{:S(2)}) %collective-permute-start.2) | collective-permute-done | bytes 32800 | tf_op jit(solution)/shard_map/ppermute | solution.py:443
  14.3 0.3 collective-permute-done.3.b2_ref
  14.6 0.0 collective-permute-done.1.d_ref
  14.6 0.0 collective-permute-done.c_ref
  14.6 15.6 %shard_map.102 = (bf16[16,2688]{1,0:T(8,128)(2,1)S(1)}, bf16[8,4096]{1,0:T(8,128)(2,1)S(1)}, bf16[8,3072]{1,0:T(8,128)(2,1)S(1)}, bf16[8,2048]{1,0:T(8,128)(2,1)S(1)}, bf16[8,2048]{1,0:T(8,128)(2,1)S(1)}) custom-call(bf16[16,2688]{1,0:T(8,128)(2,1)S(1)} %get-tuple-element.25.a_ref, bf16[8,4096]{1,0:T(8,128)(2,1)S(1)} %collective-permute-done.c_ref, ...), custom_call_target="tpu_custom_call" | custom-call | tf_op jit(solution)/shard_map/pallas_call | solution.py:395
  30.3 1.4 %collective-permute-start.4 = (bf16[8,4096]{1,0:T(8,128)(2,1)S(1)}, bf16[8,4096]{1,0:T(8,128)(2,1)S(1)}, u32[]{:S(2)}, u32[]{:S(2)}) collective-permute-start(bf16[8,4096]{1,0:T(8,128)(2,1)S(1)} %get-tuple-element.41), channel_id=1, source_target_pairs={{15,0},{0,1},{1,2},{2,3},{3,4},{4,5},{5,6},{6,7},{7,8},{8,9},{9,10... | collective-permute-start | bytes 196616 | tf_op jit(solution)/shard_map/ppermute | solution.py:443
  31.6 0.5 %collective-permute-start.5 = (bf16[8,3072]{1,0:T(8,128)(2,1)S(1)}, bf16[8,3072]{1,0:T(8,128)(2,1)S(1)}, u32[]{:S(2)}, u32[]{:S(2)}) collective-permute-start(bf16[8,3072]{1,0:T(8,128)(2,1)S(1)} %get-tuple-element.42), channel_id=1, source_target_pairs={{255,0},{240,1},{241,2},{242,3},{243,4},{244,5},{245,6},{246,7},{2... | collective-permute-start | bytes 147464 | tf_op jit(solution)/shard_map/ppermute | solution.py:443
  32.1 0.0 collective-permute-start.6
  32.2 0.3 collective-permute-start.7
  32.4 5.1 %collective-permute-done.6.b_ref = bf16[8,2048]{1,0:T(8,128)(2,1)S(1)} collective-permute-done((bf16[8,2048]{1,0:T(8,128)(2,1)S(1)}, bf16[8,2048]{1,0:T(8,128)(2,1)S(1)}, u32[]{:S(2)}, u32[]{:S(2)}) %collective-permute-start.6) | collective-permute-done | bytes 32800 | tf_op jit(solution)/shard_map/ppermute | solution.py:443
  37.6 0.4 collective-permute-done.7.b2_ref
  37.9 6.4 %collective-permute-done.5.d_ref = bf16[8,3072]{1,0:T(8,128)(2,1)S(1)} collective-permute-done((bf16[8,3072]{1,0:T(8,128)(2,1)S(1)}, bf16[8,3072]{1,0:T(8,128)(2,1)S(1)}, u32[]{:S(2)}, u32[]{:S(2)}) %collective-permute-start.5) | collective-permute-done | bytes 49184 | tf_op jit(solution)/shard_map/ppermute | solution.py:443
  44.4 0.0 collective-permute-done.4.c_ref
  44.4 0.8 %shard_map.103 = bf16[7,7,2688]{2,1,0:T(8,128)(2,1)} custom-call(bf16[16,2688]{1,0:T(8,128)(2,1)S(1)} %get-tuple-element.40.a_ref, bf16[8,4096]{1,0:T(8,128)(2,1)S(1)} %collective-permute-done.4.c_ref, bf16[8,3072]{1,0:T(8,128)(2,1)S(1)} %collective-permute-done.5.d_ref, bf16[8,2048]{1,0:T(8,128)(2,1)S(1)} %collective-permute-done.6.b_ref, ...), custom_call_target="tpu_custom_call" | custom-call | tf_op jit(solution)/shard_map/pallas_call | solution.py:377
  (16 shorter events, 0.0 us)
Async XLA Ops:
  0.0 1.0 %copy-start = (bf16[7,7,2688]{2,1,0:T(8,128)(2,1)S(1)}, bf16[7,7,2688]{2,1,0:T(8,128)(2,1)}, u32[]{:S(2)}) copy-start(bf16[7,7,2688]{2,1,0:T(8,128)(2,1)} %f_ref.1) | copy-start | bytes 790276
  1.0 11.8 %copy-start.1 = (bf16[96,288]{1,0:T(8,128)(2,1)S(1)}, bf16[96,288]{1,0:T(8,128)(2,1)}, u32[]{:S(2)}) copy-start(bf16[96,288]{1,0:T(8,128)(2,1)} %qkv_ref.3) | copy-start | bytes 165892
  1.0 11.8 %copy-start.2 = (bf16[96,384]{1,0:T(8,128)(2,1)S(1)}, bf16[96,384]{1,0:T(8,128)(2,1)}, u32[]{:S(2)}) copy-start(bf16[96,384]{1,0:T(8,128)(2,1)} %up_ref.3) | copy-start | bytes 221188
  1.0 11.8 %copy-start.3 = (bf16[384,96]{0,1:T(8,128)(2,1)S(1)}, bf16[384,96]{0,1:T(8,128)(2,1)}, u32[]{:S(2)}) copy-start(bf16[384,96]{0,1:T(8,128)(2,1)} %param.18) | copy-start | bytes 221188
  1.0 11.8 %copy-start.4 = (bf16[96,96]{1,0:T(8,128)(2,1)S(1)}, bf16[96,96]{1,0:T(8,128)(2,1)}, u32[]{:S(2)}) copy-start(bf16[96,96]{1,0:T(8,128)(2,1)} %proj_ref.3) | copy-start | bytes 55300
  1.0 11.8 %copy-start.5 = (s32[7,7,28]{2,1,0:T(8,128)S(1)}, s32[7,7,28]{2,1,0:T(8,128)}, u32[]{:S(2)}) copy-start(s32[7,7,28]{2,1,0:T(8,128)} %region_ref.1) | copy-start | bytes 16468
  1.0 11.8 %copy-start.6 = (s32[7,7,28]{2,1,0:T(8,128)S(1)}, s32[7,7,28]{2,1,0:T(8,128)}, u32[]{:S(2)}) copy-start(s32[7,7,28]{2,1,0:T(8,128)} %labels_ref.1) | copy-start | bytes 16468
  1.1 13.5 %collective-permute-start = (bf16[8,4096]{1,0:T(8,128)(2,1)S(1)}, bf16[8,4096]{1,0:T(8,128)(2,1)S(1)}, u32[]{:S(2)}, u32[]{:S(2)}) collective-permute-start(bf16[8,4096]{1,0:T(8,128)(2,1)S(1)} %get-tuple-element.26), channel_id=1, source_target_pairs={{1,0},{2,1},{3,2},{4,3},{5,4},{6,5},{7,6},{8,7},{9,8},{10,9},{11,1... | collective-permute-start | bytes 196616 | tf_op jit(solution)/shard_map/ppermute | solution.py:443
  9.1 5.6 %collective-permute-start.1 = (bf16[8,3072]{1,0:T(8,128)(2,1)S(1)}, bf16[8,3072]{1,0:T(8,128)(2,1)S(1)}, u32[]{:S(2)}, u32[]{:S(2)}) collective-permute-start(bf16[8,3072]{1,0:T(8,128)(2,1)S(1)} %get-tuple-element.27), channel_id=1, source_target_pairs={{17,0},{18,1},{19,2},{20,3},{21,4},{22,5},{23,6},{24,7},{25,8},{26... | collective-permute-start | bytes 147464 | tf_op jit(solution)/shard_map/ppermute | solution.py:443
  11.6 2.7 %collective-permute-start.2 = (bf16[8,2048]{1,0:T(8,128)(2,1)S(1)}, bf16[8,2048]{1,0:T(8,128)(2,1)S(1)}, u32[]{:S(2)}, u32[]{:S(2)}) collective-permute-start(bf16[8,2048]{1,0:T(8,128)(2,1)S(1)} %get-tuple-element.28), channel_id=1, source_target_pairs={{16,0},{32,16},{48,32},{64,48},{80,64},{96,80},{112,96},{128,112},... | collective-permute-start | bytes 98312 | tf_op jit(solution)/shard_map/ppermute | solution.py:443
  12.7 0.7 %copy-start.7 = (bf16[96,14]{0,1:T(8,128)(2,1)S(1)}, bf16[96,14]{0,1:T(8,128)(2,1)}, u32[]{:S(2)}) copy-start(bf16[96,14]{0,1:T(8,128)(2,1)} %param.19) | copy-start | bytes 8068
  12.7 1.9 %collective-permute-start.3 = (bf16[8,2048]{1,0:T(8,128)(2,1)S(1)}, bf16[8,2048]{1,0:T(8,128)(2,1)S(1)}, u32[]{:S(2)}, u32[]{:S(2)}) collective-permute-start(bf16[8,2048]{1,0:T(8,128)(2,1)S(1)} %get-tuple-element.29), channel_id=1, source_target_pairs={{16,0},{32,16},{48,32},{64,48},{80,64},{96,80},{112,96},{128,112},... | collective-permute-start | bytes 98312 | tf_op jit(solution)/shard_map/ppermute | solution.py:443
  12.8 0.7 %copy-start.8 = (f32[96]{0:T(128)S(1)}, f32[96]{0:T(128)}, u32[]{:S(2)}) copy-start(f32[96]{0:T(128)} %param.13) | copy-start | bytes 1156
  12.8 0.7 %copy-start.9 = (f32[96]{0:T(128)S(1)}, f32[96]{0:T(128)}, u32[]{:S(2)}) copy-start(f32[96]{0:T(128)} %param.16) | copy-start | bytes 1156
  30.3 14.1 %collective-permute-start.4 = (bf16[8,4096]{1,0:T(8,128)(2,1)S(1)}, bf16[8,4096]{1,0:T(8,128)(2,1)S(1)}, u32[]{:S(2)}, u32[]{:S(2)}) collective-permute-start(bf16[8,4096]{1,0:T(8,128)(2,1)S(1)} %get-tuple-element.41), channel_id=1, source_target_pairs={{15,0},{0,1},{1,2},{2,3},{3,4},{4,5},{5,6},{6,7},{7,8},{8,9},{9,10... | collective-permute-start | bytes 196616 | tf_op jit(solution)/shard_map/ppermute | solution.py:443
  31.6 12.7 %collective-permute-start.5 = (bf16[8,3072]{1,0:T(8,128)(2,1)S(1)}, bf16[8,3072]{1,0:T(8,128)(2,1)S(1)}, u32[]{:S(2)}, u32[]{:S(2)}) collective-permute-start(bf16[8,3072]{1,0:T(8,128)(2,1)S(1)} %get-tuple-element.42), channel_id=1, source_target_pairs={{255,0},{240,1},{241,2},{242,3},{243,4},{244,5},{245,6},{246,7},{2... | collective-permute-start | bytes 147464 | tf_op jit(solution)/shard_map/ppermute | solution.py:443
  32.1 5.4 %collective-permute-start.6 = (bf16[8,2048]{1,0:T(8,128)(2,1)S(1)}, bf16[8,2048]{1,0:T(8,128)(2,1)S(1)}, u32[]{:S(2)}, u32[]{:S(2)}) collective-permute-start(bf16[8,2048]{1,0:T(8,128)(2,1)S(1)} %get-tuple-element.43), channel_id=1, source_target_pairs={{240,0},{0,16},{16,32},{32,48},{48,64},{64,80},{80,96},{96,112},{1... | collective-permute-start | bytes 98312 | tf_op jit(solution)/shard_map/ppermute | solution.py:443
  32.2 5.8 %collective-permute-start.7 = (bf16[8,2048]{1,0:T(8,128)(2,1)S(1)}, bf16[8,2048]{1,0:T(8,128)(2,1)S(1)}, u32[]{:S(2)}, u32[]{:S(2)}) collective-permute-start(bf16[8,2048]{1,0:T(8,128)(2,1)S(1)} %get-tuple-element.44), channel_id=1, source_target_pairs={{240,0},{0,16},{16,32},{32,48},{48,64},{64,80},{80,96},{96,112},{1... | collective-permute-start | bytes 98312 | tf_op jit(solution)/shard_map/ppermute | solution.py:443

commit v7 on v6

--- a/solution.py
+++ b/solution.py
@@ -78,19 +78,19 @@
     return jnp.concatenate([values[:, :WIDE], rest, blank], axis=0)
 
 
-def cut_kernel(f_ref, a_ref, c_ref, d_ref, b_ref, b2_ref):
+def cut_kernel(f_ref, a_ref, d_ref, c_ref, c2_ref, b_ref, b2_ref):
     cells = [f_ref[d].astype(F32) for d in range(WIN)]
     low, high = range(SHIFT), range(SHIFT, WIN)
     a_ref[...] = piece_rows(cells, high, (SHIFT, WIN)).astype(BF)
     halved(packed(piece_rows(cells, low, (SHIFT, WIN)), 12), b_ref, b2_ref)
-    c_ref[...] = packed(piece_rows(cells, high, (0, SHIFT)), 12)
+    halved(packed(piece_rows(cells, high, (0, SHIFT)), 12), c_ref, c2_ref)
     d_ref[...] = packed(piece_rows(cells, low, (0, SHIFT)), 9)
 
 
-def join_kernel(a_ref, c_ref, d_ref, b_ref, b2_ref, out_ref):
+def join_kernel(a_ref, d_ref, c_ref, c2_ref, b_ref, b2_ref, out_ref):
     a = a_ref[...].astype(F32)
     b = unpacked(whole_of(b_ref, b2_ref), 12)
-    c = unpacked(c_ref, 12)
+    c = unpacked(whole_of(c_ref, c2_ref), 12)
     d = unpacked(d_ref, 9)
     for i in range(WIN):
         if i < SHIFT:
@@ -226,14 +226,14 @@
 
 def main_kernel(
     scale,
-    a_ref, c_ref, d_ref, b_ref, b2_ref, ids_ref, sel_ref, gain1_ref, gain2_ref,
+    a_ref, d_ref, c_ref, c2_ref, b_ref, b2_ref, ids_ref, sel_ref, gain1_ref, gain2_ref,
     qkv_ref, qkvt_ref, proj_ref, projt_ref, up_ref, upt_ref, down_ref, downt_ref, head_ref, headt_ref,
-    oa_ref, oc_ref, od_ref, ob_ref, ob2_ref,
+    oa_ref, od_ref, oc_ref, oc2_ref, ob_ref, ob2_ref,
     x_ref, unit1_ref, inverse1_ref, q_ref, k_ref, v_ref, keyst_ref, valuest_ref, side_ref, e_ref, s0_ref, s1_ref, top0_ref, top1_ref,
     attended_ref, inverse_ref, d_hidden_ref, d_mixed_ref, extra_ref, dq_ref, dk_ref, dv_ref, slope_ref,
 ):
     sel = sel_ref[...]
-    pieces = [a_ref[...].astype(F32), unpacked(whole_of(b_ref, b2_ref), 12), unpacked(c_ref, 12), unpacked(d_ref, 9)]
+    pieces = [a_ref[...].astype(F32), unpacked(whole_of(b_ref, b2_ref), 12), unpacked(whole_of(c_ref, c2_ref), 12), unpacked(d_ref, 9)]
     rows = jnp.concatenate(pieces, axis=0)
     tall = rows.T
     wides = []
@@ -359,22 +359,22 @@
     rows = jnp.concatenate(blocks, axis=0).T
     oa_ref[...] = rows[:16].astype(BF)
     halved(packed(rows[16:32], 12), ob_ref, ob2_ref)
-    oc_ref[...] = packed(rows[32:48], 12)
+    halved(packed(rows[32:48], 12), oc_ref, oc2_ref)
     od_ref[...] = packed(rows[48:], 9)
 
 
 VMEM = pl.BlockSpec(memory_space=pltpu.VMEM)
 SMALL = pltpu.CompilerParams(vmem_limit_bytes=8 * 2**20)
-PIECES = [jax.ShapeDtypeStruct(s, BF) for s in ((16, WIDE), (8, 4096), (8, 3072), (8, 2048), (8, 2048))]
+PIECES = [jax.ShapeDtypeStruct(s, BF) for s in ((16, WIDE), (8, 3072), (8, 2048), (8, 2048), (8, 2048), (8, 2048))]
 
 
 def cut(features):
-    return pl.pallas_call(cut_kernel, out_shape=PIECES, in_specs=[VMEM], out_specs=[VMEM] * 5, compiler_params=SMALL)(features)
+    return pl.pallas_call(cut_kernel, out_shape=PIECES, in_specs=[VMEM], out_specs=[VMEM] * 6, compiler_params=SMALL)(features)
 
 
 def join(*pieces):
     out = jax.ShapeDtypeStruct((WIN, WIN, WIDE), BF)
-    return pl.pallas_call(join_kernel, out_shape=out, in_specs=[VMEM] * 5, out_specs=VMEM, compiler_params=SMALL)(*pieces)
+    return pl.pallas_call(join_kernel, out_shape=out, in_specs=[VMEM] * 6, out_specs=VMEM, compiler_params=SMALL)(*pieces)
 
 
 def ready(region, labels, attn_gain, mlp_gain, qkv_weight, proj_weight, up_weight, down_weight, head_weight):
@@ -395,8 +395,8 @@
     return pl.pallas_call(
         functools.partial(main_kernel, scale),
         out_shape=PIECES,
-        in_specs=[VMEM] * 19,
-        out_specs=[VMEM] * 5,
+        in_specs=[VMEM] * 20,
+        out_specs=[VMEM] * 6,
         scratch_shapes=[
             pltpu.VMEM((C, WINDOWS * LANES), F32),
             pltpu.VMEM((C, WINDOWS * LANES), F32),
@@ -443,7 +443,7 @@
     return lax.ppermute(piece, axes if len(axes) > 1 else axes[0], route)
 
 
-ROADS = (("gy",), ("gz", "gy"), ("gz",), ("gz",))
+ROADS = (("gz", "gy"), ("gy",), ("gy",), ("gz",), ("gz",))
 
 
 def body(

time: 45.5 us -> 45.4 us (level)
  waiting for transfers between devices: 12.8 us -> 11.1 us
  starting transfers between devices: 13.8 us -> 15.5 us
    ppermute x8 -> x10, starting transfers between devices: 13.8 us -> 15.5 us  [moved(): return lax.ppermute(piece, axes if len(axes) > 1 else axes[0], route)]
    ppermute x8 -> x10, waiting for transfers between devices: 12.8 us -> 11.1 us  [moved(): return lax.ppermute(piece, axes if len(axes) > 1 else axes[0], route)]
  transfers between devices with their start and end apart: 8 -> 10, of which waited for: 5 -> 5; matrix products, arithmetic and copies ran while one was open for 0% -> 0% of each run, Pallas kernels for 1% -> 1%
where the time goes in v7:
time: 45.4 us; the launch traced here: 45.2 us
  Pallas kernels  16.9 us (37%)
  starting transfers between devices  15.5 us (34%)
  waiting for transfers between devices  11.1 us (24%)
  local copies, waits for them, and re-layouts  1.6 us (4%)
    pallas_call x1, Pallas kernels, gradient(): pl.pallas_call(functools.partial(main_kernel, scale), out_shape=PIECES, i...  15.6 us
    ppermute x10, starting transfers between devices, moved(): return lax.ppermute(piece, axes if len(axes) > 1 else axes[0], route)  15.5 us
    ppermute x10, waiting for transfers between devices, moved(): return lax.ppermute(piece, axes if len(axes) > 1 else axes[0], route)  11.1 us
    unnamed x20, local copies, waits for them, and re-layouts  1.6 us
  transfers between devices with their start and end apart: 10, of which 5 were waited for; matrix products, arithmetic and copies ran while one was open for 0% of the time, Pallas kernels for 1%

profile of v7, /device:TPU:32, one launch (start us, length us, event | category | flops | bytes accessed | tf_op | source)
XLA Modules:
  0.0 45.2 jit_solution(4675622963347957360)
XLA Ops:
  0.0 1.0 %copy-done = bf16[7,7,2688]{2,1,0:T(8,128)(2,1)S(1)} copy-done((bf16[7,7,2688]{2,1,0:T(8,128)(2,1)S(1)}, bf16[7,7,2688]{2,1,0:T(8,128)(2,1)}, u32[]{:S(2)}) %copy-start) | copy-done | bytes 263448
  1.0 0.1 shard_map.100
  1.1 10.0 %collective-permute-start = (bf16[8,3072]{1,0:T(8,128)(2,1)S(1)}, bf16[8,3072]{1,0:T(8,128)(2,1)S(1)}, u32[]{:S(2)}, u32[]{:S(2)}) collective-permute-start(bf16[8,3072]{1,0:T(8,128)(2,1)S(1)} %get-tuple-element.28), channel_id=1, source_target_pairs={{17,0},{18,1},{19,2},{20,3},{21,4},{22,5},{23,6},{24,7},{25,8},{26... | collective-permute-start | bytes 147464 | tf_op jit(solution)/shard_map/ppermute | solution.py:443
  11.1 0.7 %collective-permute-start.1 = (bf16[8,2048]{1,0:T(8,128)(2,1)S(1)}, bf16[8,2048]{1,0:T(8,128)(2,1)S(1)}, u32[]{:S(2)}, u32[]{:S(2)}) collective-permute-start(bf16[8,2048]{1,0:T(8,128)(2,1)S(1)} %get-tuple-element.29), channel_id=1, source_target_pairs={{1,0},{2,1},{3,2},{4,3},{5,4},{6,5},{7,6},{8,7},{9,8},{10,9},{11,1... | collective-permute-start | bytes 98312 | tf_op jit(solution)/shard_map/ppermute | solution.py:443
  11.9 0.5 collective-permute-start.2
  12.3 0.3 collective-permute-start.3
  12.6 0.6 %collective-permute-start.4 = (bf16[8,2048]{1,0:T(8,128)(2,1)S(1)}, bf16[8,2048]{1,0:T(8,128)(2,1)S(1)}, u32[]{:S(2)}, u32[]{:S(2)}) collective-permute-start(bf16[8,2048]{1,0:T(8,128)(2,1)S(1)} %get-tuple-element.32), channel_id=1, source_target_pairs={{16,0},{32,16},{48,32},{64,48},{80,64},{96,80},{112,96},{128,112},... | collective-permute-start | bytes 98312 | tf_op jit(solution)/shard_map/ppermute | solution.py:443
  13.3 0.6 %copy-done.8 = f32[96]{0:T(128)S(1)} copy-done((f32[96]{0:T(128)S(1)}, f32[96]{0:T(128)}, u32[]{:S(2)}) %copy-start.8) | copy-done | bytes 408
  13.9 0.0 copy-done.9
  13.9 0.4 shard_map.101
  14.3 0.7 %collective-permute-done.1.c_ref = bf16[8,2048]{1,0:T(8,128)(2,1)S(1)} collective-permute-done((bf16[8,2048]{1,0:T(8,128)(2,1)S(1)}, bf16[8,2048]{1,0:T(8,128)(2,1)S(1)}, u32[]{:S(2)}, u32[]{:S(2)}) %collective-permute-start.1) | collective-permute-done | bytes 32800 | tf_op jit(solution)/shard_map/ppermute | solution.py:443
  15.0 0.7 %collective-permute-done.2.c2_ref = bf16[8,2048]{1,0:T(8,128)(2,1)S(1)} collective-permute-done((bf16[8,2048]{1,0:T(8,128)(2,1)S(1)}, bf16[8,2048]{1,0:T(8,128)(2,1)S(1)}, u32[]{:S(2)}, u32[]{:S(2)}) %collective-permute-start.2) | collective-permute-done | bytes 32800 | tf_op jit(solution)/shard_map/ppermute | solution.py:443
  15.8 0.0 collective-permute-done.3.b_ref
  15.8 0.0 collective-permute-done.4.b2_ref
  15.8 0.0 collective-permute-done.d_ref
  15.8 15.6 %shard_map.102 = (bf16[16,2688]{1,0:T(8,128)(2,1)S(1)}, bf16[8,3072]{1,0:T(8,128)(2,1)S(1)}, bf16[8,2048]{1,0:T(8,128)(2,1)S(1)}, bf16[8,2048]{1,0:T(8,128)(2,1)...) custom-call(bf16[16,2688]{1,0:T(8,128)(2,1)S(1)} %get-tuple-element.27.a_ref, ...), custom_call_target="tpu_custom_call" | custom-call | tf_op jit(solution)/shard_map/pallas_call | solution.py:395
  31.4 1.6 %collective-permute-start.5 = (bf16[8,3072]{1,0:T(8,128)(2,1)S(1)}, bf16[8,3072]{1,0:T(8,128)(2,1)S(1)}, u32[]{:S(2)}, u32[]{:S(2)}) collective-permute-start(bf16[8,3072]{1,0:T(8,128)(2,1)S(1)} %get-tuple-element.44), channel_id=1, source_target_pairs={{255,0},{240,1},{241,2},{242,3},{243,4},{244,5},{245,6},{246,7},{2... | collective-permute-start | bytes 147464 | tf_op jit(solution)/shard_map/ppermute | solution.py:443
  33.1 1.3 %collective-permute-start.6 = (bf16[8,2048]{1,0:T(8,128)(2,1)S(1)}, bf16[8,2048]{1,0:T(8,128)(2,1)S(1)}, u32[]{:S(2)}, u32[]{:S(2)}) collective-permute-start(bf16[8,2048]{1,0:T(8,128)(2,1)S(1)} %get-tuple-element.45), channel_id=1, source_target_pairs={{15,0},{0,1},{1,2},{2,3},{3,4},{4,5},{5,6},{6,7},{7,8},{8,9},{9,10... | collective-permute-start | bytes 98312 | tf_op jit(solution)/shard_map/ppermute | solution.py:443
  34.3 0.0 collective-permute-start.7
  34.4 0.5 %collective-permute-start.9 = (bf16[8,2048]{1,0:T(8,128)(2,1)S(1)}, bf16[8,2048]{1,0:T(8,128)(2,1)S(1)}, u32[]{:S(2)}, u32[]{:S(2)}) collective-permute-start(bf16[8,2048]{1,0:T(8,128)(2,1)S(1)} %get-tuple-element.48), channel_id=1, source_target_pairs={{240,0},{0,16},{16,32},{32,48},{48,64},{64,80},{80,96},{96,112},{1... | collective-permute-start | bytes 98312 | tf_op jit(solution)/shard_map/ppermute | solution.py:443
  34.8 7.4 %collective-permute-done.6.c_ref = bf16[8,2048]{1,0:T(8,128)(2,1)S(1)} collective-permute-done((bf16[8,2048]{1,0:T(8,128)(2,1)S(1)}, bf16[8,2048]{1,0:T(8,128)(2,1)S(1)}, u32[]{:S(2)}, u32[]{:S(2)}) %collective-permute-start.6) | collective-permute-done | bytes 32800 | tf_op jit(solution)/shard_map/ppermute | solution.py:443
  42.2 1.3 %collective-permute-done.7.c2_ref = bf16[8,2048]{1,0:T(8,128)(2,1)S(1)} collective-permute-done((bf16[8,2048]{1,0:T(8,128)(2,1)S(1)}, bf16[8,2048]{1,0:T(8,128)(2,1)S(1)}, u32[]{:S(2)}, u32[]{:S(2)}) %collective-permute-start.7) | collective-permute-done | bytes 32800 | tf_op jit(solution)/shard_map/ppermute | solution.py:443
  43.5 0.9 %collective-permute-done.5.d_ref = bf16[8,3072]{1,0:T(8,128)(2,1)S(1)} collective-permute-done((bf16[8,3072]{1,0:T(8,128)(2,1)S(1)}, bf16[8,3072]{1,0:T(8,128)(2,1)S(1)}, u32[]{:S(2)}, u32[]{:S(2)}) %collective-permute-start.5) | collective-permute-done | bytes 49184 | tf_op jit(solution)/shard_map/ppermute | solution.py:443
  44.4 0.8 %shard_map.103 = bf16[7,7,2688]{2,1,0:T(8,128)(2,1)} custom-call(bf16[16,2688]{1,0:T(8,128)(2,1)S(1)} %get-tuple-element.43.a_ref, bf16[8,3072]{1,0:T(8,128)(2,1)S(1)} %collective-permute-done.5.d_ref, bf16[8,2048]{1,0:T(8,128)(2,1)S(1)} %collective-permute-done.6.c_ref, bf16[8,2048]{1,0:T(8,128)(2,1)S(1)} %collective-permute-done.7.c2_ref, ...), custom_call_target="tpu_custom_call" | custom-call | tf_op jit(solution)/shard_map/pallas_call | solution.py:377
  (20 shorter events, 0.0 us)
Async XLA Ops:
  0.0 1.0 %copy-start = (bf16[7,7,2688]{2,1,0:T(8,128)(2,1)S(1)}, bf16[7,7,2688]{2,1,0:T(8,128)(2,1)}, u32[]{:S(2)}) copy-start(bf16[7,7,2688]{2,1,0:T(8,128)(2,1)} %f_ref.1) | copy-start | bytes 790276
  1.0 12.3 %copy-start.1 = (bf16[96,288]{1,0:T(8,128)(2,1)S(1)}, bf16[96,288]{1,0:T(8,128)(2,1)}, u32[]{:S(2)}) copy-start(bf16[96,288]{1,0:T(8,128)(2,1)} %qkv_ref.3) | copy-start | bytes 165892
  1.0 12.3 %copy-start.2 = (bf16[96,384]{1,0:T(8,128)(2,1)S(1)}, bf16[96,384]{1,0:T(8,128)(2,1)}, u32[]{:S(2)}) copy-start(bf16[96,384]{1,0:T(8,128)(2,1)} %up_ref.3) | copy-start | bytes 221188
  1.0 12.3 %copy-start.3 = (bf16[384,96]{0,1:T(8,128)(2,1)S(1)}, bf16[384,96]{0,1:T(8,128)(2,1)}, u32[]{:S(2)}) copy-start(bf16[384,96]{0,1:T(8,128)(2,1)} %param.18) | copy-start | bytes 221188
  1.0 12.3 %copy-start.4 = (bf16[96,96]{1,0:T(8,128)(2,1)S(1)}, bf16[96,96]{1,0:T(8,128)(2,1)}, u32[]{:S(2)}) copy-start(bf16[96,96]{1,0:T(8,128)(2,1)} %proj_ref.3) | copy-start | bytes 55300
  1.0 12.3 %copy-start.5 = (s32[7,7,28]{2,1,0:T(8,128)S(1)}, s32[7,7,28]{2,1,0:T(8,128)}, u32[]{:S(2)}) copy-start(s32[7,7,28]{2,1,0:T(8,128)} %region_ref.1) | copy-start | bytes 16468
  1.0 12.3 %copy-start.6 = (s32[7,7,28]{2,1,0:T(8,128)S(1)}, s32[7,7,28]{2,1,0:T(8,128)}, u32[]{:S(2)}) copy-start(s32[7,7,28]{2,1,0:T(8,128)} %labels_ref.1) | copy-start | bytes 16468
  1.1 14.7 %collective-permute-start = (bf16[8,3072]{1,0:T(8,128)(2,1)S(1)}, bf16[8,3072]{1,0:T(8,128)(2,1)S(1)}, u32[]{:S(2)}, u32[]{:S(2)}) collective-permute-start(bf16[8,3072]{1,0:T(8,128)(2,1)S(1)} %get-tuple-element.28), channel_id=1, source_target_pairs={{17,0},{18,1},{19,2},{20,3},{21,4},{22,5},{23,6},{24,7},{25,8},{26... | collective-permute-start | bytes 147464 | tf_op jit(solution)/shard_map/ppermute | solution.py:443
  11.1 3.9 %collective-permute-start.1 = (bf16[8,2048]{1,0:T(8,128)(2,1)S(1)}, bf16[8,2048]{1,0:T(8,128)(2,1)S(1)}, u32[]{:S(2)}, u32[]{:S(2)}) collective-permute-start(bf16[8,2048]{1,0:T(8,128)(2,1)S(1)} %get-tuple-element.29), channel_id=1, source_target_pairs={{1,0},{2,1},{3,2},{4,3},{5,4},{6,5},{7,6},{8,7},{9,8},{10,9},{11,1... | collective-permute-start | bytes 98312 | tf_op jit(solution)/shard_map/ppermute | solution.py:443
  11.9 3.9 %collective-permute-start.2 = (bf16[8,2048]{1,0:T(8,128)(2,1)S(1)}, bf16[8,2048]{1,0:T(8,128)(2,1)S(1)}, u32[]{:S(2)}, u32[]{:S(2)}) collective-permute-start(bf16[8,2048]{1,0:T(8,128)(2,1)S(1)} %get-tuple-element.30), channel_id=1, source_target_pairs={{1,0},{2,1},{3,2},{4,3},{5,4},{6,5},{7,6},{8,7},{9,8},{10,9},{11,1... | collective-permute-start | bytes 98312 | tf_op jit(solution)/shard_map/ppermute | solution.py:443
  12.3 3.5 %collective-permute-start.3 = (bf16[8,2048]{1,0:T(8,128)(2,1)S(1)}, bf16[8,2048]{1,0:T(8,128)(2,1)S(1)}, u32[]{:S(2)}, u32[]{:S(2)}) collective-permute-start(bf16[8,2048]{1,0:T(8,128)(2,1)S(1)} %get-tuple-element.31), channel_id=1, source_target_pairs={{16,0},{32,16},{48,32},{64,48},{80,64},{96,80},{112,96},{128,112},... | collective-permute-start | bytes 98312 | tf_op jit(solution)/shard_map/ppermute | solution.py:443
  12.6 0.7 %copy-start.7 = (bf16[96,14]{0,1:T(8,128)(2,1)S(1)}, bf16[96,14]{0,1:T(8,128)(2,1)}, u32[]{:S(2)}) copy-start(bf16[96,14]{0,1:T(8,128)(2,1)} %param.19) | copy-start | bytes 8068
  12.6 3.2 %collective-permute-start.4 = (bf16[8,2048]{1,0:T(8,128)(2,1)S(1)}, bf16[8,2048]{1,0:T(8,128)(2,1)S(1)}, u32[]{:S(2)}, u32[]{:S(2)}) collective-permute-start(bf16[8,2048]{1,0:T(8,128)(2,1)S(1)} %get-tuple-element.32), channel_id=1, source_target_pairs={{16,0},{32,16},{48,32},{64,48},{80,64},{96,80},{112,96},{128,112},... | collective-permute-start | bytes 98312 | tf_op jit(solution)/shard_map/ppermute | solution.py:443
  13.3 0.7 %copy-start.8 = (f32[96]{0:T(128)S(1)}, f32[96]{0:T(128)}, u32[]{:S(2)}) copy-start(f32[96]{0:T(128)} %param.13) | copy-start | bytes 1156
  13.3 0.7 %copy-start.9 = (f32[96]{0:T(128)S(1)}, f32[96]{0:T(128)}, u32[]{:S(2)}) copy-start(f32[96]{0:T(128)} %param.16) | copy-start | bytes 1156
  31.4 13.0 %collective-permute-start.5 = (bf16[8,3072]{1,0:T(8,128)(2,1)S(1)}, bf16[8,3072]{1,0:T(8,128)(2,1)S(1)}, u32[]{:S(2)}, u32[]{:S(2)}) collective-permute-start(bf16[8,3072]{1,0:T(8,128)(2,1)S(1)} %get-tuple-element.44), channel_id=1, source_target_pairs={{255,0},{240,1},{241,2},{242,3},{243,4},{244,5},{245,6},{246,7},{2... | collective-permute-start | bytes 147464 | tf_op jit(solution)/shard_map/ppermute | solution.py:443
  33.1 9.1 %collective-permute-start.6 = (bf16[8,2048]{1,0:T(8,128)(2,1)S(1)}, bf16[8,2048]{1,0:T(8,128)(2,1)S(1)}, u32[]{:S(2)}, u32[]{:S(2)}) collective-permute-start(bf16[8,2048]{1,0:T(8,128)(2,1)S(1)} %get-tuple-element.45), channel_id=1, source_target_pairs={{15,0},{0,1},{1,2},{2,3},{3,4},{4,5},{5,6},{6,7},{7,8},{8,9},{9,10... | collective-permute-start | bytes 98312 | tf_op jit(solution)/shard_map/ppermute | solution.py:443
  34.3 9.1 %collective-permute-start.7 = (bf16[8,2048]{1,0:T(8,128)(2,1)S(1)}, bf16[8,2048]{1,0:T(8,128)(2,1)S(1)}, u32[]{:S(2)}, u32[]{:S(2)}) collective-permute-start(bf16[8,2048]{1,0:T(8,128)(2,1)S(1)} %get-tuple-element.46), channel_id=1, source_target_pairs={{15,0},{0,1},{1,2},{2,3},{3,4},{4,5},{5,6},{6,7},{7,8},{8,9},{9,10... | collective-permute-start | bytes 98312 | tf_op jit(solution)/shard_map/ppermute | solution.py:443
  34.4 9.1 %collective-permute-start.8 = (bf16[8,2048]{1,0:T(8,128)(2,1)S(1)}, bf16[8,2048]{1,0:T(8,128)(2,1)S(1)}, u32[]{:S(2)}, u32[]{:S(2)}) collective-permute-start(bf16[8,2048]{1,0:T(8,128)(2,1)S(1)} %get-tuple-element.47), channel_id=1, source_target_pairs={{240,0},{0,16},{16,32},{32,48},{48,64},{64,80},{80,96},{96,112},{1... | collective-permute-start | bytes 98312 | tf_op jit(solution)/shard_map/ppermute | solution.py:443
  34.4 9.1 %collective-permute-start.9 = (bf16[8,2048]{1,0:T(8,128)(2,1)S(1)}, bf16[8,2048]{1,0:T(8,128)(2,1)S(1)}, u32[]{:S(2)}, u32[]{:S(2)}) collective-permute-start(bf16[8,2048]{1,0:T(8,128)(2,1)S(1)} %get-tuple-element.48), channel_id=1, source_target_pairs={{240,0},{0,16},{16,32},{32,48},{48,64},{64,80},{80,96},{96,112},{1... | collective-permute-start | bytes 98312 | tf_op jit(solution)/shard_map/ppermute | solution.py:443
